TPU v7x, 512 devices: a whole 4x4x16 slice. The times are simulated.
512 devices in a mesh: row: 64 (over y, x, z_hi, core), col: 8 (over z_lo).
Axes of the slice: x: 4, y: 4, z: 16 (z_hi: 2, z_lo: 8; z = z_hi * 8 + z_lo), core: 2. Of those that a mesh axis runs over, the one named last changes fastest.
Arguments:
- flow_state: float32 [4, 128, 256, 1024], P(None, 'row', 'col'), may hold values from -6 to 6
- spacing: float32 [128], replicated, may hold values from 0.004 to 0.012
- diffusivity: float32 [4], replicated, may hold values from 0.03 to 0.1
Outputs:
- flow_next: float32 [4, 128, 256, 1024], P(None, 'row', 'col')
All inputs are finite; a program needn't handle non-finite values.
Results may differ from a plain program's by a relative error of at most 0.00023.
Values sent between devices are 32-bit elements; how exact they have to be, the bound alone decides.
No kernel may reach another device: no remote copies, remote signals or barrier semaphores. Data moves between devices by JAX's collectives and lax.ppermute only.
A program may use at most 64 MiB of HBM per device.

v0:
```python
import jax
import jax.numpy as jnp
from jax import lax
from jax.sharding import PartitionSpec as P

time_step = 0.02
cell_width = 0.1
buoyancy = 1.0


def shifted(value, axis, by):
    size = lax.axis_size(axis)
    pairs = [(i, i + by) for i in range(size) if 0 <= i + by < size]
    return lax.ppermute(value, axis, pairs)


def passed_along(block, axis, distance):
    devices = range(lax.axis_size(axis))
    route = [((i - distance) % len(devices), i) for i in devices]
    return lax.ppermute(block, axis, route)


def wall_geometry(spacing):
    centres = jnp.cumsum(spacing)
    positions = jnp.concatenate([centres[:1] - spacing[:1], centres, centres[-1:] + spacing[-1:]])
    gap_below = positions[1:-1] - positions[:-2]
    gap_above = positions[2:] - positions[1:-1]
    across = positions[2:] - positions[:-2]
    return (gap_below, gap_above, across)


def line_system(spacing, diffusivity):
    gap_below, gap_above, across = wall_geometry(spacing)
    diffuse_rate = time_step * diffusivity[:, None]
    lower_band = -2.0 * diffuse_rate / (across * gap_below)
    upper_band = -2.0 * diffuse_rate / (across * gap_above)
    middle = 1.0 - lower_band - upper_band
    levels = jnp.arange(spacing.shape[0])
    lower_band = jnp.where(levels == 0, 0.0, lower_band)
    upper_band = jnp.where(levels == spacing.shape[0] - 1, 0.0, upper_band)
    return (lower_band, middle, upper_band)


def advance(
    centre, speeds, z_down, z_up, y_left, y_right, x_left, x_right, across, diffusivity, forcing
):
    advection = speeds[0] * (x_right - x_left) / (2.0 * cell_width)
    advection = advection + speeds[1] * (y_right - y_left) / (2.0 * cell_width)
    advection = advection + speeds[2] * (z_up - z_down) / across[:, None, None]
    laplace = (x_right + x_left - 2.0 * centre) / cell_width**2
    laplace = laplace + (y_right + y_left - 2.0 * centre) / cell_width**2
    return centre + time_step * (diffusivity * laplace - advection + forcing)


def make_solver(lower_band, middle, upper_band):
    order = middle.shape[1]
    identity = jnp.broadcast_to(jnp.eye(order, dtype=middle.dtype), (middle.shape[0], order, order))
    inverse = lax.linalg.tridiagonal_solve(lower_band, middle, upper_band, identity)

    def solve_one(line_cols, component):
        return jnp.dot(inverse[component], line_cols, precision=lax.Precision.HIGHEST)

    return solve_one


def forcing_of(fields):
    return jnp.concatenate([jnp.zeros_like(fields[:2]), buoyancy * fields[3:4], fields[2:3]])


def shards(flow_state, spacing, diffusivity):
    z_local = flow_state.shape[1]
    groups = lax.axis_size("row")
    gap_below, gap_above, across = wall_geometry(spacing)
    lower_band, middle, upper_band = line_system(spacing, diffusivity)
    solve_one = make_solver(lower_band, middle, upper_band)
    rates = diffusivity[:, None, None, None]
    across_local = lax.dynamic_slice_in_dim(across, lax.axis_index("row") * z_local, z_local)
    from_below = shifted(flow_state[:, -1:], "row", 1)
    from_above = shifted(flow_state[:, :1], "row", -1)
    z_down = jnp.concatenate([from_below, flow_state[:, :-1]], axis=1)
    z_up = jnp.concatenate([flow_state[:, 1:], from_above], axis=1)
    from_left = passed_along(flow_state[:, :, -1:], "col", 1)
    from_right = passed_along(flow_state[:, :, :1], "col", -1)
    y_left = jnp.concatenate([from_left, flow_state[:, :, :-1]], axis=2)
    y_right = jnp.concatenate([flow_state[:, :, 1:], from_right], axis=2)
    x_left = jnp.roll(flow_state, 1, axis=-1)
    x_right = jnp.roll(flow_state, -1, axis=-1)
    stepped = advance(
        flow_state,
        flow_state,
        z_down,
        z_up,
        y_left,
        y_right,
        x_left,
        x_right,
        across_local,
        rates,
        forcing_of(flow_state),
    )
    blocks = [
        stepped[component].reshape(z_local, groups, -1).transpose(1, 0, 2) for component in range(4)
    ]
    arrived = lax.all_to_all(tuple(blocks), "row", split_axis=0, concat_axis=0, tiled=True)
    solved = tuple(
        (
            solve_one(
                arrived[component].reshape(-1, arrived[component].shape[2]), component
            ).reshape(groups, z_local, -1)
            for component in range(4)
        )
    )
    returned = lax.all_to_all(solved, "row", split_axis=0, concat_axis=0, tiled=True)
    return jnp.stack([piece.transpose(1, 0, 2).reshape(flow_state.shape[1:]) for piece in returned])


def solution(mesh):
    placed = (P(None, "row", "col", None), P(), P())
    return jax.shard_map(
        shards, mesh=mesh, in_specs=placed, out_specs=P(None, "row", "col", None), check_vma=False
    )
```

profile of v0, /device:TPU:1, one launch (start us, length us, event | category | flops | bytes accessed | tf_op | source)
XLA Modules:
  0.0 494.9 jit_solution(9989718315889993904)
XLA Ops:
  0.0 2.4 fusion.655
  2.4 8.8 %collective-permute-start.2 = (f32[4,1,32,1024]{3,2,1,0:T(8,128)}, f32[4,1,32,1024]{3,2,1,0:T(8,128)}, u32[]{:S(2)}, u32[]{:S(2)}) collective-permute-start(f32[4,1,32,1024]{3,2,1,0:T(8,128)} %get-tuple-element.561), channel_id=1, source_target_pairs={{8,0},{16,8},{24,16},{32,24},{40,32},{48,40},{56,48},{64,56},{72,6... | collective-permute-start | bytes 1572872 | tf_op jit(solution)/shard_map/ppermute | solution.py:14
  11.2 10.0 %collective-permute-start.3 = (f32[4,1,32,1024]{3,2,1,0:T(8,128)}, f32[4,1,32,1024]{3,2,1,0:T(8,128)}, u32[]{:S(2)}, u32[]{:S(2)}) collective-permute-start(f32[4,1,32,1024]{3,2,1,0:T(8,128)} %get-tuple-element.560), channel_id=1, source_target_pairs={{0,8},{8,16},{16,24},{24,32},{32,40},{40,48},{48,56},{56,64},{64,7... | collective-permute-start | bytes 1572872 | tf_op jit(solution)/shard_map/ppermute | solution.py:14
  21.8 2.6 collective-permute-start.1
  24.5 9.2 %collective-permute-start = (f32[4,2,1,1024]{3,2,1,0:T(1,128)}, f32[4,2,1,1024]{3,2,1,0:T(1,128)}, u32[]{:S(2)}, u32[]{:S(2)}) collective-permute-start(f32[4,2,1,1024]{3,2,1,0:T(1,128)} %get-tuple-element.558), channel_id=1, source_target_pairs={{1,0},{2,1},{3,2},{4,3},{5,4},{6,5},{7,6},{0,7},{9,8},{10,9},{11,1... | collective-permute-start | bytes 98312 | tf_op jit(solution)/shard_map/ppermute | solution.py:20
  47.4 164.4 %while.32 = (s32[]{:T(128)}, f32[4]{0:T(128)S(1)}, f32[4,128]{1,0:T(4,128)S(1)}, f32[3,32,4]{1,0,2:T(4,128)}, f32[3,32,4,128]{3,2,1,0:T(4,128)}, /*index=5*/f32[...) while((s32[]{:T(128)}, f32[4]{0:T(128)S(1)}, ...), condition=%wide.region_2.3_spmd, body=%wide.region_1.2_spmd.sunk | while | flops 74265 | bytes 465121 | solution.py:58
  95.9 1.3 copy.467
  97.2 1.5 concatenate.72
  150.7 1.3 copy.467
  152.1 1.5 concatenate.72
  205.5 1.3 copy.467
  206.9 1.5 concatenate.72
  211.8 1.6 constant_dynamic-update-slice_fusion.95
  213.5 2.2 fusion.404
  237.3 1.7 fusion.651
  242.4 3.7 fusion.358
  247.1 20.1 %all-to-all-start.6 = ((f32[64,2,512]{2,1,0:T(2,128)}), f32[64,2,512]{2,1,0:T(2,128)S(1)}, u32[]{:S(2)}, u32[]{:S(2)}) async-start(f32[64,2,512]{2,1,0:T(2,128)} %bitcast.2164), calls=%async_computation.6 | async-start | bytes 524288 | tf_op jit(solution)/shard_map/all_to_all | solution.py:104
  274.3 11.6 %all-to-all-done.6 = f32[64,2,512]{2,1,0:T(2,128)S(1)} async-done(((f32[64,2,512]{2,1,0:T(2,128)}), f32[64,2,512]{2,1,0:T(2,128)S(1)}, u32[]{:S(2)}, u32[]{:S(2)}) %all-to-all-start.6) | async-done | bytes 262176 | tf_op jit(solution)/shard_map/all_to_all | solution.py:104
  285.9 11.9 %all-to-all-start.4 = ((f32[64,2,512]{2,1,0:T(2,128)}), f32[64,2,512]{2,1,0:T(2,128)S(1)}, u32[]{:S(2)}, u32[]{:S(2)}) async-start(f32[64,2,512]{2,1,0:T(2,128)} %bitcast.2165), calls=%async_computation.4 | async-start | bytes 524288 | tf_op jit(solution)/shard_map/all_to_all | solution.py:104
  305.3 11.1 %all-to-all-done.4 = f32[64,2,512]{2,1,0:T(2,128)S(1)} async-done(((f32[64,2,512]{2,1,0:T(2,128)}), f32[64,2,512]{2,1,0:T(2,128)S(1)}, u32[]{:S(2)}, u32[]{:S(2)}) %all-to-all-start.4) | async-done | bytes 262176 | tf_op jit(solution)/shard_map/all_to_all | solution.py:104
  316.4 9.0 %all-to-all-start.2 = ((f32[64,2,512]{2,1,0:T(2,128)}), f32[64,2,512]{2,1,0:T(2,128)S(1)}, u32[]{:S(2)}, u32[]{:S(2)}) async-start(f32[64,2,512]{2,1,0:T(2,128)} %bitcast.2166), calls=%async_computation.2 | async-start | bytes 524288 | tf_op jit(solution)/shard_map/all_to_all | solution.py:104
  355.9 17.5 %all-to-all-start = ((f32[64,2,512]{2,1,0:T(2,128)}), f32[64,2,512]{2,1,0:T(2,128)S(1)}, u32[]{:S(2)}, u32[]{:S(2)}) async-start(f32[64,2,512]{2,1,0:T(2,128)} %bitcast.2167), calls=%async_computation | async-start | bytes 524288 | tf_op jit(solution)/shard_map/all_to_all | solution.py:104
  373.5 5.2 %while.33 = (s32[]{:T(128)}, f32[4,128]{1,0:T(4,128)S(1)}, f32[3,32,4,128]{3,1,0,2:T(8,128)S(1)}, f32[3,32,4,128]{3,2,1,0:T(4,128)S(1)}, f32[3,32,4]{2,1,0:T(8,1...) while((s32[]{:T(128)}, f32[4,128]{1,0:T(4,128)S(1)}, ...), condition=%wide.region_4.5_spmd, body=%wide.region_3.4_spmd.sunk | while | flops 48161 | bytes 405093 | solution.py:58
  382.5 9.6 %all-to-all-done = f32[64,2,512]{2,1,0:T(2,128)S(1)} async-done(((f32[64,2,512]{2,1,0:T(2,128)}), f32[64,2,512]{2,1,0:T(2,128)S(1)}, u32[]{:S(2)}, u32[]{:S(2)}) %all-to-all-start) | async-done | bytes 262176 | tf_op jit(solution)/shard_map/all_to_all | solution.py:104
  392.2 7.9 %all-to-all-start.7 = ((f32[64,2,512]{2,1,0:T(2,128)}), f32[64,2,512]{2,1,0:T(2,128)S(1)}, u32[]{:S(2)}, u32[]{:S(2)}) async-start(f32[64,2,512]{2,1,0:T(2,128)} %copy.378), calls=%async_computation.7 | async-start | bytes 524288 | tf_op jit(solution)/shard_map/all_to_all | solution.py:113
  401.6 17.2 %all-to-all-done.7 = f32[64,2,512]{2,1,0:T(2,128)S(1)} async-done(((f32[64,2,512]{2,1,0:T(2,128)}), f32[64,2,512]{2,1,0:T(2,128)S(1)}, u32[]{:S(2)}, u32[]{:S(2)}) %all-to-all-start.7) | async-done | bytes 262176 | tf_op jit(solution)/shard_map/all_to_all | solution.py:113
  418.8 6.4 %all-to-all-start.5 = ((f32[64,2,512]{2,1,0:T(2,128)}), f32[64,2,512]{2,1,0:T(2,128)S(1)}, u32[]{:S(2)}, u32[]{:S(2)}) async-start(f32[64,2,512]{2,1,0:T(2,128)} %copy.374), calls=%async_computation.5 | async-start | bytes 524288 | tf_op jit(solution)/shard_map/all_to_all | solution.py:113
  426.7 17.2 %all-to-all-done.5 = f32[64,2,512]{2,1,0:T(2,128)S(1)} async-done(((f32[64,2,512]{2,1,0:T(2,128)}), f32[64,2,512]{2,1,0:T(2,128)S(1)}, u32[]{:S(2)}, u32[]{:S(2)}) %all-to-all-start.5) | async-done | bytes 262176 | tf_op jit(solution)/shard_map/all_to_all | solution.py:113
  443.9 6.2 %all-to-all-start.3 = ((f32[64,2,512]{2,1,0:T(2,128)}), f32[64,2,512]{2,1,0:T(2,128)S(1)}, u32[]{:S(2)}, u32[]{:S(2)}) async-start(f32[64,2,512]{2,1,0:T(2,128)} %copy.370), calls=%async_computation.3 | async-start | bytes 524288 | tf_op jit(solution)/shard_map/all_to_all | solution.py:113
  451.6 17.2 %all-to-all-done.3 = f32[64,2,512]{2,1,0:T(2,128)S(1)} async-done(((f32[64,2,512]{2,1,0:T(2,128)}), f32[64,2,512]{2,1,0:T(2,128)S(1)}, u32[]{:S(2)}, u32[]{:S(2)}) %all-to-all-start.3) | async-done | bytes 262176 | tf_op jit(solution)/shard_map/all_to_all | solution.py:113
  468.8 6.2 %all-to-all-start.1 = ((f32[64,2,512]{2,1,0:T(2,128)}), f32[64,2,512]{2,1,0:T(2,128)S(1)}, u32[]{:S(2)}, u32[]{:S(2)}) async-start(f32[64,2,512]{2,1,0:T(2,128)} %copy.366), calls=%async_computation.1 | async-start | bytes 524288 | tf_op jit(solution)/shard_map/all_to_all | solution.py:113
  475.5 18.2 %all-to-all-done.1 = f32[64,2,512]{2,1,0:T(2,128)S(1)} async-done(((f32[64,2,512]{2,1,0:T(2,128)}), f32[64,2,512]{2,1,0:T(2,128)S(1)}, u32[]{:S(2)}, u32[]{:S(2)}) %all-to-all-start.1) | async-done | bytes 262176 | tf_op jit(solution)/shard_map/all_to_all | solution.py:113
  (866 shorter events, 253.0 us)
Async XLA Ops:
  0.0 21.2 %copy-start = (f32[4,2,32,1024]{3,2,1,0:T(8,128)S(1)}, f32[4,2,32,1024]{3,2,1,0:T(8,128)}, u32[]{:S(2)}) copy-start(f32[4,2,32,1024]{3,2,1,0:T(8,128)} %param.7) | copy-start | bytes 3145732
  2.4 239.3 %collective-permute-start.2 = (f32[4,1,32,1024]{3,2,1,0:T(8,128)}, f32[4,1,32,1024]{3,2,1,0:T(8,128)}, u32[]{:S(2)}, u32[]{:S(2)}) collective-permute-start(f32[4,1,32,1024]{3,2,1,0:T(8,128)} %get-tuple-element.561), channel_id=1, source_target_pairs={{8,0},{16,8},{24,16},{32,24},{40,32},{48,40},{56,48},{64,56},{72,6... | collective-permute-start | bytes 1572872 | tf_op jit(solution)/shard_map/ppermute | solution.py:14
  11.2 230.5 %collective-permute-start.3 = (f32[4,1,32,1024]{3,2,1,0:T(8,128)}, f32[4,1,32,1024]{3,2,1,0:T(8,128)}, u32[]{:S(2)}, u32[]{:S(2)}) collective-permute-start(f32[4,1,32,1024]{3,2,1,0:T(8,128)} %get-tuple-element.560), channel_id=1, source_target_pairs={{0,8},{8,16},{16,24},{24,32},{32,40},{40,48},{48,56},{56,64},{64,7... | collective-permute-start | bytes 1572872 | tf_op jit(solution)/shard_map/ppermute | solution.py:14
  21.8 219.8 %collective-permute-start.1 = (f32[4,2,1,1024]{3,2,1,0:T(1,128)}, f32[4,2,1,1024]{3,2,1,0:T(1,128)}, u32[]{:S(2)}, u32[]{:S(2)}) collective-permute-start(f32[4,2,1,1024]{3,2,1,0:T(1,128)} %get-tuple-element.559), channel_id=1, source_target_pairs={{7,0},{0,1},{1,2},{2,3},{3,4},{4,5},{5,6},{6,7},{15,8},{8,9},{9,10... | collective-permute-start | bytes 98312 | tf_op jit(solution)/shard_map/ppermute | solution.py:20
  24.5 217.2 %collective-permute-start = (f32[4,2,1,1024]{3,2,1,0:T(1,128)}, f32[4,2,1,1024]{3,2,1,0:T(1,128)}, u32[]{:S(2)}, u32[]{:S(2)}) collective-permute-start(f32[4,2,1,1024]{3,2,1,0:T(1,128)} %get-tuple-element.558), channel_id=1, source_target_pairs={{1,0},{2,1},{3,2},{4,3},{5,4},{6,5},{7,6},{0,7},{9,8},{10,9},{11,1... | collective-permute-start | bytes 98312 | tf_op jit(solution)/shard_map/ppermute | solution.py:20
  42.3 3.3 copy-start.3
  44.3 1.3 copy-start.7
  47.4 13.8 %copy-start.5 = (f32[3,32,4]{2,1,0:T(8,128)}, f32[3,32,4]{2,1,0:T(8,128)S(1)}, u32[]{:S(2)}) copy-start(f32[3,32,4]{2,1,0:T(8,128)S(1)} %get-tuple-element.1167) | copy-start | bytes 4612 | tf_op jit(solution)/shard_map/vmap()/while
  61.1 3.7 copy-start.11
  62.3 2.5 copy-start.13
  102.2 13.8 %copy-start.5 = (f32[3,32,4]{2,1,0:T(8,128)}, f32[3,32,4]{2,1,0:T(8,128)S(1)}, u32[]{:S(2)}) copy-start(f32[3,32,4]{2,1,0:T(8,128)S(1)} %get-tuple-element.1167) | copy-start | bytes 4612 | tf_op jit(solution)/shard_map/vmap()/while
  116.0 3.7 copy-start.11
  117.1 2.5 copy-start.13
  157.0 13.8 %copy-start.5 = (f32[3,32,4]{2,1,0:T(8,128)}, f32[3,32,4]{2,1,0:T(8,128)S(1)}, u32[]{:S(2)}) copy-start(f32[3,32,4]{2,1,0:T(8,128)S(1)} %get-tuple-element.1167) | copy-start | bytes 4612 | tf_op jit(solution)/shard_map/vmap()/while
  170.8 3.7 copy-start.11
  171.9 2.5 copy-start.13
  211.8 1.6 copy-start.26
  211.8 1.6 copy-start.4
  215.6 23.3 %copy-start.40 = (f32[4]{0:T(128)}, f32[4]{0:T(128)S(1)}, u32[]{:S(2)}) copy-start(f32[4]{0:T(128)S(1)} %get-tuple-element.460) | copy-start | bytes 52
  237.3 4.5 copy-start.1
  237.3 4.5 copy-start.2
  247.1 20.1 %copy-start.104 = (f32[4]{0:T(128)S(1)}, f32[4]{0:T(128)}, u32[]{:S(2)}) copy-start(f32[4]{0:T(128)} %get-tuple-element.458) | copy-start | bytes 52
  247.1 20.1 %copy-start.106 = (f32[4]{0:T(128)S(1)}, f32[4]{0:T(128)}, u32[]{:S(2)}) copy-start(f32[4]{0:T(128)} %get-tuple-element.603) | copy-start | bytes 52
  247.1 20.1 %copy-start.107 = (f32[128]{0:T(128)S(1)}, f32[128]{0:T(128)}, u32[]{:S(2)}) copy-start(f32[128]{0:T(128)} %get-tuple-element.584) | copy-start | bytes 1540
  247.1 38.8 %all-to-all-start.6 = ((f32[64,2,512]{2,1,0:T(2,128)}), f32[64,2,512]{2,1,0:T(2,128)S(1)}, u32[]{:S(2)}, u32[]{:S(2)}) async-start(f32[64,2,512]{2,1,0:T(2,128)} %bitcast.2164), calls=%async_computation.6 | async-start | bytes 524288 | tf_op jit(solution)/shard_map/all_to_all | solution.py:104
  285.9 30.6 %all-to-all-start.4 = ((f32[64,2,512]{2,1,0:T(2,128)}), f32[64,2,512]{2,1,0:T(2,128)S(1)}, u32[]{:S(2)}, u32[]{:S(2)}) async-start(f32[64,2,512]{2,1,0:T(2,128)} %bitcast.2165), calls=%async_computation.4 | async-start | bytes 524288 | tf_op jit(solution)/shard_map/all_to_all | solution.py:104
  316.4 39.5 %all-to-all-start.2 = ((f32[64,2,512]{2,1,0:T(2,128)}), f32[64,2,512]{2,1,0:T(2,128)S(1)}, u32[]{:S(2)}, u32[]{:S(2)}) async-start(f32[64,2,512]{2,1,0:T(2,128)} %bitcast.2166), calls=%async_computation.2 | async-start | bytes 524288 | tf_op jit(solution)/shard_map/all_to_all | solution.py:104
  355.9 36.3 %all-to-all-start = ((f32[64,2,512]{2,1,0:T(2,128)}), f32[64,2,512]{2,1,0:T(2,128)S(1)}, u32[]{:S(2)}, u32[]{:S(2)}) async-start(f32[64,2,512]{2,1,0:T(2,128)} %bitcast.2167), calls=%async_computation | async-start | bytes 524288 | tf_op jit(solution)/shard_map/all_to_all | solution.py:104
  392.2 26.6 %all-to-all-start.7 = ((f32[64,2,512]{2,1,0:T(2,128)}), f32[64,2,512]{2,1,0:T(2,128)S(1)}, u32[]{:S(2)}, u32[]{:S(2)}) async-start(f32[64,2,512]{2,1,0:T(2,128)} %copy.378), calls=%async_computation.7 | async-start | bytes 524288 | tf_op jit(solution)/shard_map/all_to_all | solution.py:113
  418.8 25.1 %all-to-all-start.5 = ((f32[64,2,512]{2,1,0:T(2,128)}), f32[64,2,512]{2,1,0:T(2,128)S(1)}, u32[]{:S(2)}, u32[]{:S(2)}) async-start(f32[64,2,512]{2,1,0:T(2,128)} %copy.374), calls=%async_computation.5 | async-start | bytes 524288 | tf_op jit(solution)/shard_map/all_to_all | solution.py:113
  443.9 24.9 %all-to-all-start.3 = ((f32[64,2,512]{2,1,0:T(2,128)}), f32[64,2,512]{2,1,0:T(2,128)S(1)}, u32[]{:S(2)}, u32[]{:S(2)}) async-start(f32[64,2,512]{2,1,0:T(2,128)} %copy.370), calls=%async_computation.3 | async-start | bytes 524288 | tf_op jit(solution)/shard_map/all_to_all | solution.py:113
  468.8 24.9 %all-to-all-start.1 = ((f32[64,2,512]{2,1,0:T(2,128)}), f32[64,2,512]{2,1,0:T(2,128)S(1)}, u32[]{:S(2)}, u32[]{:S(2)}) async-start(f32[64,2,512]{2,1,0:T(2,128)} %copy.366), calls=%async_computation.1 | async-start | bytes 524288 | tf_op jit(solution)/shard_map/all_to_all | solution.py:113
  (162 other events, 102.6 us)
where the time goes:
time: 498 us; the launch traced here: 495 us
  local copies, waits for them, and re-layouts  204 us (41%)
  starting transfers between devices  116 us (23%)
  waiting for transfers between devices  102 us (20%)
  other arithmetic  68 us (14%)
    broadcast_in_dim x127, local copies, waits for them, and re-layouts, make_solver(): lax.linalg.tridiagonal_solve(lower_band, middle, upper_band, identity)  92.4 us
    all_to_all x4, waiting for transfers between devices, shards(): lax.all_to_all(solved, 'row', split_axis=0, concat_axis=0, tiled=True)  69.9 us
    all_to_all x4, starting transfers between devices, shards(): lax.all_to_all(tuple(blocks), 'row', split_axis=0, concat_axis=0, tiled=T...  58.5 us
    unnamed x232, local copies, waits for them, and re-layouts  45.3 us
    all_to_all x4, waiting for transfers between devices, shards(): lax.all_to_all(tuple(blocks), 'row', split_axis=0, concat_axis=0, tiled=T...  32.3 us
    while x183, local copies, waits for them, and re-layouts  30.4 us
    sub x50, other arithmetic, make_solver(): lax.linalg.tridiagonal_solve(lower_band, middle, upper_band, identity)  28 us
    all_to_all x4, starting transfers between devices, shards(): lax.all_to_all(solved, 'row', split_axis=0, concat_axis=0, tiled=True)  26.7 us
  transfers between devices with their start and end apart: 12, of which 7 were waited for; matrix products, arithmetic and copies ran while one was open for 39% of the time, Pallas kernels for 0%

commit v1 on v0

v1 whole, which is shorter than its diff:
```python
import jax
import jax.numpy as jnp
import numpy as np
from jax import lax
from jax.experimental import pallas as pl
from jax.experimental.pallas import tpu as pltpu
from jax.sharding import Mesh
from jax.sharding import PartitionSpec as P

time_step = 0.02
cell_width = 0.1
buoyancy = 1.0

AXES = ("y", "x", "zh", "core", "zl")
ROW = AXES[:4]
PLANE = AXES[:3]
LIMIT = 48 * 2**20


def whole(space=pltpu.VMEM):
    return pl.BlockSpec(memory_space=space)


def params():
    return pltpu.CompilerParams(vmem_limit_bytes=LIMIT)


def prefix(matrix, lane, backward):
    a, b, c, d = matrix
    step = 1
    while step < 128:
        by = 128 - step if backward else step
        edge = lane >= 128 - step if backward else lane < step
        pa, pb, pc, pd = (pltpu.roll(m, by, 1) for m in (a, b, c, d))
        pa, pb = jnp.where(edge, 1.0, pa), jnp.where(edge, 0.0, pb)
        pc, pd = jnp.where(edge, 0.0, pc), jnp.where(edge, 1.0, pd)
        a, b, c, d = a * pa + b * pc, a * pb + b * pd, c * pa + d * pc, c * pb + d * pd
        scale = 1.0 / (a + b + c + d)
        a, b, c, d = a * scale, b * scale, c * scale, d * scale
        step *= 2
    return (a + b) / (c + d)


def chip_index():
    return (lax.axis_index("y") * 4 + lax.axis_index("x")) * 2 + lax.axis_index("zh")


def coefficients_kernel(spacing_ref, diffusivity_ref, own_ref, scan_ref):
    shape = (8, 128)
    lane = lax.broadcasted_iota(jnp.int32, shape, 1)
    row = lax.broadcasted_iota(jnp.int32, shape, 0)
    below = jnp.broadcast_to(spacing_ref[...], shape)
    above = jnp.where(lane == 127, below, pltpu.roll(below, 127, 1))
    across = below + above
    rate = jnp.full(shape, diffusivity_ref[3], jnp.float32)
    for component in range(3):
        rate = jnp.where(row % 4 == component, diffusivity_ref[component], rate)
    rate = time_step * rate
    low, up = 2.0 * rate / (across * below), 2.0 * rate / (across * above)
    up_before = jnp.where(lane == 0, 0.0, pltpu.roll(up, 1, 1))
    low_after = jnp.where(lane == 127, 0.0, pltpu.roll(low, 127, 1))
    one = jnp.ones(shape, jnp.float32)
    t = prefix((1.0 + low, up_before, one, up_before), lane, False)
    tau = prefix((1.0 + up, low_after, one, low_after), lane, True)
    r = jnp.where(lane == 0, 0.0, low / (low + tau))
    s = jnp.where(lane == 127, 0.0, up / (up + t))
    g = 1.0 / (t + tau - 1.0)
    rs = jnp.where(row < 4, r, s)
    gc = jnp.where(row < 4, g, time_step / across)
    four = rs * pltpu.roll(rs, 127, 1)
    four = four * pltpu.roll(four, 126, 1)
    scan_ref[...] = four
    turn = lax.rem(129 - 4 * chip_index(), 128)
    own_ref[0:8, :] = pltpu.roll(rs, turn, 1)
    own_ref[8:16, :] = pltpu.roll(gc, turn, 1)


def local_kernel(
    own_ref, other_ref, same_ref, cross_ref, w3_ref, w4_ref, cf_ref, dif_ref, part_ref, send_ref
):
    core = lax.axis_index("core")
    first = core == 0
    sub = lax.broadcasted_iota(jnp.int32, (8, 1024), 0)
    rate = time_step / (2.0 * cell_width)

    def tile(c, level, rows):
        return jnp.where(
            core == level // 2, own_ref[c, level % 2, rows, :], other_ref[c, level % 2, rows, :]
        )

    def far(c, level):
        line = 2 * c + level % 2
        return jnp.where(
            core == level // 2, same_ref[line : line + 1, :], cross_ref[line : line + 1, :]
        )

    for half in range(2):
        rows = pl.ds(pl.multiple_of(core * 16 + 8 * half, 8), 8)
        here = slice(8 * half, 8 * half + 8)
        w_low = jnp.where(first, w3_ref[here, :], w4_ref[here, :])
        w_high = jnp.where(first, w4_ref[here, :], w3_ref[here, :])
        w_low, w_high = w_low * -cf_ref[12, 0], w_high * cf_ref[12, 5]
        u = [tile(0, level, rows) * rate for level in range(4)]
        v = [tile(1, level, rows) * rate for level in range(4)]
        w = [tile(2, level, rows) for level in range(4)]
        wc = [w[level] * cf_ref[12, level + 1] for level in range(4)]
        for c in range(4):
            r = [cf_ref[c, j] for j in range(6)]
            s = [cf_ref[4 + c, j] for j in range(6)]
            g = [cf_ref[8 + c, j] for j in range(6)]
            spread = dif_ref[c] * (time_step / cell_width**2)
            q = w if c == 2 else [tile(c, level, rows) for level in range(4)]
            gs = []
            for level in range(4):
                centre = q[level]
                left, right = pltpu.roll(centre, 1, 1), pltpu.roll(centre, 1023, 1)
                if half == 0:
                    top = jnp.where(first, far(c, level), tile(c, level, slice(15, 16)))
                    bottom = tile(c, level, pl.ds(pl.multiple_of(core * 16 + 8, 8), 8))[:1]
                else:
                    top = tile(c, level, pl.ds(pl.multiple_of(core * 16, 8), 8))[7:]
                    bottom = jnp.where(first, tile(c, level, slice(16, 17)), far(c, level))
                front = jnp.where(sub == 0, top, pltpu.roll(centre, 1, 0))
                back = jnp.where(sub == 7, bottom, pltpu.roll(centre, 7, 0))
                total = centre + spread * ((left + right) + (front + back) - 4.0 * centre)
                total = total - u[level] * (right - left) - v[level] * (back - front)
                if level == 0:
                    total = total - wc[0] * q[1]
                elif level == 3:
                    total = total + wc[3] * q[2]
                else:
                    total = total - wc[level] * (q[level + 1] - q[level - 1])
                if c == 2:
                    total = total + (time_step * buoyancy) * tile(3, level, rows)
                elif c == 3:
                    total = total + time_step * w[level]
                gs.append(g[level + 1] * total)
            g_low, g_high = g[0] * (w_low * q[0]), g[5] * (w_high * q[3])
            a = [r[1] * g_low + gs[0]]
            for level in range(1, 4):
                a.append(r[level + 1] * a[-1] + gs[level])
            p = r[5] * a[3] + g_high
            b = s[4] * g_high
            part_ref[c, 3, here, :] = a[3] + b
            for level in (2, 1, 0):
                b = s[level + 1] * (b + gs[level + 1])
                part_ref[c, level, here, :] = a[level] + b
            b = s[0] * (b + gs[0]) + g_low
            for block in range(8):
                lanes = slice(128 * block, 128 * block + 128)
                send_ref[8 * half + block, c] = p[:, lanes]
                send_ref[16 + 8 * half + block, c] = b[:, lanes]


def scan_kernel(in_ref, cf_ref, out_ref):
    upward = lax.axis_index("y") < 2

    @pl.when(upward)
    def _():
        for c in range(4):
            carry = jnp.zeros((8, 128), jnp.float32)
            for chip in range(32):
                out_ref[chip, c] = carry
                carry = cf_ref[c, 4 * chip + 1] * carry + in_ref[chip, c]

    @pl.when(jnp.logical_not(upward))
    def _():
        for c in range(4):
            carry = jnp.zeros((8, 128), jnp.float32)
            for chip in range(31, -1, -1):
                out_ref[chip, c] = carry
                carry = cf_ref[4 + c, (4 * chip + 127) % 128] * carry + in_ref[chip, c]


def finish_kernel(part_ref, carry_ref, cf_ref, out_ref, send_ref):
    core = lax.axis_index("core")
    for c in range(4):
        r = [cf_ref[c, j] for j in range(6)]
        s = [cf_ref[4 + c, j] for j in range(6)]
        up = [1.0, r[2], r[2] * r[3], r[2] * r[3] * r[4]]
        down = [s[1] * s[2] * s[3], s[2] * s[3], s[3], 1.0]
        for half in range(2):
            here = slice(8 * half, 8 * half + 8)
            rows = pl.ds(pl.multiple_of(core * 16 + 8 * half, 8), 8)
            for block in range(8):
                lanes = slice(128 * block, 128 * block + 128)
                p = carry_ref[8 * half + block, c]
                q = carry_ref[16 + 8 * half + block, c]
                x = [
                    part_ref[c, level, here, lanes] + up[level] * p + down[level] * q
                    for level in range(4)
                ]
                for k in range(2):
                    out_ref[c, k, rows, lanes] = jnp.where(core == 0, x[k], x[2 + k])
                    send_ref[c, k, here, lanes] = jnp.where(core == 0, x[2 + k], x[k])


def shards(flow_state, spacing, diffusivity):
    core = lax.axis_index("core")
    f32 = jnp.float32

    def route(value, axes, sizes, to):
        pairs = []
        for source in range(int(np.prod(sizes))):
            target = to(*(int(i) for i in np.unravel_index(source, sizes)))
            if target is not None:
                pairs.append((source, target))
        return lax.ppermute(value, axes, pairs)

    def level_rows(start):
        at = (2, core, start, 0)
        return lax.dynamic_slice(flow_state, at, (1, 1, 16, 1024)).reshape(16, 1024)

    def edge_row(start):
        return lax.dynamic_slice_in_dim(flow_state, start, 1, 2).reshape(8, 1024)

    def within(chip, k):
        return 2 * chip + k if 0 <= chip < 32 else None

    def by_chip(turned):
        def to(chip, k):
            return within(chip + 1 if k else chip - 1, 1 - k if turned else k)

        return to

    def by_col(turned):
        def to(k, z):
            return (1 - k if turned else k) * 8 + (z + (-1 if k != turned else 1)) % 8

        return to

    w3 = route(level_rows(16 * (1 - core)), ROW, (32, 2), by_chip(True))
    w4 = route(level_rows(16 * core), ROW, (32, 2), by_chip(False))
    same = route(edge_row(31 * (1 - core)), ("core", "zl"), (2, 8), by_col(False))
    cross = route(edge_row(31 * core), ("core", "zl"), (2, 8), by_col(True))
    other = lax.ppermute(flow_state, "core", [(0, 1), (1, 0)])

    own_cf, scan_cf = pl.pallas_call(
        coefficients_kernel,
        out_shape=(jax.ShapeDtypeStruct((16, 128), f32), jax.ShapeDtypeStruct((8, 128), f32)),
        in_specs=[whole(), whole(pltpu.SMEM)],
        out_specs=(whole(), whole()),
        name="coefficients",
    )(spacing.reshape(1, 128), diffusivity)

    part, moments = pl.pallas_call(
        local_kernel,
        out_shape=(
            jax.ShapeDtypeStruct((4, 4, 16, 1024), f32),
            jax.ShapeDtypeStruct((32, 4, 8, 128), f32),
        ),
        in_specs=[whole()] * 6 + [whole(pltpu.SMEM)] * 2,
        out_specs=(whole(), whole()),
        compiler_params=params(),
        name="local_step",
    )(flow_state, other, same, cross, w3, w4, own_cf, diffusivity)

    arrived = lax.all_to_all(moments, PLANE, split_axis=0, concat_axis=0, tiled=True)
    carried = pl.pallas_call(
        scan_kernel,
        out_shape=jax.ShapeDtypeStruct((32, 4, 8, 128), f32),
        in_specs=[whole(), whole(pltpu.SMEM)],
        out_specs=whole(),
        compiler_params=params(),
        name="scan_chips",
    )(arrived, scan_cf)
    returned = lax.all_to_all(carried, PLANE, split_axis=0, concat_axis=0, tiled=True)

    kept, leaving = pl.pallas_call(
        finish_kernel,
        out_shape=(
            jax.ShapeDtypeStruct((4, 2, 32, 1024), f32),
            jax.ShapeDtypeStruct((4, 2, 16, 1024), f32),
        ),
        in_specs=[whole(), whole(), whole(pltpu.SMEM)],
        out_specs=(whole(), whole()),
        compiler_params=params(),
        name="finish",
    )(part, returned, own_cf)
    back = lax.ppermute(leaving, "core", [(0, 1), (1, 0)])
    return lax.dynamic_update_slice_in_dim(kept, back, 16 * (1 - core), 2)


def solution(mesh):
    fine = Mesh(mesh.devices.reshape(4, 4, 2, 2, 8), AXES)
    field = P(None, ROW, "zl", None)
    return jax.shard_map(
        shards, mesh=fine, in_specs=(field, P(), P()), out_specs=field, check_vma=False
    )
```

time: 498 us -> 127 us (0.26)
  the two profiles are of different devices: /device:TPU:1 before, /device:TPU:33 now
where the time goes in v1:
time: 127 us
  blocking collectives  70 us (55%)
  starting transfers between devices  41 us (32%)
  Pallas kernels  6.87 us (5%)
  local copies, waits for them, and re-layouts  4.95 us (4%)
  waiting for transfers between devices  3.94 us (3%)
    all_to_all x1, blocking collectives, shards(): lax.all_to_all(moments, PLANE, split_axis=0, concat_axis=0, tiled=True)  43.4 us
    all_to_all x1, blocking collectives, shards(): lax.all_to_all(carried, PLANE, split_axis=0, concat_axis=0, tiled=True)  26.7 us
    ppermute x4, starting transfers between devices, route(): return lax.ppermute(value, axes, pairs)  23.2 us
    ppermute x1, starting transfers between devices, shards(): back = lax.ppermute(leaving, 'core', [(0, 1), (1, 0)])  15.2 us
    ppermute x1, starting transfers between devices, shards(): other = lax.ppermute(flow_state, 'core', [(0, 1), (1, 0)])  2.57 us
  transfers between devices with their start and end apart: 6, of which 3 were waited for; matrix products, arithmetic and copies ran while one was open for 2% of the time, Pallas kernels for 2%

profile of v1, /device:TPU:33, one launch (start us, length us, event | category | flops | bytes accessed | tf_op | source)
XLA Modules:
  0.0 126.9 jit_solution(15315216201502650158)
XLA Ops:
  0.0 2.6 %collective-permute-start = (f32[4,2,32,1024]{3,2,1,0:T(8,128)}, f32[4,2,32,1024]{3,2,1,0:T(8,128)S(1)}, u32[]{:S(2)}, u32[]{:S(2)}) collective-permute-start(f32[4,2,32,1024]{3,2,1,0:T(8,128)} %own_ref.1), channel_id=1, source_target_pairs={{0,8},{8,0},{1,9},{9,1},{2,10},{10,2},{3,11},{11,3},{4,12},{12,4},... | collective-permute-start | bytes 3145736 | tf_op jit(solution)/shard_map/ppermute | solution.py:236
  2.6 0.9 dynamic-slice_bitcast_fusion
  3.5 14.5 %collective-permute-start.4 = (f32[16,1024]{1,0:T(8,128)S(1)}, f32[16,1024]{1,0:T(8,128)S(1)}, u32[]{:S(2)}, u32[]{:S(2)}) collective-permute-start(f32[16,1024]{1,0:T(8,128)S(1)} %get-tuple-element.19), channel_id=1, source_target_pairs={{8,24},{16,0},{24,40},{32,16},{40,56},{48,32},{56,72},{64,48},{72,... | collective-permute-start | bytes 196616 | tf_op jit(solution)/shard_map/ppermute | solution.py:208
  18.0 1.9 %collective-permute-start.3 = (f32[16,1024]{1,0:T(8,128)S(1)}, f32[16,1024]{1,0:T(8,128)S(1)}, u32[]{:S(2)}, u32[]{:S(2)}) collective-permute-start(f32[16,1024]{1,0:T(8,128)S(1)} %get-tuple-element.20), channel_id=1, source_target_pairs={{8,16},{16,8},{24,32},{32,24},{40,48},{48,40},{56,64},{64,56},{72,... | collective-permute-start | bytes 196616 | tf_op jit(solution)/shard_map/ppermute | solution.py:208
  20.0 1.2 dynamic-slice_reduce_fusion
  21.2 4.8 %collective-permute-start.1 = (f32[8,1024]{1,0:T(8,128)S(1)}, f32[8,1024]{1,0:T(8,128)S(1)}, u32[]{:S(2)}, u32[]{:S(2)}) collective-permute-start(f32[8,1024]{1,0:T(8,128)S(1)} %reshape.15), channel_id=1, source_target_pairs={{0,1},{1,2},{2,3},{3,4},{4,5},{5,6},{6,7},{7,0},{8,15},{9,8},{10,9... | collective-permute-start | bytes 98312 | tf_op jit(solution)/shard_map/ppermute | solution.py:208
  26.1 1.9 %collective-permute-start.2 = (f32[8,1024]{1,0:T(8,128)S(1)}, f32[8,1024]{1,0:T(8,128)S(1)}, u32[]{:S(2)}, u32[]{:S(2)}) collective-permute-start(f32[8,1024]{1,0:T(8,128)S(1)} %reshape.16), channel_id=1, source_target_pairs={{0,15},{1,8},{2,9},{3,10},{4,11},{5,12},{6,13},{7,14},{8,1},{9,2},... | collective-permute-start | bytes 98312 | tf_op jit(solution)/shard_map/ppermute | solution.py:208
  28.0 2.3 %coefficients.1 = (f32[16,128]{1,0:T(8,128)}, f32[8,128]{1,0:T(8,128)}) custom-call(f32[1,128]{1,0:T(1,128)} %bitcast.5, f32[4]{0:T(128)} %dif_ref.1), custom_call_target="tpu_custom_call" | custom-call | tf_op jit(solution)/shard_map/coefficients/pallas_call | solution.py:238
  30.3 0.0 copy-start.4
  30.3 0.0 collective-permute-done.1.same_ref
  30.3 1.0 collective-permute-done.2.cross_ref
  31.3 0.0 collective-permute-done.4.w4_ref
  31.3 1.4 %collective-permute-done.3.w3_ref = f32[16,1024]{1,0:T(8,128)S(1)} collective-permute-done((f32[16,1024]{1,0:T(8,128)S(1)}, f32[16,1024]{1,0:T(8,128)S(1)}, u32[]{:S(2)}, u32[]{:S(2)}) %collective-permute-start.3) | collective-permute-done | bytes 65568 | tf_op jit(solution)/shard_map/ppermute | solution.py:208
  32.7 0.0 collective-permute-done.other_ref
  32.7 0.0 copy-done.4
  32.7 0.0 copy-start
  32.7 1.2 copy-done
  34.0 0.0 copy-start.1
  34.0 0.7 copy-done.1
  34.7 2.1 %local_step.1 = (f32[4,4,16,1024]{3,2,1,0:T(8,128)S(1)}, f32[32,4,8,128]{3,2,1,0:T(8,128)S(1)}) custom-call(f32[4,2,32,1024]{3,2,1,0:T(8,128)S(1)} %copy-done, f32[4,2,32,1024]{3,2,1,0:T(8,128)S(1)} %collective-permute-done.other_ref, f32[8,1024]{1,0:T(8,128)S(1)} %collective-permute-done.1.same_ref, f32[8,1024]{1,0:T(8,128)S(1)} %collective-permute-done.2.cross_ref, ...), custom_call_target="tpu_custom_call" | custom-call | tf_op jit(solution)/shard_map/local_step/pallas_call | solution.py:246
  36.8 0.0 copy-start.3
  36.8 43.4 %all_to_all.10.in_ref = f32[32,4,8,128]{3,2,1,0:T(8,128)S(1)} all-to-all(f32[32,4,8,128]{3,2,1,0:T(8,128)S(1)} %get-tuple-element.13), channel_id=1, replica_groups=mesh['y'=4,'x'=4,'zh'=2,'core'=2,'zl'=8] {'y','x','zh'}, dimensions={0} | all-to-all | bytes 1048576 | tf_op jit(solution)/shard_map/all_to_all | solution.py:258
  80.1 0.0 copy-done.3
  80.1 0.7 scan_chips.1
  80.8 0.0 copy-start.2
  80.9 26.7 %all_to_all.11.carry_ref = f32[32,4,8,128]{3,2,1,0:T(8,128)S(1)} all-to-all(f32[32,4,8,128]{3,2,1,0:T(8,128)S(1)} %scan_chips.1), channel_id=1, replica_groups=mesh['y'=4,'x'=4,'zh'=2,'core'=2,'zl'=8] {'y','x','zh'}, dimensions={0} | all-to-all | bytes 1048576 | tf_op jit(solution)/shard_map/all_to_all | solution.py:267
  107.5 0.0 copy-done.2
  107.5 1.8 %finish.1 = (f32[4,2,32,1024]{3,2,1,0:T(8,128)}, f32[4,2,16,1024]{3,2,1,0:T(8,128)S(1)}) custom-call(f32[4,4,16,1024]{3,2,1,0:T(8,128)S(1)} %get-tuple-element.12.part_ref, f32[32,4,8,128]{3,2,1,0:T(8,128)S(1)} %all_to_all.11.carry_ref, f32[16,128]{1,0:T(8,128)S(1)} %copy-done.2), custom_call_target="tpu_custom_call" | custom-call | tf_op jit(solution)/shard_map/finish/pallas_call | solution.py:269
  109.3 15.2 %collective-permute-start.5 = (f32[4,2,16,1024]{3,2,1,0:T(8,128)S(1)}, f32[4,2,16,1024]{3,2,1,0:T(8,128)S(1)}, u32[]{:S(2)}, u32[]{:S(2)}) collective-permute-start(f32[4,2,16,1024]{3,2,1,0:T(8,128)S(1)} %get-tuple-element.16), channel_id=1, source_target_pairs={{0,8},{8,0},{1,9},{9,1},{2,10},{10,2},{3,11},{11,3},{4,12},{12,4},... | collective-permute-start | bytes 1572872 | tf_op jit(solution)/shard_map/ppermute | solution.py:280
  124.5 1.5 %collective-permute-done.5 = f32[4,2,16,1024]{3,2,1,0:T(8,128)S(1)} collective-permute-done((f32[4,2,16,1024]{3,2,1,0:T(8,128)S(1)}, f32[4,2,16,1024]{3,2,1,0:T(8,128)S(1)}, u32[]{:S(2)}, u32[]{:S(2)}) %collective-permute-start.5) | collective-permute-done | bytes 524320 | tf_op jit(solution)/shard_map/ppermute | solution.py:280
  126.0 0.8 constant_dynamic-update-slice_fusion
  (2 shorter events, 0.0 us)
Async XLA Ops:
  0.0 32.7 %collective-permute-start = (f32[4,2,32,1024]{3,2,1,0:T(8,128)}, f32[4,2,32,1024]{3,2,1,0:T(8,128)S(1)}, u32[]{:S(2)}, u32[]{:S(2)}) collective-permute-start(f32[4,2,32,1024]{3,2,1,0:T(8,128)} %own_ref.1), channel_id=1, source_target_pairs={{0,8},{8,0},{1,9},{9,1},{2,10},{10,2},{3,11},{11,3},{4,12},{12,4},... | collective-permute-start | bytes 3145736 | tf_op jit(solution)/shard_map/ppermute | solution.py:236
  3.5 27.9 %collective-permute-start.4 = (f32[16,1024]{1,0:T(8,128)S(1)}, f32[16,1024]{1,0:T(8,128)S(1)}, u32[]{:S(2)}, u32[]{:S(2)}) collective-permute-start(f32[16,1024]{1,0:T(8,128)S(1)} %get-tuple-element.19), channel_id=1, source_target_pairs={{8,24},{16,0},{24,40},{32,16},{40,56},{48,32},{56,72},{64,48},{72,... | collective-permute-start | bytes 196616 | tf_op jit(solution)/shard_map/ppermute | solution.py:208
  18.0 14.7 %collective-permute-start.3 = (f32[16,1024]{1,0:T(8,128)S(1)}, f32[16,1024]{1,0:T(8,128)S(1)}, u32[]{:S(2)}, u32[]{:S(2)}) collective-permute-start(f32[16,1024]{1,0:T(8,128)S(1)} %get-tuple-element.20), channel_id=1, source_target_pairs={{8,16},{16,8},{24,32},{32,24},{40,48},{48,40},{56,64},{64,56},{72,... | collective-permute-start | bytes 196616 | tf_op jit(solution)/shard_map/ppermute | solution.py:208
  21.2 9.1 %collective-permute-start.1 = (f32[8,1024]{1,0:T(8,128)S(1)}, f32[8,1024]{1,0:T(8,128)S(1)}, u32[]{:S(2)}, u32[]{:S(2)}) collective-permute-start(f32[8,1024]{1,0:T(8,128)S(1)} %reshape.15), channel_id=1, source_target_pairs={{0,1},{1,2},{2,3},{3,4},{4,5},{5,6},{6,7},{7,0},{8,15},{9,8},{10,9... | collective-permute-start | bytes 98312 | tf_op jit(solution)/shard_map/ppermute | solution.py:208
  26.1 5.2 %collective-permute-start.2 = (f32[8,1024]{1,0:T(8,128)S(1)}, f32[8,1024]{1,0:T(8,128)S(1)}, u32[]{:S(2)}, u32[]{:S(2)}) collective-permute-start(f32[8,1024]{1,0:T(8,128)S(1)} %reshape.16), channel_id=1, source_target_pairs={{0,15},{1,8},{2,9},{3,10},{4,11},{5,12},{6,13},{7,14},{8,1},{9,2},... | collective-permute-start | bytes 98312 | tf_op jit(solution)/shard_map/ppermute | solution.py:208
  30.3 2.4 %copy-start.4 = (f32[4]{0:T(128)S(1)}, f32[4]{0:T(128)}, u32[]{:S(2)}) copy-start(f32[4]{0:T(128)} %dif_ref.1) | copy-start | bytes 52
  32.7 1.2 copy-start
  34.0 0.7 copy-start.1
  36.8 43.4 %copy-start.3 = (f32[8,128]{1,0:T(8,128)S(1)}, f32[8,128]{1,0:T(8,128)}, u32[]{:S(2)}) copy-start(f32[8,128]{1,0:T(8,128)} %get-tuple-element.14.cf_ref) | copy-start | bytes 12292
  80.8 26.7 %copy-start.2 = (f32[16,128]{1,0:T(8,128)S(1)}, f32[16,128]{1,0:T(8,128)}, u32[]{:S(2)}) copy-start(f32[16,128]{1,0:T(8,128)} %get-tuple-element.11.cf_ref) | copy-start | bytes 24580
  109.3 16.7 %collective-permute-start.5 = (f32[4,2,16,1024]{3,2,1,0:T(8,128)S(1)}, f32[4,2,16,1024]{3,2,1,0:T(8,128)S(1)}, u32[]{:S(2)}, u32[]{:S(2)}) collective-permute-start(f32[4,2,16,1024]{3,2,1,0:T(8,128)S(1)} %get-tuple-element.16), channel_id=1, source_target_pairs={{0,8},{8,0},{1,9},{9,1},{2,10},{10,2},{3,11},{11,3},{4,12},{12,4},... | collective-permute-start | bytes 1572872 | tf_op jit(solution)/shard_map/ppermute | solution.py:280

commit v2 on v1

--- a/solution.py
+++ b/solution.py
@@ -75,9 +75,15 @@
     own_ref[8:16, :] = pltpu.roll(gc, turn, 1)
 
 
-def local_kernel(
-    own_ref, other_ref, same_ref, cross_ref, w3_ref, w4_ref, cf_ref, dif_ref, part_ref, send_ref
-):
+def ends_kernel(own_ref, other_ref, out_ref):
+    first = lax.axis_index("core") == 0
+    for line in range(8):
+        c, k = line // 2, line % 2
+        for at, ref in ((line, own_ref), (8 + line, other_ref)):
+            out_ref[at : at + 1, :] = jnp.where(first, ref[c, k, 0:1, :], ref[c, k, 31:32, :])
+
+
+def local_kernel(own_ref, other_ref, halo_ref, cf_ref, dif_ref, part_ref, send_ref):
     core = lax.axis_index("core")
     first = core == 0
     sub = lax.broadcasted_iota(jnp.int32, (8, 1024), 0)
@@ -91,15 +97,12 @@
     def far(c, level):
         line = 2 * c + level % 2
         return jnp.where(
-            core == level // 2, same_ref[line : line + 1, :], cross_ref[line : line + 1, :]
+            core == level // 2, halo_ref[8 + line : 9 + line, :], halo_ref[line : line + 1, :]
         )
 
     for half in range(2):
         rows = pl.ds(pl.multiple_of(core * 16 + 8 * half, 8), 8)
         here = slice(8 * half, 8 * half + 8)
-        w_low = jnp.where(first, w3_ref[here, :], w4_ref[here, :])
-        w_high = jnp.where(first, w4_ref[here, :], w3_ref[here, :])
-        w_low, w_high = w_low * -cf_ref[12, 0], w_high * cf_ref[12, 5]
         u = [tile(0, level, rows) * rate for level in range(4)]
         v = [tile(1, level, rows) * rate for level in range(4)]
         w = [tile(2, level, rows) for level in range(4)]
@@ -135,21 +138,47 @@
                 elif c == 3:
                     total = total + time_step * w[level]
                 gs.append(g[level + 1] * total)
-            g_low, g_high = g[0] * (w_low * q[0]), g[5] * (w_high * q[3])
-            a = [r[1] * g_low + gs[0]]
+            a = [gs[0]]
             for level in range(1, 4):
                 a.append(r[level + 1] * a[-1] + gs[level])
-            p = r[5] * a[3] + g_high
-            b = s[4] * g_high
-            part_ref[c, 3, here, :] = a[3] + b
-            for level in (2, 1, 0):
+            p = r[5] * a[3]
+            part_ref[c, 3, here, :] = a[3]
+            b = s[3] * gs[3]
+            part_ref[c, 2, here, :] = a[2] + b
+            for level in (1, 0):
                 b = s[level + 1] * (b + gs[level + 1])
                 part_ref[c, level, here, :] = a[level] + b
-            b = s[0] * (b + gs[0]) + g_low
+            b = s[0] * (b + gs[0])
             for block in range(8):
                 lanes = slice(128 * block, 128 * block + 128)
                 send_ref[8 * half + block, c] = p[:, lanes]
                 send_ref[16 + 8 * half + block, c] = b[:, lanes]
+
+
+def edges_kernel(own_ref, other_ref, far_ref, near_ref, moments_ref, cf_ref, send_ref, mine_ref):
+    core = lax.axis_index("core")
+    first = core == 0
+    for half in range(2):
+        rows = pl.ds(pl.multiple_of(core * 16 + 8 * half, 8), 8)
+        far, near = far_ref[rows, :], near_ref[rows, :]
+        w_low = jnp.where(first, far, near) * -cf_ref[12, 0]
+        w_high = jnp.where(first, near, far) * cf_ref[12, 5]
+        for c in range(4):
+            r = [cf_ref[c, j] for j in range(6)]
+            s = [cf_ref[4 + c, j] for j in range(6)]
+            lowest = jnp.where(first, own_ref[c, 0, rows, :], other_ref[c, 0, rows, :])
+            highest = jnp.where(first, other_ref[c, 1, rows, :], own_ref[c, 1, rows, :])
+            low, high = cf_ref[8 + c, 0] * (w_low * lowest), cf_ref[8 + c, 5] * (w_high * highest)
+            from_low, from_high = r[1] * low, s[4] * high
+            p = (r[2] * r[3] * r[4] * r[5]) * from_low + high
+            q = (s[0] * s[1] * s[2] * s[3]) * from_high + low
+            for block in range(8):
+                lanes = slice(128 * block, 128 * block + 128)
+                up, down = 8 * half + block, 16 + 8 * half + block
+                send_ref[up, c] = moments_ref[up, c] + p[:, lanes]
+                send_ref[down, c] = moments_ref[down, c] + q[:, lanes]
+                mine_ref[up, c] = from_low[:, lanes]
+                mine_ref[down, c] = from_high[:, lanes]
 
 
 def scan_kernel(in_ref, cf_ref, out_ref):
@@ -172,7 +201,7 @@
                 carry = cf_ref[4 + c, (4 * chip + 127) % 128] * carry + in_ref[chip, c]
 
 
-def finish_kernel(part_ref, carry_ref, cf_ref, out_ref, send_ref):
+def finish_kernel(part_ref, carry_ref, mine_ref, cf_ref, out_ref, send_ref):
     core = lax.axis_index("core")
     for c in range(4):
         r = [cf_ref[c, j] for j in range(6)]
@@ -184,8 +213,8 @@
             rows = pl.ds(pl.multiple_of(core * 16 + 8 * half, 8), 8)
             for block in range(8):
                 lanes = slice(128 * block, 128 * block + 128)
-                p = carry_ref[8 * half + block, c]
-                q = carry_ref[16 + 8 * half + block, c]
+                p = carry_ref[8 * half + block, c] + mine_ref[8 * half + block, c]
+                q = carry_ref[16 + 8 * half + block, c] + mine_ref[16 + 8 * half + block, c]
                 x = [
                     part_ref[c, level, here, lanes] + up[level] * p + down[level] * q
                     for level in range(4)
@@ -207,33 +236,30 @@
                 pairs.append((source, target))
         return lax.ppermute(value, axes, pairs)
 
-    def level_rows(start):
-        at = (2, core, start, 0)
-        return lax.dynamic_slice(flow_state, at, (1, 1, 16, 1024)).reshape(16, 1024)
-
-    def edge_row(start):
-        return lax.dynamic_slice_in_dim(flow_state, start, 1, 2).reshape(8, 1024)
+    def across_cores(value):
+        return lax.ppermute(value, "core", [(0, 1), (1, 0)])
 
     def within(chip, k):
         return 2 * chip + k if 0 <= chip < 32 else None
 
-    def by_chip(turned):
-        def to(chip, k):
-            return within(chip + 1 if k else chip - 1, 1 - k if turned else k)
-
-        return to
-
-    def by_col(turned):
-        def to(k, z):
-            return (1 - k if turned else k) * 8 + (z + (-1 if k != turned else 1)) % 8
-
-        return to
-
-    w3 = route(level_rows(16 * (1 - core)), ROW, (32, 2), by_chip(True))
-    w4 = route(level_rows(16 * core), ROW, (32, 2), by_chip(False))
-    same = route(edge_row(31 * (1 - core)), ("core", "zl"), (2, 8), by_col(False))
-    cross = route(edge_row(31 * core), ("core", "zl"), (2, 8), by_col(True))
-    other = lax.ppermute(flow_state, "core", [(0, 1), (1, 0)])
+    def to_chip(chip, k):
+        return within(chip + 1 if k else chip - 1, 1 - k)
+
+    def to_col(k, z):
+        return (1 - k) * 8 + (z + (1 if k else -1)) % 8
+
+    other = across_cores(flow_state)
+    edge = lax.dynamic_slice(flow_state, (2, core, 0, 0), (1, 1, 32, 1024)).reshape(32, 1024)
+    w_far = route(edge, ROW, (32, 2), to_chip)
+    ends = pl.pallas_call(
+        ends_kernel,
+        out_shape=jax.ShapeDtypeStruct((16, 1024), f32),
+        in_specs=[whole()] * 2,
+        out_specs=whole(),
+        compiler_params=params(),
+        name="row_ends",
+    )(flow_state, other)
+    halo = route(ends, ("core", "zl"), (2, 8), to_col)
 
     own_cf, scan_cf = pl.pallas_call(
         coefficients_kernel,
@@ -243,22 +269,31 @@
         name="coefficients",
     )(spacing.reshape(1, 128), diffusivity)
 
+    pieces = jax.ShapeDtypeStruct((32, 4, 8, 128), f32)
     part, moments = pl.pallas_call(
         local_kernel,
-        out_shape=(
-            jax.ShapeDtypeStruct((4, 4, 16, 1024), f32),
-            jax.ShapeDtypeStruct((32, 4, 8, 128), f32),
-        ),
-        in_specs=[whole()] * 6 + [whole(pltpu.SMEM)] * 2,
+        out_shape=(jax.ShapeDtypeStruct((4, 4, 16, 1024), f32), pieces),
+        in_specs=[whole()] * 3 + [whole(pltpu.SMEM)] * 2,
         out_specs=(whole(), whole()),
         compiler_params=params(),
         name="local_step",
-    )(flow_state, other, same, cross, w3, w4, own_cf, diffusivity)
+    )(flow_state, other, halo, own_cf, diffusivity)
+
+    w_far, moments, part = lax.optimization_barrier((w_far, moments, part))
+    w_near = across_cores(w_far)
+    moments, mine = pl.pallas_call(
+        edges_kernel,
+        out_shape=(pieces, pieces),
+        in_specs=[whole()] * 5 + [whole(pltpu.SMEM)],
+        out_specs=(whole(), whole()),
+        compiler_params=params(),
+        name="edge_products",
+    )(flow_state, other, w_far, w_near, moments, own_cf)
 
     arrived = lax.all_to_all(moments, PLANE, split_axis=0, concat_axis=0, tiled=True)
     carried = pl.pallas_call(
         scan_kernel,
-        out_shape=jax.ShapeDtypeStruct((32, 4, 8, 128), f32),
+        out_shape=pieces,
         in_specs=[whole(), whole(pltpu.SMEM)],
         out_specs=whole(),
         compiler_params=params(),
@@ -272,12 +307,12 @@
             jax.ShapeDtypeStruct((4, 2, 32, 1024), f32),
             jax.ShapeDtypeStruct((4, 2, 16, 1024), f32),
         ),
-        in_specs=[whole(), whole(), whole(pltpu.SMEM)],
+        in_specs=[whole(), whole(), whole(), whole(pltpu.SMEM)],
         out_specs=(whole(), whole()),
         compiler_params=params(),
         name="finish",
-    )(part, returned, own_cf)
-    back = lax.ppermute(leaving, "core", [(0, 1), (1, 0)])
+    )(part, returned, mine, own_cf)
+    back = across_cores(leaving)
     return lax.dynamic_update_slice_in_dim(kept, back, 16 * (1 - core), 2)
 
 

time: 127 us -> 123 us (0.969)
  starting transfers between devices: 41 us -> 23.4 us
  blocking collectives: 70 us -> 81.4 us
  waiting for transfers between devices: 3.94 us -> 6.66 us
  local copies, waits for them, and re-layouts: 4.95 us -> 3.68 us
    all_to_all x1, blocking collectives: 43.4 us -> 54.8 us  [shards(): lax.all_to_all(moments, PLANE, split_axis=0, concat_axis=0, tiled=True)]
    ppermute x2 -> x3, starting transfers between devices: 17.8 us -> 6.87 us  [across_cores(): return lax.ppermute(value, 'core', [(0, 1), (1, 0)])]
    ppermute x4 -> x2, starting transfers between devices: 23.2 us -> 16.5 us  [route(): return lax.ppermute(value, axes, pairs)]
    ppermute x4 -> x2, waiting for transfers between devices: 2.42 us -> 3.83 us  [route(): return lax.ppermute(value, axes, pairs)]
    ppermute x2 -> x3, waiting for transfers between devices: 1.52 us -> 2.83 us  [across_cores(): return lax.ppermute(value, 'core', [(0, 1), (1, 0)])]
  transfers between devices with their start and end apart: 6 -> 5, of which waited for: 3 -> 4; matrix products, arithmetic and copies ran while one was open for 2% -> 1% of each run, Pallas kernels for 2% -> 3%
where the time goes in v2:
time: 123 us
  blocking collectives  81.4 us (66%)
  starting transfers between devices  23.4 us (19%)
  Pallas kernels  7.62 us (6%)
  waiting for transfers between devices  6.66 us (5%)
  local copies, waits for them, and re-layouts  3.68 us (3%)
    all_to_all x1, blocking collectives, shards(): lax.all_to_all(moments, PLANE, split_axis=0, concat_axis=0, tiled=True)  54.8 us
    all_to_all x1, blocking collectives, shards(): lax.all_to_all(carried, PLANE, split_axis=0, concat_axis=0, tiled=True)  26.5 us
    ppermute x2, starting transfers between devices, route(): return lax.ppermute(value, axes, pairs)  16.5 us
    ppermute x3, starting transfers between devices, across_cores(): return lax.ppermute(value, 'core', [(0, 1), (1, 0)])  6.87 us
    ppermute x2, waiting for transfers between devices, route(): return lax.ppermute(value, axes, pairs)  3.83 us
    ppermute x3, waiting for transfers between devices, across_cores(): return lax.ppermute(value, 'core', [(0, 1), (1, 0)])  2.83 us
  transfers between devices with their start and end apart: 5, of which 4 were waited for; matrix products, arithmetic and copies ran while one was open for 1% of the time, Pallas kernels for 3%

profile of v2, /device:TPU:33, one launch (start us, length us, event | category | flops | bytes accessed | tf_op | source)
XLA Modules:
  0.0 122.8 jit_solution(10168319359689489863)
XLA Ops:
  0.0 2.6 %collective-permute-start.1 = (f32[4,2,32,1024]{3,2,1,0:T(8,128)}, f32[4,2,32,1024]{3,2,1,0:T(8,128)S(1)}, u32[]{:S(2)}, u32[]{:S(2)}) collective-permute-start(f32[4,2,32,1024]{3,2,1,0:T(8,128)} %own_ref.5), channel_id=1, source_target_pairs={{0,8},{8,0},{1,9},{9,1},{2,10},{10,2},{3,11},{11,3},{4,12},{12,4},... | collective-permute-start | bytes 3145736 | tf_op jit(solution)/shard_map/ppermute | solution.py:240
  2.6 0.9 dynamic-slice_bitcast_fusion
  3.5 14.4 %collective-permute-start = (f32[32,1024]{1,0:T(8,128)S(1)}, f32[32,1024]{1,0:T(8,128)S(1)}, u32[]{:S(2)}, u32[]{:S(2)}) collective-permute-start(f32[32,1024]{1,0:T(8,128)S(1)} %dynamic-slice_bitcast_fusion), channel_id=1, source_target_pairs={{8,16},{16,8},{24,32},{32,24},{40,48},{48,40},{56,64},{64,56},{72,... | collective-permute-start | bytes 393224 | tf_op jit(solution)/shard_map/ppermute | solution.py:237
  18.0 0.0 collective-permute-done.1.other_ref
  18.0 0.0 copy-start
  18.0 1.2 copy-done
  19.2 0.0 copy-start.1
  19.2 2.1 %collective-permute-start.2 = (f32[16,1024]{1,0:T(8,128)S(1)}, f32[16,1024]{1,0:T(8,128)S(1)}, u32[]{:S(2)}, u32[]{:S(2)}) collective-permute-start(f32[16,1024]{1,0:T(8,128)S(1)} %row_ends.1), channel_id=1, source_target_pairs={{0,15},{1,8},{2,9},{3,10},{4,11},{5,12},{6,13},{7,14},{8,1},{9,2},... | collective-permute-start | bytes 196616 | tf_op jit(solution)/shard_map/ppermute | solution.py:237
  21.3 2.3 %coefficients.1 = (f32[16,128]{1,0:T(8,128)}, f32[8,128]{1,0:T(8,128)}) custom-call(f32[1,128]{1,0:T(1,128)} %bitcast.3, f32[4]{0:T(128)} %dif_ref.1), custom_call_target="tpu_custom_call" | custom-call | tf_op jit(solution)/shard_map/coefficients/pallas_call | solution.py:264
  23.6 0.0 copy-start.5
  23.6 2.5 %collective-permute-done.2.halo_ref = f32[16,1024]{1,0:T(8,128)S(1)} collective-permute-done((f32[16,1024]{1,0:T(8,128)S(1)}, f32[16,1024]{1,0:T(8,128)S(1)}, u32[]{:S(2)}, u32[]{:S(2)}) %collective-permute-start.2) | collective-permute-done | bytes 65568 | tf_op jit(solution)/shard_map/ppermute | solution.py:237
  26.1 0.0 copy-done.1
  26.1 0.0 copy-done.5
  26.1 0.0 copy-start.2
  26.1 0.7 copy-done.2
  26.8 0.0 copy-start.3
  26.8 1.9 %local_step.1 = (f32[4,4,16,1024]{3,2,1,0:T(8,128)S(1)}, f32[32,4,8,128]{3,2,1,0:T(8,128)S(1)}) custom-call(f32[4,2,32,1024]{3,2,1,0:T(8,128)S(1)} %copy-done.1, f32[4,2,32,1024]{3,2,1,0:T(8,128)S(1)} %collective-permute-done.1.other_ref, f32[16,1024]{1,0:T(8,128)S(1)} %collective-permute-done.2.halo_ref, f32[16,128]{1,0:T(8,128)S(1)} %copy-done.2, ...), custom_call_target="tpu_custom_call" | custom-call | tf_op jit(solution)/shard_map/local_step/pallas_call | solution.py:273
  28.7 1.3 %collective-permute-done.far_ref = f32[32,1024]{1,0:T(8,128)S(1)} collective-permute-done((f32[32,1024]{1,0:T(8,128)S(1)}, f32[32,1024]{1,0:T(8,128)S(1)}, u32[]{:S(2)}, u32[]{:S(2)}) %collective-permute-start) | collective-permute-done | bytes 131104 | tf_op jit(solution)/shard_map/ppermute | solution.py:237
  30.0 1.9 %collective-permute-start.3 = (f32[32,1024]{1,0:T(8,128)S(1)}, f32[32,1024]{1,0:T(8,128)S(1)}, u32[]{:S(2)}, u32[]{:S(2)}) collective-permute-start(f32[32,1024]{1,0:T(8,128)S(1)} %collective-permute-done.far_ref), channel_id=1, source_target_pairs={{0,8},{8,0},{1,9},{9,1},{2,10},{10,2},{3,11},{11,3},{4,12},{12,4},... | collective-permute-start | bytes 393224 | tf_op jit(solution)/shard_map/ppermute | solution.py:240
  32.0 1.3 %collective-permute-done.3.near_ref = f32[32,1024]{1,0:T(8,128)S(1)} collective-permute-done((f32[32,1024]{1,0:T(8,128)S(1)}, f32[32,1024]{1,0:T(8,128)S(1)}, u32[]{:S(2)}, u32[]{:S(2)}) %collective-permute-start.3) | collective-permute-done | bytes 131104 | tf_op jit(solution)/shard_map/ppermute | solution.py:240
  33.3 0.0 copy-done.3
  33.3 0.8 edge_products.1
  34.1 0.0 copy-start.4
  34.1 54.8 %all_to_all.10.in_ref = f32[32,4,8,128]{3,2,1,0:T(8,128)S(1)} all-to-all(f32[32,4,8,128]{3,2,1,0:T(8,128)S(1)} %get-tuple-element.22), channel_id=1, replica_groups=mesh['y'=4,'x'=4,'zh'=2,'core'=2,'zl'=8] {'y','x','zh'}, dimensions={0} | all-to-all | bytes 1048576 | tf_op jit(solution)/shard_map/all_to_all | solution.py:293
  89.0 0.0 copy-done.4
  89.0 0.7 scan_chips.1
  89.7 26.5 %all_to_all.11.carry_ref = f32[32,4,8,128]{3,2,1,0:T(8,128)S(1)} all-to-all(f32[32,4,8,128]{3,2,1,0:T(8,128)S(1)} %scan_chips.1), channel_id=1, replica_groups=mesh['y'=4,'x'=4,'zh'=2,'core'=2,'zl'=8] {'y','x','zh'}, dimensions={0} | all-to-all | bytes 1048576 | tf_op jit(solution)/shard_map/all_to_all | solution.py:302
  116.2 1.9 %finish.1 = (f32[4,2,32,1024]{3,2,1,0:T(8,128)}, f32[4,2,16,1024]{3,2,1,0:T(8,128)S(1)}) custom-call(f32[4,4,16,1024]{3,2,1,0:T(8,128)S(1)} %get-tuple-element.19.part_ref, f32[32,4,8,128]{3,2,1,0:T(8,128)S(1)} %all_to_all.11.carry_ref, f32[32,4,8,128]{3,2,1,0:T(8,128)S(1)} %get-tuple-element.24.mine_ref, f32[16,128]{1,0:T(8,128)S(1)} %copy-done.3), custom_call_target="tpu_custom_call" | custom-call | tf_op jit(solution)/shard_map/finish/pallas_call | solution.py:304
  118.1 2.4 %collective-permute-start.4 = (f32[4,2,16,1024]{3,2,1,0:T(8,128)S(1)}, f32[4,2,16,1024]{3,2,1,0:T(8,128)S(1)}, u32[]{:S(2)}, u32[]{:S(2)}) collective-permute-start(f32[4,2,16,1024]{3,2,1,0:T(8,128)S(1)} %get-tuple-element.26), channel_id=1, source_target_pairs={{0,8},{8,0},{1,9},{9,1},{2,10},{10,2},{3,11},{11,3},{4,12},{12,4},... | collective-permute-start | bytes 1572872 | tf_op jit(solution)/shard_map/ppermute | solution.py:240
  120.5 1.5 %collective-permute-done.4 = f32[4,2,16,1024]{3,2,1,0:T(8,128)S(1)} collective-permute-done((f32[4,2,16,1024]{3,2,1,0:T(8,128)S(1)}, f32[4,2,16,1024]{3,2,1,0:T(8,128)S(1)}, u32[]{:S(2)}, u32[]{:S(2)}) %collective-permute-start.4) | collective-permute-done | bytes 524320 | tf_op jit(solution)/shard_map/ppermute | solution.py:240
  122.0 0.8 constant_dynamic-update-slice_fusion
  (1 shorter events, 0.0 us)
Async XLA Ops:
  0.0 18.0 %collective-permute-start.1 = (f32[4,2,32,1024]{3,2,1,0:T(8,128)}, f32[4,2,32,1024]{3,2,1,0:T(8,128)S(1)}, u32[]{:S(2)}, u32[]{:S(2)}) collective-permute-start(f32[4,2,32,1024]{3,2,1,0:T(8,128)} %own_ref.5), channel_id=1, source_target_pairs={{0,8},{8,0},{1,9},{9,1},{2,10},{10,2},{3,11},{11,3},{4,12},{12,4},... | collective-permute-start | bytes 3145736 | tf_op jit(solution)/shard_map/ppermute | solution.py:240
  3.5 26.5 %collective-permute-start = (f32[32,1024]{1,0:T(8,128)S(1)}, f32[32,1024]{1,0:T(8,128)S(1)}, u32[]{:S(2)}, u32[]{:S(2)}) collective-permute-start(f32[32,1024]{1,0:T(8,128)S(1)} %dynamic-slice_bitcast_fusion), channel_id=1, source_target_pairs={{8,16},{16,8},{24,32},{32,24},{40,48},{48,40},{56,64},{64,56},{72,... | collective-permute-start | bytes 393224 | tf_op jit(solution)/shard_map/ppermute | solution.py:237
  18.0 1.2 copy-start
  19.2 6.9 %copy-start.1 = (f32[4,2,32,1024]{3,2,1,0:T(8,128)S(1)}, f32[4,2,32,1024]{3,2,1,0:T(8,128)}, u32[]{:S(2)}) copy-start(f32[4,2,32,1024]{3,2,1,0:T(8,128)} %own_ref.5) | copy-start | bytes 3145732
  19.2 6.9 %collective-permute-start.2 = (f32[16,1024]{1,0:T(8,128)S(1)}, f32[16,1024]{1,0:T(8,128)S(1)}, u32[]{:S(2)}, u32[]{:S(2)}) collective-permute-start(f32[16,1024]{1,0:T(8,128)S(1)} %row_ends.1), channel_id=1, source_target_pairs={{0,15},{1,8},{2,9},{3,10},{4,11},{5,12},{6,13},{7,14},{8,1},{9,2},... | collective-permute-start | bytes 196616 | tf_op jit(solution)/shard_map/ppermute | solution.py:237
  23.6 2.5 %copy-start.5 = (f32[4]{0:T(128)S(1)}, f32[4]{0:T(128)}, u32[]{:S(2)}) copy-start(f32[4]{0:T(128)} %dif_ref.1) | copy-start | bytes 52
  26.1 0.7 copy-start.2
  26.8 6.5 %copy-start.3 = (f32[16,128]{1,0:T(8,128)S(1)}, f32[16,128]{1,0:T(8,128)}, u32[]{:S(2)}) copy-start(f32[16,128]{1,0:T(8,128)} %get-tuple-element.16.cf_ref) | copy-start | bytes 24580
  30.0 3.2 %collective-permute-start.3 = (f32[32,1024]{1,0:T(8,128)S(1)}, f32[32,1024]{1,0:T(8,128)S(1)}, u32[]{:S(2)}, u32[]{:S(2)}) collective-permute-start(f32[32,1024]{1,0:T(8,128)S(1)} %collective-permute-done.far_ref), channel_id=1, source_target_pairs={{0,8},{8,0},{1,9},{9,1},{2,10},{10,2},{3,11},{11,3},{4,12},{12,4},... | collective-permute-start | bytes 393224 | tf_op jit(solution)/shard_map/ppermute | solution.py:240
  34.1 54.9 %copy-start.4 = (f32[8,128]{1,0:T(8,128)S(1)}, f32[8,128]{1,0:T(8,128)}, u32[]{:S(2)}) copy-start(f32[8,128]{1,0:T(8,128)} %get-tuple-element.23.cf_ref) | copy-start | bytes 12292
  118.1 3.9 %collective-permute-start.4 = (f32[4,2,16,1024]{3,2,1,0:T(8,128)S(1)}, f32[4,2,16,1024]{3,2,1,0:T(8,128)S(1)}, u32[]{:S(2)}, u32[]{:S(2)}) collective-permute-start(f32[4,2,16,1024]{3,2,1,0:T(8,128)S(1)} %get-tuple-element.26), channel_id=1, source_target_pairs={{0,8},{8,0},{1,9},{9,1},{2,10},{10,2},{3,11},{11,3},{4,12},{12,4},... | collective-permute-start | bytes 1572872 | tf_op jit(solution)/shard_map/ppermute | solution.py:240

commit v3 on v2

--- a/solution.py
+++ b/solution.py
@@ -1,3 +1,5 @@
+import functools
+
 import jax
 import jax.numpy as jnp
 import numpy as np
@@ -14,7 +16,7 @@
 AXES = ("y", "x", "zh", "core", "zl")
 ROW = AXES[:4]
 PLANE = AXES[:3]
-LIMIT = 48 * 2**20
+LIMIT = 12 * 2**20
 
 
 def whole(space=pltpu.VMEM):
@@ -69,10 +71,24 @@
     gc = jnp.where(row < 4, g, time_step / across)
     four = rs * pltpu.roll(rs, 127, 1)
     four = four * pltpu.roll(four, 126, 1)
-    scan_ref[...] = four
+    scan_ref[...] = four * pltpu.roll(four, 124, 1)
     turn = lax.rem(129 - 4 * chip_index(), 128)
     own_ref[0:8, :] = pltpu.roll(rs, turn, 1)
     own_ref[8:16, :] = pltpu.roll(gc, turn, 1)
+    own_ref[16:24, :] = pltpu.roll(four, turn, 1)
+
+
+def pair_factors(cf_ref, c):
+    lower = lax.axis_index("zh") == 0
+    r0 = jnp.where(lower, cf_ref[16 + c, 2], cf_ref[16 + c, 126])
+    r1 = jnp.where(lower, cf_ref[16 + c, 6], cf_ref[16 + c, 2])
+    s0 = jnp.where(lower, cf_ref[20 + c, 0], cf_ref[20 + c, 124])
+    s1 = jnp.where(lower, cf_ref[20 + c, 4], cf_ref[20 + c, 0])
+    return lower, r0, r1, s0, s1
+
+
+def piece(half, block, down):
+    return 8 * down + 4 * half + block // 2
 
 
 def ends_kernel(own_ref, other_ref, out_ref):
@@ -83,7 +99,7 @@
             out_ref[at : at + 1, :] = jnp.where(first, ref[c, k, 0:1, :], ref[c, k, 31:32, :])
 
 
-def local_kernel(own_ref, other_ref, halo_ref, cf_ref, dif_ref, part_ref, send_ref):
+def local_kernel(own_ref, other_ref, halo_ref, cf_ref, dif_ref, part_ref, *send_refs):
     core = lax.axis_index("core")
     first = core == 0
     sub = lax.broadcasted_iota(jnp.int32, (8, 1024), 0)
@@ -151,11 +167,14 @@
             b = s[0] * (b + gs[0])
             for block in range(8):
                 lanes = slice(128 * block, 128 * block + 128)
-                send_ref[8 * half + block, c] = p[:, lanes]
-                send_ref[16 + 8 * half + block, c] = b[:, lanes]
-
-
-def edges_kernel(own_ref, other_ref, far_ref, near_ref, moments_ref, cf_ref, send_ref, mine_ref):
+                send_refs[c // 2][piece(half, block, 0), c % 2, block % 2] = p[:, lanes]
+                send_refs[c // 2][piece(half, block, 1), c % 2, block % 2] = b[:, lanes]
+
+
+def edges_kernel(
+    own_ref, other_ref, far_ref, near_ref, raw01_ref, raw23_ref, cf_ref,
+    sum01_ref, sum23_ref, scaled_ref, mine01_ref, mine23_ref,
+):
     core = lax.axis_index("core")
     first = core == 0
     for half in range(2):
@@ -164,6 +183,11 @@
         w_low = jnp.where(first, far, near) * -cf_ref[12, 0]
         w_high = jnp.where(first, near, far) * cf_ref[12, 5]
         for c in range(4):
+            raw_ref, sum_ref, mine_ref = (
+                (raw01_ref, sum01_ref, mine01_ref),
+                (raw23_ref, sum23_ref, mine23_ref),
+            )[c // 2]
+            lower, _, r1, s0, _ = pair_factors(cf_ref, c)
             r = [cf_ref[c, j] for j in range(6)]
             s = [cf_ref[4 + c, j] for j in range(6)]
             lowest = jnp.where(first, own_ref[c, 0, rows, :], other_ref[c, 0, rows, :])
@@ -174,49 +198,87 @@
             q = (s[0] * s[1] * s[2] * s[3]) * from_high + low
             for block in range(8):
                 lanes = slice(128 * block, 128 * block + 128)
-                up, down = 8 * half + block, 16 + 8 * half + block
-                send_ref[up, c] = moments_ref[up, c] + p[:, lanes]
-                send_ref[down, c] = moments_ref[down, c] + q[:, lanes]
-                mine_ref[up, c] = from_low[:, lanes]
-                mine_ref[down, c] = from_high[:, lanes]
-
-
-def scan_kernel(in_ref, cf_ref, out_ref):
+                up = piece(half, block, 0), c % 2, block % 2
+                down = piece(half, block, 1), c % 2, block % 2
+                total_p, total_q = raw_ref[up] + p[:, lanes], raw_ref[down] + q[:, lanes]
+                sum_ref[up] = total_p
+                sum_ref[down] = total_q
+                mine_ref[up] = from_low[:, lanes]
+                mine_ref[down] = from_high[:, lanes]
+                if c >= 2:
+                    scaled_ref[up] = jnp.where(lower, r1, 1.0) * total_p
+                    scaled_ref[down] = jnp.where(lower, 1.0, s0) * total_q
+
+
+def pair_kernel(own_ref, partner_ref, cf_ref, out_ref):
+    for c in range(2):
+        lower, _, r1, s0, _ = pair_factors(cf_ref, c)
+        own_p, partner_p = jnp.where(lower, r1, 1.0), jnp.where(lower, 1.0, r1)
+        own_q, partner_q = jnp.where(lower, 1.0, s0), jnp.where(lower, s0, 1.0)
+        out_ref[0:8, c] = own_p * own_ref[0:8, c] + partner_p * partner_ref[0:8, c]
+        out_ref[8:16, c] = own_q * own_ref[8:16, c] + partner_q * partner_ref[8:16, c]
+
+
+def scan_kernel(base, in_ref, cf_ref, out_ref):
     upward = lax.axis_index("y") < 2
 
     @pl.when(upward)
     def _():
-        for c in range(4):
-            carry = jnp.zeros((8, 128), jnp.float32)
-            for chip in range(32):
-                out_ref[chip, c] = carry
-                carry = cf_ref[c, 4 * chip + 1] * carry + in_ref[chip, c]
+        for c in range(2):
+            carry = jnp.zeros((2, 8, 128), jnp.float32)
+            for pair in range(16):
+                out_ref[pair, c] = carry
+                carry = cf_ref[base + c, 8 * pair + 1] * carry + in_ref[pair, c]
 
     @pl.when(jnp.logical_not(upward))
     def _():
-        for c in range(4):
-            carry = jnp.zeros((8, 128), jnp.float32)
-            for chip in range(31, -1, -1):
-                out_ref[chip, c] = carry
-                carry = cf_ref[4 + c, (4 * chip + 127) % 128] * carry + in_ref[chip, c]
-
-
-def finish_kernel(part_ref, carry_ref, mine_ref, cf_ref, out_ref, send_ref):
+        for c in range(2):
+            carry = jnp.zeros((2, 8, 128), jnp.float32)
+            for pair in range(15, -1, -1):
+                out_ref[pair, c] = carry
+                carry = cf_ref[4 + base + c, (8 * pair + 127) % 128] * carry + in_ref[pair, c]
+
+
+def crossing_kernel(own_ref, carry_ref, cf_ref, out_ref):
+    for c in range(2):
+        lower, r0, _, _, s1 = pair_factors(cf_ref, 2 + c)
+        up, down = carry_ref[0:8, c], carry_ref[8:16, c]
+        out_ref[0:8, c] = jnp.where(lower, r0 * up + own_ref[0:8, c], up)
+        out_ref[8:16, c] = jnp.where(lower, down, s1 * down + own_ref[8:16, c])
+
+
+def finish_kernel(
+    part_ref, carry01_ref, partner01_ref, mine01_ref, carry23_ref, partner23_ref, mine23_ref,
+    cf_ref, out_ref, send_ref,
+):
     core = lax.axis_index("core")
     for c in range(4):
+        carry_ref, partner_ref, mine_ref = (
+            (carry01_ref, partner01_ref, mine01_ref),
+            (carry23_ref, partner23_ref, mine23_ref),
+        )[c // 2]
+        lower, r0, _, _, s1 = pair_factors(cf_ref, c)
+        by_p, by_q = jnp.where(lower, 1.0, r0), jnp.where(lower, s1, 1.0)
         r = [cf_ref[c, j] for j in range(6)]
         s = [cf_ref[4 + c, j] for j in range(6)]
-        up = [1.0, r[2], r[2] * r[3], r[2] * r[3] * r[4]]
-        down = [s[1] * s[2] * s[3], s[2] * s[3], s[3], 1.0]
+        rise = [1.0, r[2], r[2] * r[3], r[2] * r[3] * r[4]]
+        fall = [s[1] * s[2] * s[3], s[2] * s[3], s[3], 1.0]
         for half in range(2):
             here = slice(8 * half, 8 * half + 8)
             rows = pl.ds(pl.multiple_of(core * 16 + 8 * half, 8), 8)
             for block in range(8):
                 lanes = slice(128 * block, 128 * block + 128)
-                p = carry_ref[8 * half + block, c] + mine_ref[8 * half + block, c]
-                q = carry_ref[16 + 8 * half + block, c] + mine_ref[16 + 8 * half + block, c]
+                up = piece(half, block, 0), c % 2, block % 2
+                down = piece(half, block, 1), c % 2, block % 2
+                p = by_p * carry_ref[up] + mine_ref[up]
+                q = by_q * carry_ref[down] + mine_ref[down]
+                if c < 2:
+                    p = p + jnp.where(lower, 0.0, partner_ref[up])
+                    q = q + jnp.where(lower, partner_ref[down], 0.0)
+                else:
+                    p, q = p + partner_ref[up], q + partner_ref[down]
                 x = [
-                    part_ref[c, level, here, lanes] + up[level] * p + down[level] * q
+                    part_ref[c, level, here, lanes] + rise[level] * p + fall[level] * q
                     for level in range(4)
                 ]
                 for k in range(2):
@@ -263,55 +325,64 @@
 
     own_cf, scan_cf = pl.pallas_call(
         coefficients_kernel,
-        out_shape=(jax.ShapeDtypeStruct((16, 128), f32), jax.ShapeDtypeStruct((8, 128), f32)),
+        out_shape=(jax.ShapeDtypeStruct((24, 128), f32), jax.ShapeDtypeStruct((8, 128), f32)),
         in_specs=[whole(), whole(pltpu.SMEM)],
         out_specs=(whole(), whole()),
         name="coefficients",
     )(spacing.reshape(1, 128), diffusivity)
 
-    pieces = jax.ShapeDtypeStruct((32, 4, 8, 128), f32)
-    part, moments = pl.pallas_call(
+    def call(kernel, name, outs, *args):
+        smem = {id(own_cf), id(scan_cf), id(diffusivity)}
+        return pl.pallas_call(
+            kernel,
+            out_shape=outs,
+            in_specs=[whole(pltpu.SMEM if id(a) in smem else pltpu.VMEM) for a in args],
+            out_specs=jax.tree.map(lambda _: whole(), outs),
+            compiler_params=params(),
+            name=name,
+        )(*args)
+
+    def in_plane(value):
+        return lax.all_to_all(value, ("y", "x"), split_axis=0, concat_axis=0, tiled=True)
+
+    def to_partner(value):
+        return lax.ppermute(value, "zh", [(0, 1), (1, 0)])
+
+    def scanned(value, base):
+        kernel = functools.partial(scan_kernel, base)
+        return in_plane(call(kernel, "scan_pairs", pieces, in_plane(value), scan_cf))
+
+    def array(*shape):
+        return jax.ShapeDtypeStruct(shape, f32)
+
+    pieces = array(16, 2, 2, 8, 128)
+    halo, w_far, own_cf, scan_cf = lax.optimization_barrier((halo, w_far, own_cf, scan_cf))
+    w_near = across_cores(w_far)
+    part, raw01, raw23 = call(
         local_kernel,
-        out_shape=(jax.ShapeDtypeStruct((4, 4, 16, 1024), f32), pieces),
-        in_specs=[whole()] * 3 + [whole(pltpu.SMEM)] * 2,
-        out_specs=(whole(), whole()),
-        compiler_params=params(),
-        name="local_step",
-    )(flow_state, other, halo, own_cf, diffusivity)
-
-    w_far, moments, part = lax.optimization_barrier((w_far, moments, part))
-    w_near = across_cores(w_far)
-    moments, mine = pl.pallas_call(
+        "local_step",
+        (array(4, 4, 16, 1024), pieces, pieces),
+        flow_state, other, halo, own_cf, diffusivity,
+    )
+    sum01, sum23, scaled, mine01, mine23 = call(
         edges_kernel,
-        out_shape=(pieces, pieces),
-        in_specs=[whole()] * 5 + [whole(pltpu.SMEM)],
-        out_specs=(whole(), whole()),
-        compiler_params=params(),
-        name="edge_products",
-    )(flow_state, other, w_far, w_near, moments, own_cf)
-
-    arrived = lax.all_to_all(moments, PLANE, split_axis=0, concat_axis=0, tiled=True)
-    carried = pl.pallas_call(
-        scan_kernel,
-        out_shape=pieces,
-        in_specs=[whole(), whole(pltpu.SMEM)],
-        out_specs=whole(),
-        compiler_params=params(),
-        name="scan_chips",
-    )(arrived, scan_cf)
-    returned = lax.all_to_all(carried, PLANE, split_axis=0, concat_axis=0, tiled=True)
-
-    kept, leaving = pl.pallas_call(
+        "edge_products",
+        (pieces,) * 5,
+        flow_state, other, w_far, w_near, raw01, raw23, own_cf,
+    )
+
+    partner01 = to_partner(sum01)
+    carry23 = scanned(scaled, 2)
+    leaving23 = call(crossing_kernel, "crossing", pieces, sum23, carry23, own_cf)
+    partner01, leaving23 = lax.optimization_barrier((partner01, leaving23))
+    partner23 = to_partner(leaving23)
+    carry01 = scanned(call(pair_kernel, "pair_moments", pieces, sum01, partner01, own_cf), 0)
+    kept, leaving = call(
         finish_kernel,
-        out_shape=(
-            jax.ShapeDtypeStruct((4, 2, 32, 1024), f32),
-            jax.ShapeDtypeStruct((4, 2, 16, 1024), f32),
-        ),
-        in_specs=[whole(), whole(), whole(), whole(pltpu.SMEM)],
-        out_specs=(whole(), whole()),
-        compiler_params=params(),
-        name="finish",
-    )(part, returned, mine, own_cf)
+        "finish",
+        (array(4, 2, 32, 1024), array(4, 2, 16, 1024)),
+        part, carry01, partner01, mine01, carry23, partner23, mine23, own_cf,
+    )
     back = across_cores(leaving)
     return lax.dynamic_update_slice_in_dim(kept, back, 16 * (1 - core), 2)
 

time: 123 us -> 127 us (1.033)
  the two profiles are of different devices: /device:TPU:33 before, /device:TPU:1 now
where the time goes in v3:
time: 127 us; the launch traced here: 125 us
  starting transfers between devices  78.1 us (61%)
  waiting for transfers between devices  14.5 us (11%)
  blocking collectives  14.4 us (11%)
  Pallas kernels  11.6 us (9%)
  local copies, waits for them, and re-layouts  6.5 us (5%)
    ppermute x2, starting transfers between devices, to_partner(): return lax.ppermute(value, 'zh', [(0, 1), (1, 0)])  26.8 us
    ppermute x3, starting transfers between devices, across_cores(): return lax.ppermute(value, 'core', [(0, 1), (1, 0)])  20.7 us
    all_to_all x3, starting transfers between devices, in_plane(): lax.all_to_all(value, ('y', 'x'), split_axis=0, concat_axis=0, tiled=True)  18.6 us
    all_to_all x1, blocking collectives, in_plane(): lax.all_to_all(value, ('y', 'x'), split_axis=0, concat_axis=0, tiled=True)  14.4 us
    ppermute x2, starting transfers between devices, route(): return lax.ppermute(value, axes, pairs)  12 us
    ppermute x2, waiting for transfers between devices, to_partner(): return lax.ppermute(value, 'zh', [(0, 1), (1, 0)])  9.26 us
    pallas_call x7, Pallas kernels, call(): pl.pallas_call(kernel, out_shape=outs, in_specs=[whole(pltpu.SMEM if id(a...  9.18 us
    unnamed x26, local copies, waits for them, and re-layouts  4.76 us
  transfers between devices with their start and end apart: 10, of which 5 were waited for; matrix products, arithmetic and copies ran while one was open for 1% of the time, Pallas kernels for 6%

profile of v3, /device:TPU:1, one launch (start us, length us, event | category | flops | bytes accessed | tf_op | source)
XLA Modules:
  0.0 125.4 jit_solution(2103631406425126756)
XLA Ops:
  0.0 8.8 %collective-permute-start = (f32[4,2,32,1024]{3,2,1,0:T(8,128)}, f32[4,2,32,1024]{3,2,1,0:T(8,128)S(1)}, u32[]{:S(2)}, u32[]{:S(2)}) collective-permute-start(f32[4,2,32,1024]{3,2,1,0:T(8,128)} %own_ref.5), channel_id=1, source_target_pairs={{0,8},{8,0},{1,9},{9,1},{2,10},{10,2},{3,11},{11,3},{4,12},{12,4},... | collective-permute-start | bytes 3145736 | tf_op jit(solution)/shard_map/ppermute | solution.py:302
  8.8 0.9 dynamic-slice_bitcast_fusion
  9.7 10.0 %collective-permute-start.2 = (f32[32,1024]{1,0:T(8,128)S(1)}, f32[32,1024]{1,0:T(8,128)S(1)}, u32[]{:S(2)}, u32[]{:S(2)}) collective-permute-start(f32[32,1024]{1,0:T(8,128)S(1)} %dynamic-slice_bitcast_fusion), channel_id=1, source_target_pairs={{8,16},{16,8},{24,32},{32,24},{40,48},{48,40},{56,64},{64,56},{72,... | collective-permute-start | bytes 393224 | tf_op jit(solution)/shard_map/ppermute | solution.py:299
  19.7 1.2 copy-done
  21.0 2.1 %collective-permute-start.1 = (f32[16,1024]{1,0:T(8,128)S(1)}, f32[16,1024]{1,0:T(8,128)S(1)}, u32[]{:S(2)}, u32[]{:S(2)}) collective-permute-start(f32[16,1024]{1,0:T(8,128)S(1)} %row_ends.1), channel_id=1, source_target_pairs={{0,15},{1,8},{2,9},{3,10},{4,11},{5,12},{6,13},{7,14},{8,1},{9,2},... | collective-permute-start | bytes 196616 | tf_op jit(solution)/shard_map/ppermute | solution.py:299
  23.0 2.3 %coefficients.1 = (f32[24,128]{1,0:T(8,128)}, f32[8,128]{1,0:T(8,128)}) custom-call(f32[1,128]{1,0:T(1,128)} %bitcast.3, f32[4]{0:T(128)} %dif_ref.1), custom_call_target="tpu_custom_call" | custom-call | tf_op jit(solution)/shard_map/coefficients/pallas_call | solution.py:326
  25.4 2.6 %collective-permute-done.1.halo_ref = f32[16,1024]{1,0:T(8,128)S(1)} collective-permute-done((f32[16,1024]{1,0:T(8,128)S(1)}, f32[16,1024]{1,0:T(8,128)S(1)}, u32[]{:S(2)}, u32[]{:S(2)}) %collective-permute-start.1) | collective-permute-done | bytes 65568 | tf_op jit(solution)/shard_map/ppermute | solution.py:299
  28.0 7.2 %collective-permute-start.3 = (f32[32,1024]{1,0:T(8,128)S(1)}, f32[32,1024]{1,0:T(8,128)S(1)}, u32[]{:S(2)}, u32[]{:S(2)}) collective-permute-start(f32[32,1024]{1,0:T(8,128)S(1)} %collective-permute-done.2.far_ref), channel_id=1, source_target_pairs={{0,8},{8,0},{1,9},{9,1},{2,10},{10,2},{3,11},{11,3},{4,12},{12,4},... | collective-permute-start | bytes 393224 | tf_op jit(solution)/shard_map/ppermute | solution.py:302
  35.2 0.7 copy-done.2
  35.9 2.0 %local_step.1 = (f32[4,4,16,1024]{3,2,1,0:T(8,128)S(1)}, f32[16,2,2,8,128]{4,3,2,1,0:T(8,128)S(1)}, f32[16,2,2,8,128]{4,3,2,1,0:T(8,128)S(1)}) custom-call(f32[4,2,32,1024]{3,2,1,0:T(8,128)S(1)} %copy-done.1, f32[4,2,32,1024]{3,2,1,0:T(8,128)S(1)} %collective-permute-done.other_ref, f32[16,1024]{1,0:T(8,128)S(1)} %collective-permute-done.1.halo_ref, ...), custom_call_target="tpu_custom_call" | custom-call | tf_op jit(solution)/shard_map/local_step/pallas_call | solution.py:336
  38.0 0.9 edge_products.1
  38.9 0.7 copy-done.4
  39.6 0.7 copy-done.6
  40.3 0.7 copy-done.8
  41.0 0.7 copy-done.10
  41.7 8.3 %all-to-all-start = ((f32[16,2,2,8,128]{4,3,2,1,0:T(8,128)}), f32[16,2,2,8,128]{4,3,2,1,0:T(8,128)S(1)}, u32[]{:S(2)}, u32[]{:S(2)}) async-start(f32[16,2,2,8,128]{4,3,2,1,0:T(8,128)} %copy-done.10), calls=%async_computation | async-start | bytes 524288 | tf_op jit(solution)/shard_map/all_to_all | solution.py:346
  50.0 10.8 %collective-permute-start.4 = (f32[16,2,2,8,128]{4,3,2,1,0:T(8,128)S(1)}, f32[16,2,2,8,128]{4,3,2,1,0:T(8,128)S(1)}, u32[]{:S(2)}, u32[]{:S(2)}) collective-permute-start(f32[16,2,2,8,128]{4,3,2,1,0:T(8,128)S(1)} %copy-done.7), channel_id=1, source_target_pairs={{0,16},{16,0},{1,17},{17,1},{2,18},{18,2},{3,19},{19,3},{4,20},{20... | collective-permute-start | bytes 786440 | tf_op jit(solution)/shard_map/ppermute | solution.py:349
  60.8 0.7 scan_pairs.2
  61.5 14.4 %all_to_all.20.carry_ref.carry23_ref = f32[16,2,2,8,128]{4,3,2,1,0:T(8,128)S(1)} all-to-all(f32[16,2,2,8,128]{4,3,2,1,0:T(8,128)S(1)} %scan_pairs.2), channel_id=1, replica_groups=mesh['y'=4,'x'=4,'zh'=2,'core'=2,'zl'=8] {'y','x'}, dimensions={0} | all-to-all | bytes 524288 | tf_op jit(solution)/shard_map/all_to_all | solution.py:346
  75.9 0.8 crossing.1
  76.7 2.8 %collective-permute-done.4.partner_ref.partner01_ref = f32[16,2,2,8,128]{4,3,2,1,0:T(8,128)S(1)} collective-permute-done((f32[16,2,2,8,128]{4,3,2,1,0:T(8,128)S(1)}, f32[16,2,2,8,128]{4,3,2,1,0:T(8,128)S(1)}, u32[]{:S(2)}, u32[]{:S(2)}) %collective-permute-start.4) | collective-permute-done | bytes 262176 | tf_op jit(solution)/shard_map/ppermute | solution.py:349
  79.5 1.5 %pair_moments.1 = f32[16,2,2,8,128]{4,3,2,1,0:T(8,128)} custom-call(f32[16,2,2,8,128]{4,3,2,1,0:T(8,128)S(1)} %copy-done.7, f32[16,2,2,8,128]{4,3,2,1,0:T(8,128)S(1)} %collective-permute-done.4.partner_ref.partner01_ref, f32[24,128]{1,0:T(8,128)S(1)} %copy-done.3), custom_call_target="tpu_custom_call" | custom-call | tf_op jit(solution)/shard_map/pair_moments/pallas_call | solution.py:336
  81.0 3.5 %all-to-all-start.2 = ((f32[16,2,2,8,128]{4,3,2,1,0:T(8,128)}), f32[16,2,2,8,128]{4,3,2,1,0:T(8,128)S(1)}, u32[]{:S(2)}, u32[]{:S(2)}) async-start(f32[16,2,2,8,128]{4,3,2,1,0:T(8,128)} %pair_moments.1), calls=%async_computation.2 | async-start | bytes 524288 | tf_op jit(solution)/shard_map/all_to_all | solution.py:346
  84.5 16.0 %collective-permute-start.5 = (f32[16,2,2,8,128]{4,3,2,1,0:T(8,128)S(1)}, f32[16,2,2,8,128]{4,3,2,1,0:T(8,128)S(1)}, u32[]{:S(2)}, u32[]{:S(2)}) collective-permute-start(f32[16,2,2,8,128]{4,3,2,1,0:T(8,128)S(1)} %crossing.1), channel_id=1, source_target_pairs={{0,16},{16,0},{1,17},{17,1},{2,18},{18,2},{3,19},{19,3},{4,20},{20... | collective-permute-start | bytes 786440 | tf_op jit(solution)/shard_map/ppermute | solution.py:349
  100.5 1.4 %scan_pairs.3 = f32[16,2,2,8,128]{4,3,2,1,0:T(8,128)} custom-call(f32[16,2,2,8,128]{4,3,2,1,0:T(8,128)S(1)} %all-to-all-done.2.in_ref, f32[8,128]{1,0:T(8,128)S(1)} %copy-done.11), custom_call_target="tpu_custom_call" | custom-call | tf_op jit(solution)/shard_map/scan_pairs/pallas_call | solution.py:336
  101.9 6.8 %all-to-all-start.3 = ((f32[16,2,2,8,128]{4,3,2,1,0:T(8,128)}), f32[16,2,2,8,128]{4,3,2,1,0:T(8,128)S(1)}, u32[]{:S(2)}, u32[]{:S(2)}) async-start(f32[16,2,2,8,128]{4,3,2,1,0:T(8,128)} %scan_pairs.3), calls=%async_computation.3 | async-start | bytes 524288 | tf_op jit(solution)/shard_map/all_to_all | solution.py:346
  108.7 6.5 %collective-permute-done.5.partner23_ref = f32[16,2,2,8,128]{4,3,2,1,0:T(8,128)S(1)} collective-permute-done((f32[16,2,2,8,128]{4,3,2,1,0:T(8,128)S(1)}, f32[16,2,2,8,128]{4,3,2,1,0:T(8,128)S(1)}, u32[]{:S(2)}, u32[]{:S(2)}) %collective-permute-start.5) | collective-permute-done | bytes 262176 | tf_op jit(solution)/shard_map/ppermute | solution.py:349
  115.2 1.2 all-to-all-done.3.carry01_ref
  116.3 1.9 %finish.1 = (f32[4,2,32,1024]{3,2,1,0:T(8,128)}, f32[4,2,16,1024]{3,2,1,0:T(8,128)S(1)}) custom-call(f32[4,4,16,1024]{3,2,1,0:T(8,128)S(1)} %get-tuple-element.27.part_ref, f32[16,2,2,8,128]{4,3,2,1,0:T(8,128)S(1)} %all-to-all-done.3.carry01_ref, f32[16,2,2,8,128]{4,3,2,1,0:T(8,128)S(1)} %collective-permute-done.4.partner_ref.partner01_ref, ...), custom_call_target="tpu_custom_call" | custom-call | tf_op jit(solution)/shard_map/finish/pallas_call | solution.py:336
  118.3 4.7 %collective-permute-start.6 = (f32[4,2,16,1024]{3,2,1,0:T(8,128)S(1)}, f32[4,2,16,1024]{3,2,1,0:T(8,128)S(1)}, u32[]{:S(2)}, u32[]{:S(2)}) collective-permute-start(f32[4,2,16,1024]{3,2,1,0:T(8,128)S(1)} %get-tuple-element.40), channel_id=1, source_target_pairs={{0,8},{8,0},{1,9},{9,1},{2,10},{10,2},{3,11},{11,3},{4,12},{12,4},... | collective-permute-start | bytes 1572872 | tf_op jit(solution)/shard_map/ppermute | solution.py:302
  123.0 1.5 %collective-permute-done.6 = f32[4,2,16,1024]{3,2,1,0:T(8,128)S(1)} collective-permute-done((f32[4,2,16,1024]{3,2,1,0:T(8,128)S(1)}, f32[4,2,16,1024]{3,2,1,0:T(8,128)S(1)}, u32[]{:S(2)}, u32[]{:S(2)}) %collective-permute-start.6) | collective-permute-done | bytes 524320 | tf_op jit(solution)/shard_map/ppermute | solution.py:302
  124.5 0.8 constant_dynamic-update-slice_fusion
  (26 shorter events, 0.1 us)
Async XLA Ops:
  0.0 19.7 %collective-permute-start = (f32[4,2,32,1024]{3,2,1,0:T(8,128)}, f32[4,2,32,1024]{3,2,1,0:T(8,128)S(1)}, u32[]{:S(2)}, u32[]{:S(2)}) collective-permute-start(f32[4,2,32,1024]{3,2,1,0:T(8,128)} %own_ref.5), channel_id=1, source_target_pairs={{0,8},{8,0},{1,9},{9,1},{2,10},{10,2},{3,11},{11,3},{4,12},{12,4},... | collective-permute-start | bytes 3145736 | tf_op jit(solution)/shard_map/ppermute | solution.py:302
  9.7 15.7 %collective-permute-start.2 = (f32[32,1024]{1,0:T(8,128)S(1)}, f32[32,1024]{1,0:T(8,128)S(1)}, u32[]{:S(2)}, u32[]{:S(2)}) collective-permute-start(f32[32,1024]{1,0:T(8,128)S(1)} %dynamic-slice_bitcast_fusion), channel_id=1, source_target_pairs={{8,16},{16,8},{24,32},{32,24},{40,48},{48,40},{56,64},{64,56},{72,... | collective-permute-start | bytes 393224 | tf_op jit(solution)/shard_map/ppermute | solution.py:299
  19.7 1.2 copy-start
  20.9 14.2 %copy-start.1 = (f32[4,2,32,1024]{3,2,1,0:T(8,128)S(1)}, f32[4,2,32,1024]{3,2,1,0:T(8,128)}, u32[]{:S(2)}) copy-start(f32[4,2,32,1024]{3,2,1,0:T(8,128)} %own_ref.5) | copy-start | bytes 3145732
  21.0 7.0 %collective-permute-start.1 = (f32[16,1024]{1,0:T(8,128)S(1)}, f32[16,1024]{1,0:T(8,128)S(1)}, u32[]{:S(2)}, u32[]{:S(2)}) collective-permute-start(f32[16,1024]{1,0:T(8,128)S(1)} %row_ends.1), channel_id=1, source_target_pairs={{0,15},{1,8},{2,9},{3,10},{4,11},{5,12},{6,13},{7,14},{8,1},{9,2},... | collective-permute-start | bytes 196616 | tf_op jit(solution)/shard_map/ppermute | solution.py:299
  28.0 7.2 %copy-start.12 = (f32[4]{0:T(128)S(1)}, f32[4]{0:T(128)}, u32[]{:S(2)}) copy-start(f32[4]{0:T(128)} %dif_ref.1) | copy-start | bytes 52
  28.0 10.0 %collective-permute-start.3 = (f32[32,1024]{1,0:T(8,128)S(1)}, f32[32,1024]{1,0:T(8,128)S(1)}, u32[]{:S(2)}, u32[]{:S(2)}) collective-permute-start(f32[32,1024]{1,0:T(8,128)S(1)} %collective-permute-done.2.far_ref), channel_id=1, source_target_pairs={{0,8},{8,0},{1,9},{9,1},{2,10},{10,2},{3,11},{11,3},{4,12},{12,4},... | collective-permute-start | bytes 393224 | tf_op jit(solution)/shard_map/ppermute | solution.py:302
  35.2 0.7 copy-start.2
  35.9 2.1 %copy-start.3 = (f32[24,128]{1,0:T(8,128)S(1)}, f32[24,128]{1,0:T(8,128)}, u32[]{:S(2)}) copy-start(f32[24,128]{1,0:T(8,128)} %get-tuple-element.26.cf_ref) | copy-start | bytes 36868
  38.9 0.7 copy-start.4
  39.6 0.7 copy-start.6
  40.3 0.7 copy-start.8
  41.0 0.7 copy-start.10
  41.7 8.3 %copy-start.7 = (f32[16,2,2,8,128]{4,3,2,1,0:T(8,128)S(1)}, f32[16,2,2,8,128]{4,3,2,1,0:T(8,128)}, u32[]{:S(2)}) copy-start(f32[16,2,2,8,128]{4,3,2,1,0:T(8,128)} %copy-done.6) | copy-start | bytes 786436
  41.7 19.1 %copy-start.11 = (f32[8,128]{1,0:T(8,128)S(1)}, f32[8,128]{1,0:T(8,128)}, u32[]{:S(2)}) copy-start(f32[8,128]{1,0:T(8,128)} %get-tuple-element.34.cf_ref) | copy-start | bytes 12292
  41.7 19.1 %all-to-all-start = ((f32[16,2,2,8,128]{4,3,2,1,0:T(8,128)}), f32[16,2,2,8,128]{4,3,2,1,0:T(8,128)S(1)}, u32[]{:S(2)}, u32[]{:S(2)}) async-start(f32[16,2,2,8,128]{4,3,2,1,0:T(8,128)} %copy-done.10), calls=%async_computation | async-start | bytes 524288 | tf_op jit(solution)/shard_map/all_to_all | solution.py:346
  50.0 29.4 %collective-permute-start.4 = (f32[16,2,2,8,128]{4,3,2,1,0:T(8,128)S(1)}, f32[16,2,2,8,128]{4,3,2,1,0:T(8,128)S(1)}, u32[]{:S(2)}, u32[]{:S(2)}) collective-permute-start(f32[16,2,2,8,128]{4,3,2,1,0:T(8,128)S(1)} %copy-done.7), channel_id=1, source_target_pairs={{0,16},{16,0},{1,17},{17,1},{2,18},{18,2},{3,19},{19,3},{4,20},{20... | collective-permute-start | bytes 786440 | tf_op jit(solution)/shard_map/ppermute | solution.py:349
  61.5 14.4 %copy-start.9 = (f32[16,2,2,8,128]{4,3,2,1,0:T(8,128)S(1)}, f32[16,2,2,8,128]{4,3,2,1,0:T(8,128)}, u32[]{:S(2)}) copy-start(f32[16,2,2,8,128]{4,3,2,1,0:T(8,128)} %copy-done.8) | copy-start | bytes 786436
  81.0 19.6 %all-to-all-start.2 = ((f32[16,2,2,8,128]{4,3,2,1,0:T(8,128)}), f32[16,2,2,8,128]{4,3,2,1,0:T(8,128)S(1)}, u32[]{:S(2)}, u32[]{:S(2)}) async-start(f32[16,2,2,8,128]{4,3,2,1,0:T(8,128)} %pair_moments.1), calls=%async_computation.2 | async-start | bytes 524288 | tf_op jit(solution)/shard_map/all_to_all | solution.py:346
  84.5 30.7 %collective-permute-start.5 = (f32[16,2,2,8,128]{4,3,2,1,0:T(8,128)S(1)}, f32[16,2,2,8,128]{4,3,2,1,0:T(8,128)S(1)}, u32[]{:S(2)}, u32[]{:S(2)}) collective-permute-start(f32[16,2,2,8,128]{4,3,2,1,0:T(8,128)S(1)} %crossing.1), channel_id=1, source_target_pairs={{0,16},{16,0},{1,17},{17,1},{2,18},{18,2},{3,19},{19,3},{4,20},{20... | collective-permute-start | bytes 786440 | tf_op jit(solution)/shard_map/ppermute | solution.py:349
  101.9 14.4 %copy-start.5 = (f32[16,2,2,8,128]{4,3,2,1,0:T(8,128)S(1)}, f32[16,2,2,8,128]{4,3,2,1,0:T(8,128)}, u32[]{:S(2)}) copy-start(f32[16,2,2,8,128]{4,3,2,1,0:T(8,128)} %copy-done.4) | copy-start | bytes 786436
  101.9 14.4 %all-to-all-start.3 = ((f32[16,2,2,8,128]{4,3,2,1,0:T(8,128)}), f32[16,2,2,8,128]{4,3,2,1,0:T(8,128)S(1)}, u32[]{:S(2)}, u32[]{:S(2)}) async-start(f32[16,2,2,8,128]{4,3,2,1,0:T(8,128)} %scan_pairs.3), calls=%async_computation.3 | async-start | bytes 524288 | tf_op jit(solution)/shard_map/all_to_all | solution.py:346
  118.3 6.3 %collective-permute-start.6 = (f32[4,2,16,1024]{3,2,1,0:T(8,128)S(1)}, f32[4,2,16,1024]{3,2,1,0:T(8,128)S(1)}, u32[]{:S(2)}, u32[]{:S(2)}) collective-permute-start(f32[4,2,16,1024]{3,2,1,0:T(8,128)S(1)} %get-tuple-element.40), channel_id=1, source_target_pairs={{0,8},{8,0},{1,9},{9,1},{2,10},{10,2},{3,11},{11,3},{4,12},{12,4},... | collective-permute-start | bytes 1572872 | tf_op jit(solution)/shard_map/ppermute | solution.py:302

commit v4 on v3

--- a/solution.py
+++ b/solution.py
@@ -71,7 +71,8 @@
     gc = jnp.where(row < 4, g, time_step / across)
     four = rs * pltpu.roll(rs, 127, 1)
     four = four * pltpu.roll(four, 126, 1)
-    scan_ref[...] = four * pltpu.roll(four, 124, 1)
+    scan_ref[0:8, :] = four * pltpu.roll(four, 124, 1)
+    scan_ref[8:16, :] = four
     turn = lax.rem(129 - 4 * chip_index(), 128)
     own_ref[0:8, :] = pltpu.roll(rs, turn, 1)
     own_ref[8:16, :] = pltpu.roll(gc, turn, 1)
@@ -171,9 +172,16 @@
                 send_refs[c // 2][piece(half, block, 1), c % 2, block % 2] = b[:, lanes]
 
 
+def weights(cf_ref, c):
+    r = [cf_ref[c, j] for j in range(6)]
+    s = [cf_ref[4 + c, j] for j in range(6)]
+    rise = [1.0, r[2], r[2] * r[3], r[2] * r[3] * r[4]]
+    return rise, [s[1] * s[2] * s[3], s[2] * s[3], s[3], 1.0]
+
+
 def edges_kernel(
-    own_ref, other_ref, far_ref, near_ref, raw01_ref, raw23_ref, cf_ref,
-    sum01_ref, sum23_ref, scaled_ref, mine01_ref, mine23_ref,
+    own_ref, other_ref, far_ref, near_ref, raw01_ref, raw23_ref, old_ref, cf_ref,
+    sum01_ref, sum23_ref, part_ref,
 ):
     core = lax.axis_index("core")
     first = core == 0
@@ -183,11 +191,7 @@
         w_low = jnp.where(first, far, near) * -cf_ref[12, 0]
         w_high = jnp.where(first, near, far) * cf_ref[12, 5]
         for c in range(4):
-            raw_ref, sum_ref, mine_ref = (
-                (raw01_ref, sum01_ref, mine01_ref),
-                (raw23_ref, sum23_ref, mine23_ref),
-            )[c // 2]
-            lower, _, r1, s0, _ = pair_factors(cf_ref, c)
+            raw_ref, sum_ref = ((raw01_ref, sum01_ref), (raw23_ref, sum23_ref))[c // 2]
             r = [cf_ref[c, j] for j in range(6)]
             s = [cf_ref[4 + c, j] for j in range(6)]
             lowest = jnp.where(first, own_ref[c, 0, rows, :], other_ref[c, 0, rows, :])
@@ -200,14 +204,14 @@
                 lanes = slice(128 * block, 128 * block + 128)
                 up = piece(half, block, 0), c % 2, block % 2
                 down = piece(half, block, 1), c % 2, block % 2
-                total_p, total_q = raw_ref[up] + p[:, lanes], raw_ref[down] + q[:, lanes]
-                sum_ref[up] = total_p
-                sum_ref[down] = total_q
-                mine_ref[up] = from_low[:, lanes]
-                mine_ref[down] = from_high[:, lanes]
-                if c >= 2:
-                    scaled_ref[up] = jnp.where(lower, r1, 1.0) * total_p
-                    scaled_ref[down] = jnp.where(lower, 1.0, s0) * total_q
+                sum_ref[up] = raw_ref[up] + p[:, lanes]
+                sum_ref[down] = raw_ref[down] + q[:, lanes]
+            rise, fall = weights(cf_ref, c)
+            here = slice(8 * half, 8 * half + 8)
+            for level in range(4):
+                part_ref[c, level, here, :] = old_ref[c, level, here, :] + (
+                    rise[level] * from_low + fall[level] * from_high
+                )
 
 
 def pair_kernel(own_ref, partner_ref, cf_ref, out_ref):
@@ -221,6 +225,11 @@
 
 def scan_kernel(base, in_ref, cf_ref, out_ref):
     upward = lax.axis_index("y") < 2
+    lower = lax.axis_index("zh") == 0
+
+    def scaled(pair, c, at, by):
+        value = in_ref[pair, c]
+        return value if base == 0 else jnp.where(by, cf_ref[8 + at, (8 * pair + 5 if at < 4 else 8 * pair + 127) % 128], 1.0) * value
 
     @pl.when(upward)
     def _():
@@ -228,7 +237,7 @@
             carry = jnp.zeros((2, 8, 128), jnp.float32)
             for pair in range(16):
                 out_ref[pair, c] = carry
-                carry = cf_ref[base + c, 8 * pair + 1] * carry + in_ref[pair, c]
+                carry = cf_ref[base + c, 8 * pair + 1] * carry + scaled(pair, c, base + c, lower)
 
     @pl.when(jnp.logical_not(upward))
     def _():
@@ -236,7 +245,9 @@
             carry = jnp.zeros((2, 8, 128), jnp.float32)
             for pair in range(15, -1, -1):
                 out_ref[pair, c] = carry
-                carry = cf_ref[4 + base + c, (8 * pair + 127) % 128] * carry + in_ref[pair, c]
+                at = 4 + base + c
+                kept = cf_ref[at, (8 * pair + 127) % 128] * carry
+                carry = kept + scaled(pair, c, at, jnp.logical_not(lower))
 
 
 def crossing_kernel(own_ref, carry_ref, cf_ref, out_ref):
@@ -248,21 +259,17 @@
 
 
 def finish_kernel(
-    part_ref, carry01_ref, partner01_ref, mine01_ref, carry23_ref, partner23_ref, mine23_ref,
-    cf_ref, out_ref, send_ref,
+    part_ref, carry01_ref, partner01_ref, carry23_ref, partner23_ref, cf_ref, out_ref, send_ref
 ):
     core = lax.axis_index("core")
     for c in range(4):
-        carry_ref, partner_ref, mine_ref = (
-            (carry01_ref, partner01_ref, mine01_ref),
-            (carry23_ref, partner23_ref, mine23_ref),
+        carry_ref, partner_ref = (
+            (carry01_ref, partner01_ref),
+            (carry23_ref, partner23_ref),
         )[c // 2]
         lower, r0, _, _, s1 = pair_factors(cf_ref, c)
         by_p, by_q = jnp.where(lower, 1.0, r0), jnp.where(lower, s1, 1.0)
-        r = [cf_ref[c, j] for j in range(6)]
-        s = [cf_ref[4 + c, j] for j in range(6)]
-        rise = [1.0, r[2], r[2] * r[3], r[2] * r[3] * r[4]]
-        fall = [s[1] * s[2] * s[3], s[2] * s[3], s[3], 1.0]
+        rise, fall = weights(cf_ref, c)
         for half in range(2):
             here = slice(8 * half, 8 * half + 8)
             rows = pl.ds(pl.multiple_of(core * 16 + 8 * half, 8), 8)
@@ -270,8 +277,8 @@
                 lanes = slice(128 * block, 128 * block + 128)
                 up = piece(half, block, 0), c % 2, block % 2
                 down = piece(half, block, 1), c % 2, block % 2
-                p = by_p * carry_ref[up] + mine_ref[up]
-                q = by_q * carry_ref[down] + mine_ref[down]
+                p = by_p * carry_ref[up]
+                q = by_q * carry_ref[down]
                 if c < 2:
                     p = p + jnp.where(lower, 0.0, partner_ref[up])
                     q = q + jnp.where(lower, partner_ref[down], 0.0)
@@ -325,13 +332,14 @@
 
     own_cf, scan_cf = pl.pallas_call(
         coefficients_kernel,
-        out_shape=(jax.ShapeDtypeStruct((24, 128), f32), jax.ShapeDtypeStruct((8, 128), f32)),
+        out_shape=(jax.ShapeDtypeStruct((24, 128), f32), jax.ShapeDtypeStruct((16, 128), f32)),
         in_specs=[whole(), whole(pltpu.SMEM)],
         out_specs=(whole(), whole()),
+        compiler_params=params(),
         name="coefficients",
     )(spacing.reshape(1, 128), diffusivity)
 
-    def call(kernel, name, outs, *args):
+    def call(kernel, name, outs, *args, **more):
         smem = {id(own_cf), id(scan_cf), id(diffusivity)}
         return pl.pallas_call(
             kernel,
@@ -340,6 +348,7 @@
             out_specs=jax.tree.map(lambda _: whole(), outs),
             compiler_params=params(),
             name=name,
+            **more,
         )(*args)
 
     def in_plane(value):
@@ -364,24 +373,30 @@
         (array(4, 4, 16, 1024), pieces, pieces),
         flow_state, other, halo, own_cf, diffusivity,
     )
-    sum01, sum23, scaled, mine01, mine23 = call(
+    sum01, sum23, part = call(
         edges_kernel,
         "edge_products",
-        (pieces,) * 5,
-        flow_state, other, w_far, w_near, raw01, raw23, own_cf,
+        (pieces, pieces, array(4, 4, 16, 1024)),
+        flow_state, other, w_far, w_near, raw01, raw23, part, own_cf,
+        input_output_aliases={4: 0, 5: 1, 6: 2},
     )
 
     partner01 = to_partner(sum01)
-    carry23 = scanned(scaled, 2)
+    once = lax.optimization_barrier(jnp.int32(1))
+    carry23 = lax.fori_loop(0, once, lambda _, value: scanned(value, 2), sum23)
     leaving23 = call(crossing_kernel, "crossing", pieces, sum23, carry23, own_cf)
-    partner01, leaving23 = lax.optimization_barrier((partner01, leaving23))
     partner23 = to_partner(leaving23)
-    carry01 = scanned(call(pair_kernel, "pair_moments", pieces, sum01, partner01, own_cf), 0)
+
+    def scan_pairs01(_, value):
+        return scanned(call(pair_kernel, "pair_moments", pieces, value, partner01, own_cf), 0)
+
+    sum01, _ = lax.optimization_barrier((sum01, leaving23))
+    carry01 = lax.fori_loop(0, once, scan_pairs01, sum01)
     kept, leaving = call(
         finish_kernel,
         "finish",
         (array(4, 2, 32, 1024), array(4, 2, 16, 1024)),
-        part, carry01, partner01, mine01, carry23, partner23, mine23, own_cf,
+        part, carry01, partner01, carry23, partner23, own_cf,
     )
     back = across_cores(leaving)
     return lax.dynamic_update_slice_in_dim(kept, back, 16 * (1 - core), 2)

time: 127 us -> 118 us (0.929)
  starting transfers between devices: 78.1 us -> 51.3 us
  blocking collectives: 14.4 us -> 31.1 us
  waiting for transfers between devices: 14.5 us -> 20.3 us
  local copies, waits for them, and re-layouts: 6.5 us -> 3 us
    ppermute x2, starting transfers between devices: 26.8 us -> 9.43 us  [to_partner(): return lax.ppermute(value, 'zh', [(0, 1), (1, 0)])]
    all_to_all x1 -> x2, blocking collectives: 14.4 us -> 31.1 us  [in_plane(): lax.all_to_all(value, ('y', 'x'), split_axis=0, concat_axis=0, tiled=True)]
    all_to_all x3 -> x2, waiting for transfers between devices: 1.16 us -> 15.3 us  [in_plane(): lax.all_to_all(value, ('y', 'x'), split_axis=0, concat_axis=0, tiled=True)]
    all_to_all x3 -> x2, starting transfers between devices: 18.6 us -> 7.07 us  [in_plane(): lax.all_to_all(value, ('y', 'x'), split_axis=0, concat_axis=0, tiled=True)]
    ppermute x2, waiting for transfers between devices: 9.26 us -> 0.01 us  [to_partner(): return lax.ppermute(value, 'zh', [(0, 1), (1, 0)])]
    unnamed x26 -> x9, local copies, waits for them, and re-layouts: 4.76 us -> 1.26 us
    ppermute x3, starting transfers between devices: 20.7 us -> 22.8 us  [across_cores(): return lax.ppermute(value, 'core', [(0, 1), (1, 0)])]
  transfers between devices with their start and end apart: 10 -> 9, of which waited for: 5 -> 5; matrix products, arithmetic and copies ran while one was open for 1% -> 1% of each run, Pallas kernels for 6% -> 7%
where the time goes in v4:
time: 118 us; the launch traced here: 117 us
  starting transfers between devices  51.3 us (43%)
  blocking collectives  31.1 us (26%)
  waiting for transfers between devices  20.3 us (17%)
  Pallas kernels  11.1 us (9%)
  local copies, waits for them, and re-layouts  3 us (3%)
    all_to_all x2, blocking collectives, in_plane(): lax.all_to_all(value, ('y', 'x'), split_axis=0, concat_axis=0, tiled=True)  31.1 us
    ppermute x3, starting transfers between devices, across_cores(): return lax.ppermute(value, 'core', [(0, 1), (1, 0)])  22.8 us
    all_to_all x2, waiting for transfers between devices, in_plane(): lax.all_to_all(value, ('y', 'x'), split_axis=0, concat_axis=0, tiled=True)  15.3 us
    ppermute x2, starting transfers between devices, route(): return lax.ppermute(value, axes, pairs)  12 us
    pallas_call x7, Pallas kernels, call(): pl.pallas_call(kernel, out_shape=outs, in_specs=[whole(pltpu.SMEM if id(a...  9.58 us
    ppermute x2, starting transfers between devices, to_partner(): return lax.ppermute(value, 'zh', [(0, 1), (1, 0)])  9.43 us
    all_to_all x2, starting transfers between devices, in_plane(): lax.all_to_all(value, ('y', 'x'), split_axis=0, concat_axis=0, tiled=True)  7.07 us
    ppermute x2, waiting for transfers between devices, route(): return lax.ppermute(value, axes, pairs)  3.46 us
  transfers between devices with their start and end apart: 9, of which 5 were waited for; matrix products, arithmetic and copies ran while one was open for 1% of the time, Pallas kernels for 7%

profile of v4, /device:TPU:1, one launch (start us, length us, event | category | flops | bytes accessed | tf_op | source)
XLA Modules:
  0.0 117.0 jit_solution(9732080532294084470)
XLA Ops:
  0.0 8.8 %collective-permute-start = (f32[4,2,32,1024]{3,2,1,0:T(8,128)}, f32[4,2,32,1024]{3,2,1,0:T(8,128)S(1)}, u32[]{:S(2)}, u32[]{:S(2)}) collective-permute-start(f32[4,2,32,1024]{3,2,1,0:T(8,128)} %own_ref.5), channel_id=1, source_target_pairs={{0,8},{8,0},{1,9},{9,1},{2,10},{10,2},{3,11},{11,3},{4,12},{12,4},... | collective-permute-start | bytes 3145736 | tf_op jit(solution)/shard_map/ppermute | solution.py:309
  8.8 0.9 dynamic-slice_bitcast_fusion
  9.7 10.0 %collective-permute-start.2 = (f32[32,1024]{1,0:T(8,128)S(1)}, f32[32,1024]{1,0:T(8,128)S(1)}, u32[]{:S(2)}, u32[]{:S(2)}) collective-permute-start(f32[32,1024]{1,0:T(8,128)S(1)} %dynamic-slice_bitcast_fusion), channel_id=1, source_target_pairs={{8,16},{16,8},{24,32},{32,24},{40,48},{48,40},{56,64},{64,56},{72,... | collective-permute-start | bytes 393224 | tf_op jit(solution)/shard_map/ppermute | solution.py:306
  19.7 0.0 copy-start
  19.7 1.2 %copy-done = f32[4,2,32,1024]{3,2,1,0:T(8,128)S(1)} copy-done((f32[4,2,32,1024]{3,2,1,0:T(8,128)S(1)}, f32[4,2,32,1024]{3,2,1,0:T(8,128)}, u32[]{:S(2)}) %copy-start) | copy-done | bytes 1048600
  21.0 0.0 copy-start.2
  21.0 0.0 copy-start.3
  21.0 2.1 %collective-permute-start.1 = (f32[16,1024]{1,0:T(8,128)S(1)}, f32[16,1024]{1,0:T(8,128)S(1)}, u32[]{:S(2)}, u32[]{:S(2)}) collective-permute-start(f32[16,1024]{1,0:T(8,128)S(1)} %row_ends.1), channel_id=1, source_target_pairs={{0,15},{1,8},{2,9},{3,10},{4,11},{5,12},{6,13},{7,14},{8,1},{9,2},... | collective-permute-start | bytes 196616 | tf_op jit(solution)/shard_map/ppermute | solution.py:306
  23.1 1.5 %coefficients.1 = (f32[24,128]{1,0:T(8,128)S(1)}, f32[16,128]{1,0:T(8,128)S(1)}) custom-call(f32[1,128]{1,0:T(1,128)S(1)} %bitcast.3, f32[4]{0:T(128)S(1)} %copy-done.2), custom_call_target="tpu_custom_call" | custom-call | tf_op jit(solution)/shard_map/coefficients/pallas_call | solution.py:333
  24.5 0.5 collective-permute-done.2.far_ref
  25.1 2.9 %collective-permute-done.1.halo_ref = f32[16,1024]{1,0:T(8,128)S(1)} collective-permute-done((f32[16,1024]{1,0:T(8,128)S(1)}, f32[16,1024]{1,0:T(8,128)S(1)}, u32[]{:S(2)}, u32[]{:S(2)}) %collective-permute-start.1) | collective-permute-done | bytes 65568 | tf_op jit(solution)/shard_map/ppermute | solution.py:306
  28.0 7.0 %collective-permute-start.3 = (f32[32,1024]{1,0:T(8,128)S(1)}, f32[32,1024]{1,0:T(8,128)S(1)}, u32[]{:S(2)}, u32[]{:S(2)}) collective-permute-start(f32[32,1024]{1,0:T(8,128)S(1)} %collective-permute-done.2.far_ref), channel_id=1, source_target_pairs={{0,8},{8,0},{1,9},{9,1},{2,10},{10,2},{3,11},{11,3},{4,12},{12,4},... | collective-permute-start | bytes 393224 | tf_op jit(solution)/shard_map/ppermute | solution.py:309
  35.0 2.0 %local_step.1 = (f32[4,4,16,1024]{3,2,1,0:T(8,128)S(1)}, f32[16,2,2,8,128]{4,3,2,1,0:T(8,128)S(1)}, f32[16,2,2,8,128]{4,3,2,1,0:T(8,128)S(1)}) custom-call(f32[4,2,32,1024]{3,2,1,0:T(8,128)S(1)} %copy-done.1, f32[4,2,32,1024]{3,2,1,0:T(8,128)S(1)} %collective-permute-done.other_ref, f32[16,1024]{1,0:T(8,128)S(1)} %collective-permute-done.1.halo_ref, ...), custom_call_target="tpu_custom_call" | custom-call | tf_op jit(solution)/shard_map/local_step/pallas_call | solution.py:344
  37.1 1.3 %edge_products.1 = (f32[16,2,2,8,128]{4,3,2,1,0:T(8,128)S(1)}, f32[16,2,2,8,128]{4,3,2,1,0:T(8,128)S(1)}, f32[4,4,16,1024]{3,2,1,0:T(8,128)S(1)}) custom-call(f32[4,2,32,1024]{3,2,1,0:T(8,128)S(1)} %copy-done.1, f32[4,2,32,1024]{3,2,1,0:T(8,128)S(1)} %collective-permute-done.other_ref, ...), custom_call_target="tpu_custom_call", output_to_operand_aliasing={{0}: (4, {}), {1}: (5, {}), {2}: (6, {})} | custom-call | tf_op jit(solution)/shard_map/edge_products/pallas_call | solution.py:344
  38.3 5.6 %collective-permute-start.4 = (f32[16,2,2,8,128]{4,3,2,1,0:T(8,128)S(1)}, f32[16,2,2,8,128]{4,3,2,1,0:T(8,128)S(1)}, u32[]{:S(2)}, u32[]{:S(2)}) collective-permute-start(f32[16,2,2,8,128]{4,3,2,1,0:T(8,128)S(1)} %get-tuple-element.193), channel_id=1, source_target_pairs={{0,16},{16,0},{1,17},{17,1},{2,18},{18,2},{3,19},{19,3},{4,20},{20... | collective-permute-start | bytes 786440 | tf_op jit(solution)/shard_map/ppermute | solution.py:358
  44.0 33.2 %while.20 = (s32[]{:T(128)}, f32[16,2,2,8,128]{4,3,2,1,0:T(8,128)S(1)}, s32[]{:T(128)}, f32[16,128]{1,0:T(8,128)S(1)}, s32[]{:T(128)}) while((s32[]{:T(128)}, f32[16,2,2,8,128]{4,3,2,1,0:T(8,128)S(1)}, s32[]{:T(128)}, f32[16,128]{1,0:T(8,128)S(1)}, s32[]{:T(128)}) %tuple.35), condition=%wide.region_1.0_spmd, body=%wide.region_0.0_spmd.sunk | while | flops 2 | bytes 1310813 | solution.py:386
  44.0 20.7 %all_to_all.24.in_ref = f32[16,2,2,8,128]{4,3,2,1,0:T(8,128)S(1)} all-to-all(f32[16,2,2,8,128]{4,3,2,1,0:T(8,128)S(1)} %get-tuple-element.183), channel_id=1, replica_groups=mesh['y'=4,'x'=4,'zh'=2,'core'=2,'zl'=8] {'y','x'}, dimensions={0} | all-to-all | bytes 524288 | tf_op jit(solution)/shard_map/while/body/all_to_all | solution.py:355
  64.7 1.4 %scan_pairs.2 = f32[16,2,2,8,128]{4,3,2,1,0:T(8,128)} custom-call(f32[16,2,2,8,128]{4,3,2,1,0:T(8,128)S(1)} %all_to_all.24.in_ref, f32[16,128]{1,0:T(8,128)S(1)} %get-tuple-element.190.cf_ref), custom_call_target="tpu_custom_call" | custom-call | tf_op jit(solution)/shard_map/while/body/scan_pairs/pallas_call | solution.py:344
  66.1 3.5 %all-to-all-start.1 = ((f32[16,2,2,8,128]{4,3,2,1,0:T(8,128)}), f32[16,2,2,8,128]{4,3,2,1,0:T(8,128)S(1)}, u32[]{:S(2)}, u32[]{:S(2)}) async-start(f32[16,2,2,8,128]{4,3,2,1,0:T(8,128)} %scan_pairs.2), calls=%async_computation.1 | async-start | bytes 524288 | tf_op jit(solution)/shard_map/while/body/all_to_all | solution.py:355
  69.7 7.5 %all-to-all-done.1 = f32[16,2,2,8,128]{4,3,2,1,0:T(8,128)S(1)} async-done(((f32[16,2,2,8,128]{4,3,2,1,0:T(8,128)}), f32[16,2,2,8,128]{4,3,2,1,0:T(8,128)S(1)}, u32[]{:S(2)}, u32[]{:S(2)}) %all-to-all-start.1) | async-done | bytes 262176 | tf_op jit(solution)/shard_map/while/body/all_to_all | solution.py:355
  77.2 0.8 crossing.1
  77.9 3.8 %collective-permute-start.5 = (f32[16,2,2,8,128]{4,3,2,1,0:T(8,128)S(1)}, f32[16,2,2,8,128]{4,3,2,1,0:T(8,128)S(1)}, u32[]{:S(2)}, u32[]{:S(2)}) collective-permute-start(f32[16,2,2,8,128]{4,3,2,1,0:T(8,128)S(1)} %crossing.1), channel_id=1, source_target_pairs={{0,16},{16,0},{1,17},{17,1},{2,18},{18,2},{3,19},{19,3},{4,20},{20... | collective-permute-start | bytes 786440 | tf_op jit(solution)/shard_map/ppermute | solution.py:358
  81.8 24.0 %while.21 = (s32[]{:T(128)}, f32[16,2,2,8,128]{4,3,2,1,0:T(8,128)S(1)}, s32[]{:T(128)}, f32[16,2,2,8,128]{4,3,2,1,0:T(8,128)S(1)}, f32[24,128]{1,0:T(8,128)S(1)}, /*index=5*/f32[16,128]{1,0:T(8,128)S(1)}, s32[]{:T(128)}) while((s32[]{:T(128)}, f32[16,2,2,8,128]{4,3,2,1,0:T(8,128)S(1)}, s32[]{:T(128)}, f32[16,2,2,8,128]{4,3,2,1,0:T(8,128)S(1)}, ...), condition=%wide.region_3.0_spmd, body=%wide.region_2.0_spmd.sunk | while | flops 2 | bytes 1310829 | solution.py:394
  81.8 0.8 pair_moments.1
  82.6 10.5 %all_to_all.25.in_ref = f32[16,2,2,8,128]{4,3,2,1,0:T(8,128)S(1)} all-to-all(f32[16,2,2,8,128]{4,3,2,1,0:T(8,128)S(1)} %pair_moments.1), channel_id=1, replica_groups=mesh['y'=4,'x'=4,'zh'=2,'core'=2,'zl'=8] {'y','x'}, dimensions={0} | all-to-all | bytes 524288 | tf_op jit(solution)/shard_map/while/body/all_to_all | solution.py:355
  93.0 1.4 %scan_pairs.3 = f32[16,2,2,8,128]{4,3,2,1,0:T(8,128)} custom-call(f32[16,2,2,8,128]{4,3,2,1,0:T(8,128)S(1)} %all_to_all.25.in_ref, f32[16,128]{1,0:T(8,128)S(1)} %get-tuple-element.211.cf_ref), custom_call_target="tpu_custom_call" | custom-call | tf_op jit(solution)/shard_map/while/body/scan_pairs/pallas_call | solution.py:344
  94.5 3.5 %all-to-all-start.3 = ((f32[16,2,2,8,128]{4,3,2,1,0:T(8,128)}), f32[16,2,2,8,128]{4,3,2,1,0:T(8,128)S(1)}, u32[]{:S(2)}, u32[]{:S(2)}) async-start(f32[16,2,2,8,128]{4,3,2,1,0:T(8,128)} %scan_pairs.3), calls=%async_computation.3 | async-start | bytes 524288 | tf_op jit(solution)/shard_map/while/body/all_to_all | solution.py:355
  98.0 7.8 %all-to-all-done.3 = f32[16,2,2,8,128]{4,3,2,1,0:T(8,128)S(1)} async-done(((f32[16,2,2,8,128]{4,3,2,1,0:T(8,128)}), f32[16,2,2,8,128]{4,3,2,1,0:T(8,128)S(1)}, u32[]{:S(2)}, u32[]{:S(2)}) %all-to-all-start.3) | async-done | bytes 262176 | tf_op jit(solution)/shard_map/while/body/all_to_all | solution.py:355
  105.8 1.9 %finish.1 = (f32[4,2,32,1024]{3,2,1,0:T(8,128)}, f32[4,2,16,1024]{3,2,1,0:T(8,128)S(1)}) custom-call(f32[4,4,16,1024]{3,2,1,0:T(8,128)S(1)} %get-tuple-element.84.part_ref, f32[16,2,2,8,128]{4,3,2,1,0:T(8,128)S(1)} %get-tuple-element.90.carry01_ref, f32[16,2,2,8,128]{4,3,2,1,0:T(8,128)S(1)} %get-tuple-element.227, ...), custom_call_target="tpu_custom_call" | custom-call | tf_op jit(solution)/shard_map/finish/pallas_call | solution.py:344
  107.7 7.0 %collective-permute-start.6 = (f32[4,2,16,1024]{3,2,1,0:T(8,128)S(1)}, f32[4,2,16,1024]{3,2,1,0:T(8,128)S(1)}, u32[]{:S(2)}, u32[]{:S(2)}) collective-permute-start(f32[4,2,16,1024]{3,2,1,0:T(8,128)S(1)} %get-tuple-element.92), channel_id=1, source_target_pairs={{0,8},{8,0},{1,9},{9,1},{2,10},{10,2},{3,11},{11,3},{4,12},{12,4},... | collective-permute-start | bytes 1572872 | tf_op jit(solution)/shard_map/ppermute | solution.py:309
  114.7 1.5 %collective-permute-done.6 = f32[4,2,16,1024]{3,2,1,0:T(8,128)S(1)} collective-permute-done((f32[4,2,16,1024]{3,2,1,0:T(8,128)S(1)}, f32[4,2,16,1024]{3,2,1,0:T(8,128)S(1)}, u32[]{:S(2)}, u32[]{:S(2)}) %collective-permute-start.6) | collective-permute-done | bytes 524320 | tf_op jit(solution)/shard_map/ppermute | solution.py:309
  116.2 0.8 constant_dynamic-update-slice_fusion
  (10 shorter events, 0.1 us)
Async XLA Ops:
  0.0 19.7 %collective-permute-start = (f32[4,2,32,1024]{3,2,1,0:T(8,128)}, f32[4,2,32,1024]{3,2,1,0:T(8,128)S(1)}, u32[]{:S(2)}, u32[]{:S(2)}) collective-permute-start(f32[4,2,32,1024]{3,2,1,0:T(8,128)} %own_ref.5), channel_id=1, source_target_pairs={{0,8},{8,0},{1,9},{9,1},{2,10},{10,2},{3,11},{11,3},{4,12},{12,4},... | collective-permute-start | bytes 3145736 | tf_op jit(solution)/shard_map/ppermute | solution.py:309
  9.7 15.4 %collective-permute-start.2 = (f32[32,1024]{1,0:T(8,128)S(1)}, f32[32,1024]{1,0:T(8,128)S(1)}, u32[]{:S(2)}, u32[]{:S(2)}) collective-permute-start(f32[32,1024]{1,0:T(8,128)S(1)} %dynamic-slice_bitcast_fusion), channel_id=1, source_target_pairs={{8,16},{16,8},{24,32},{32,24},{40,48},{48,40},{56,64},{64,56},{72,... | collective-permute-start | bytes 393224 | tf_op jit(solution)/shard_map/ppermute | solution.py:306
  19.7 1.2 %copy-start = (f32[4,2,32,1024]{3,2,1,0:T(8,128)S(1)}, f32[4,2,32,1024]{3,2,1,0:T(8,128)}, u32[]{:S(2)}) copy-start(f32[4,2,32,1024]{3,2,1,0:T(8,128)} %own_ref.5) | copy-start | bytes 3145732
  20.9 14.1 %copy-start.1 = (f32[4,2,32,1024]{3,2,1,0:T(8,128)S(1)}, f32[4,2,32,1024]{3,2,1,0:T(8,128)}, u32[]{:S(2)}) copy-start(f32[4,2,32,1024]{3,2,1,0:T(8,128)} %own_ref.5) | copy-start | bytes 3145732
  21.0 2.1 %copy-start.2 = (f32[4]{0:T(128)S(1)}, f32[4]{0:T(128)}, u32[]{:S(2)}) copy-start(f32[4]{0:T(128)} %dif_ref.1) | copy-start | bytes 52
  21.0 2.1 %copy-start.3 = (f32[128]{0:T(128)S(1)}, f32[128]{0:T(128)}, u32[]{:S(2)}) copy-start(f32[128]{0:T(128)} %param.8) | copy-start | bytes 1540
  21.0 7.0 %collective-permute-start.1 = (f32[16,1024]{1,0:T(8,128)S(1)}, f32[16,1024]{1,0:T(8,128)S(1)}, u32[]{:S(2)}, u32[]{:S(2)}) collective-permute-start(f32[16,1024]{1,0:T(8,128)S(1)} %row_ends.1), channel_id=1, source_target_pairs={{0,15},{1,8},{2,9},{3,10},{4,11},{5,12},{6,13},{7,14},{8,1},{9,2},... | collective-permute-start | bytes 196616 | tf_op jit(solution)/shard_map/ppermute | solution.py:306
  28.0 9.0 %collective-permute-start.3 = (f32[32,1024]{1,0:T(8,128)S(1)}, f32[32,1024]{1,0:T(8,128)S(1)}, u32[]{:S(2)}, u32[]{:S(2)}) collective-permute-start(f32[32,1024]{1,0:T(8,128)S(1)} %collective-permute-done.2.far_ref), channel_id=1, source_target_pairs={{0,8},{8,0},{1,9},{9,1},{2,10},{10,2},{3,11},{11,3},{4,12},{12,4},... | collective-permute-start | bytes 393224 | tf_op jit(solution)/shard_map/ppermute | solution.py:309
  38.3 43.4 %collective-permute-start.4 = (f32[16,2,2,8,128]{4,3,2,1,0:T(8,128)S(1)}, f32[16,2,2,8,128]{4,3,2,1,0:T(8,128)S(1)}, u32[]{:S(2)}, u32[]{:S(2)}) collective-permute-start(f32[16,2,2,8,128]{4,3,2,1,0:T(8,128)S(1)} %get-tuple-element.193), channel_id=1, source_target_pairs={{0,16},{16,0},{1,17},{17,1},{2,18},{18,2},{3,19},{19,3},{4,20},{20... | collective-permute-start | bytes 786440 | tf_op jit(solution)/shard_map/ppermute | solution.py:358
  66.1 11.0 %all-to-all-start.1 = ((f32[16,2,2,8,128]{4,3,2,1,0:T(8,128)}), f32[16,2,2,8,128]{4,3,2,1,0:T(8,128)S(1)}, u32[]{:S(2)}, u32[]{:S(2)}) async-start(f32[16,2,2,8,128]{4,3,2,1,0:T(8,128)} %scan_pairs.2), calls=%async_computation.1 | async-start | bytes 524288 | tf_op jit(solution)/shard_map/while/body/all_to_all | solution.py:355
  77.9 27.9 %collective-permute-start.5 = (f32[16,2,2,8,128]{4,3,2,1,0:T(8,128)S(1)}, f32[16,2,2,8,128]{4,3,2,1,0:T(8,128)S(1)}, u32[]{:S(2)}, u32[]{:S(2)}) collective-permute-start(f32[16,2,2,8,128]{4,3,2,1,0:T(8,128)S(1)} %crossing.1), channel_id=1, source_target_pairs={{0,16},{16,0},{1,17},{17,1},{2,18},{18,2},{3,19},{19,3},{4,20},{20... | collective-permute-start | bytes 786440 | tf_op jit(solution)/shard_map/ppermute | solution.py:358
  94.5 11.3 %all-to-all-start.3 = ((f32[16,2,2,8,128]{4,3,2,1,0:T(8,128)}), f32[16,2,2,8,128]{4,3,2,1,0:T(8,128)S(1)}, u32[]{:S(2)}, u32[]{:S(2)}) async-start(f32[16,2,2,8,128]{4,3,2,1,0:T(8,128)} %scan_pairs.3), calls=%async_computation.3 | async-start | bytes 524288 | tf_op jit(solution)/shard_map/while/body/all_to_all | solution.py:355
  107.7 8.5 %collective-permute-start.6 = (f32[4,2,16,1024]{3,2,1,0:T(8,128)S(1)}, f32[4,2,16,1024]{3,2,1,0:T(8,128)S(1)}, u32[]{:S(2)}, u32[]{:S(2)}) collective-permute-start(f32[4,2,16,1024]{3,2,1,0:T(8,128)S(1)} %get-tuple-element.92), channel_id=1, source_target_pairs={{0,8},{8,0},{1,9},{9,1},{2,10},{10,2},{3,11},{11,3},{4,12},{12,4},... | collective-permute-start | bytes 1572872 | tf_op jit(solution)/shard_map/ppermute | solution.py:309

commit v5 on v4

--- a/solution.py
+++ b/solution.py
@@ -259,9 +259,11 @@
 
 
 def finish_kernel(
-    part_ref, carry01_ref, partner01_ref, carry23_ref, partner23_ref, cf_ref, out_ref, send_ref
+    kept, part_ref, carry01_ref, partner01_ref, carry23_ref, partner23_ref, cf_ref, out_ref
 ):
     core = lax.axis_index("core")
+    upper = (core == 1) if kept else (core == 0)
+    base = 2 * core if kept else 2 - 2 * core
     for c in range(4):
         carry_ref, partner_ref = (
             (carry01_ref, partner01_ref),
@@ -270,9 +272,11 @@
         lower, r0, _, _, s1 = pair_factors(cf_ref, c)
         by_p, by_q = jnp.where(lower, 1.0, r0), jnp.where(lower, s1, 1.0)
         rise, fall = weights(cf_ref, c)
+        rises = [jnp.where(upper, rise[2 + k], rise[k]) for k in range(2)]
+        falls = [jnp.where(upper, fall[2 + k], fall[k]) for k in range(2)]
         for half in range(2):
             here = slice(8 * half, 8 * half + 8)
-            rows = pl.ds(pl.multiple_of(core * 16 + 8 * half, 8), 8)
+            rows = pl.ds(pl.multiple_of(core * 16 + 8 * half, 8), 8) if kept else here
             for block in range(8):
                 lanes = slice(128 * block, 128 * block + 128)
                 up = piece(half, block, 0), c % 2, block % 2
@@ -284,13 +288,9 @@
                     q = q + jnp.where(lower, partner_ref[down], 0.0)
                 else:
                     p, q = p + partner_ref[up], q + partner_ref[down]
-                x = [
-                    part_ref[c, level, here, lanes] + rise[level] * p + fall[level] * q
-                    for level in range(4)
-                ]
                 for k in range(2):
-                    out_ref[c, k, rows, lanes] = jnp.where(core == 0, x[k], x[2 + k])
-                    send_ref[c, k, here, lanes] = jnp.where(core == 0, x[2 + k], x[k])
+                    own = part_ref[c, base + k, here, lanes]
+                    out_ref[c, k, rows, lanes] = own + rises[k] * p + falls[k] * q
 
 
 def shards(flow_state, spacing, diffusivity):
@@ -357,9 +357,15 @@
     def to_partner(value):
         return lax.ppermute(value, "zh", [(0, 1), (1, 0)])
 
-    def scanned(value, base):
+    def sent_back(value, base):
         kernel = functools.partial(scan_kernel, base)
-        return in_plane(call(kernel, "scan_pairs", pieces, in_plane(value), scan_cf))
+        return in_plane(call(kernel, "scan_pairs", pieces, value, scan_cf))
+
+    def in_loop(step, value):
+        once = lax.optimization_barrier(jnp.int32(1))
+        return lax.while_loop(
+            lambda state: state[0] > 0, lambda state: (jnp.int32(0), step(state[1])), (once, value)
+        )[1]
 
     def array(*shape):
         return jax.ShapeDtypeStruct(shape, f32)
@@ -382,23 +388,22 @@
     )
 
     partner01 = to_partner(sum01)
-    once = lax.optimization_barrier(jnp.int32(1))
-    carry23 = lax.fori_loop(0, once, lambda _, value: scanned(value, 2), sum23)
+    carry23 = in_loop(lambda value: sent_back(value, 2), in_plane(sum23))
     leaving23 = call(crossing_kernel, "crossing", pieces, sum23, carry23, own_cf)
     partner23 = to_partner(leaving23)
 
-    def scan_pairs01(_, value):
-        return scanned(call(pair_kernel, "pair_moments", pieces, value, partner01, own_cf), 0)
+    def scan_pairs01(value):
+        moments = call(pair_kernel, "pair_moments", pieces, value, partner01, own_cf)
+        return sent_back(in_plane(moments), 0)
 
     sum01, _ = lax.optimization_barrier((sum01, leaving23))
-    carry01 = lax.fori_loop(0, once, scan_pairs01, sum01)
-    kept, leaving = call(
-        finish_kernel,
-        "finish",
-        (array(4, 2, 32, 1024), array(4, 2, 16, 1024)),
-        part, carry01, partner01, carry23, partner23, own_cf,
+    carry01 = in_loop(scan_pairs01, sum01)
+    ready = part, carry01, partner01, carry23, partner23, own_cf
+    leaving = call(
+        functools.partial(finish_kernel, False), "finish_other", array(4, 2, 16, 1024), *ready
     )
     back = across_cores(leaving)
+    kept = call(functools.partial(finish_kernel, True), "finish_own", array(4, 2, 32, 1024), *ready)
     return lax.dynamic_update_slice_in_dim(kept, back, 16 * (1 - core), 2)
 
 

time: 118 us -> 125 us (1.059)
  the two profiles are of different devices: /device:TPU:1 before, /device:TPU:65 now
where the time goes in v5:
time: 125 us; the launch traced here: 124 us
  starting transfers between devices  74 us (59%)
  waiting for transfers between devices  19.7 us (16%)
  blocking collectives  14 us (11%)
  Pallas kernels  13.5 us (11%)
  local copies, waits for them, and re-layouts  3 us (2%)
    all_to_all x3, starting transfers between devices, in_plane(): lax.all_to_all(value, ('y', 'x'), split_axis=0, concat_axis=0, tiled=True)  23.5 us
    ppermute x3, starting transfers between devices, across_cores(): return lax.ppermute(value, 'core', [(0, 1), (1, 0)])  18.3 us
    ppermute x2, starting transfers between devices, to_partner(): return lax.ppermute(value, 'zh', [(0, 1), (1, 0)])  16.6 us
    ppermute x2, starting transfers between devices, route(): return lax.ppermute(value, axes, pairs)  15.6 us
    all_to_all x3, waiting for transfers between devices, in_plane(): lax.all_to_all(value, ('y', 'x'), split_axis=0, concat_axis=0, tiled=True)  15.3 us
    all_to_all x1, blocking collectives, in_plane(): lax.all_to_all(value, ('y', 'x'), split_axis=0, concat_axis=0, tiled=True)  14 us
    pallas_call x8, Pallas kernels, call(): pl.pallas_call(kernel, out_shape=outs, in_specs=[whole(pltpu.SMEM if id(a...  12 us
    ppermute x2, waiting for transfers between devices, route(): return lax.ppermute(value, axes, pairs)  2.82 us
  transfers between devices with their start and end apart: 10, of which 5 were waited for; matrix products, arithmetic and copies ran while one was open for 1% of the time, Pallas kernels for 9%

profile of v5, /device:TPU:65, one launch (start us, length us, event | category | flops | bytes accessed | tf_op | source)
XLA Modules:
  0.0 124.3 jit_solution(6311606967449340008)
XLA Ops:
  0.0 2.6 %collective-permute-start = (f32[4,2,32,1024]{3,2,1,0:T(8,128)}, f32[4,2,32,1024]{3,2,1,0:T(8,128)S(1)}, u32[]{:S(2)}, u32[]{:S(2)}) collective-permute-start(f32[4,2,32,1024]{3,2,1,0:T(8,128)} %own_ref.5), channel_id=1, source_target_pairs={{0,8},{8,0},{1,9},{9,1},{2,10},{10,2},{3,11},{11,3},{4,12},{12,4},... | collective-permute-start | bytes 3145736 | tf_op jit(solution)/shard_map/ppermute | solution.py:309
  2.6 0.9 dynamic-slice_bitcast_fusion
  3.5 13.5 %collective-permute-start.2 = (f32[32,1024]{1,0:T(8,128)S(1)}, f32[32,1024]{1,0:T(8,128)S(1)}, u32[]{:S(2)}, u32[]{:S(2)}) collective-permute-start(f32[32,1024]{1,0:T(8,128)S(1)} %dynamic-slice_bitcast_fusion), channel_id=1, source_target_pairs={{8,16},{16,8},{24,32},{32,24},{40,48},{48,40},{56,64},{64,56},{72,... | collective-permute-start | bytes 393224 | tf_op jit(solution)/shard_map/ppermute | solution.py:306
  17.1 0.0 copy-start
  17.1 1.2 copy-done
  18.3 0.0 copy-start.2
  18.4 2.1 %collective-permute-start.1 = (f32[16,1024]{1,0:T(8,128)S(1)}, f32[16,1024]{1,0:T(8,128)S(1)}, u32[]{:S(2)}, u32[]{:S(2)}) collective-permute-start(f32[16,1024]{1,0:T(8,128)S(1)} %row_ends.1), channel_id=1, source_target_pairs={{0,15},{1,8},{2,9},{3,10},{4,11},{5,12},{6,13},{7,14},{8,1},{9,2},... | collective-permute-start | bytes 196616 | tf_op jit(solution)/shard_map/ppermute | solution.py:306
  20.4 1.5 %coefficients.1 = (f32[24,128]{1,0:T(8,128)S(1)}, f32[16,128]{1,0:T(8,128)S(1)}) custom-call(f32[1,128]{1,0:T(1,128)S(1)} %bitcast.3, f32[4]{0:T(128)S(1)} %copy-done.2), custom_call_target="tpu_custom_call" | custom-call | tf_op jit(solution)/shard_map/coefficients/pallas_call | solution.py:333
  21.9 2.1 %collective-permute-done.2.far_ref = f32[32,1024]{1,0:T(8,128)S(1)} collective-permute-done((f32[32,1024]{1,0:T(8,128)S(1)}, f32[32,1024]{1,0:T(8,128)S(1)}, u32[]{:S(2)}, u32[]{:S(2)}) %collective-permute-start.2) | collective-permute-done | bytes 131104 | tf_op jit(solution)/shard_map/ppermute | solution.py:306
  24.0 0.7 collective-permute-done.1.halo_ref
  24.7 1.9 %collective-permute-start.3 = (f32[32,1024]{1,0:T(8,128)S(1)}, f32[32,1024]{1,0:T(8,128)S(1)}, u32[]{:S(2)}, u32[]{:S(2)}) collective-permute-start(f32[32,1024]{1,0:T(8,128)S(1)} %collective-permute-done.2.far_ref), channel_id=1, source_target_pairs={{0,8},{8,0},{1,9},{9,1},{2,10},{10,2},{3,11},{11,3},{4,12},{12,4},... | collective-permute-start | bytes 393224 | tf_op jit(solution)/shard_map/ppermute | solution.py:309
  26.7 2.7 %local_step.1 = (f32[4,4,16,1024]{3,2,1,0:T(8,128)S(1)}, f32[16,2,2,8,128]{4,3,2,1,0:T(8,128)S(1)}, f32[16,2,2,8,128]{4,3,2,1,0:T(8,128)}) custom-call(f32[4,2,32,1024]{3,2,1,0:T(8,128)S(1)} %copy-done.1, f32[4,2,32,1024]{3,2,1,0:T(8,128)S(1)} %collective-permute-done.other_ref, f32[16,1024]{1,0:T(8,128)S(1)} %collective-permute-done.1.halo_ref, ...), custom_call_target="tpu_custom_call" | custom-call | tf_op jit(solution)/shard_map/local_step/pallas_call | solution.py:344
  29.4 2.0 %edge_products.1 = (f32[16,2,2,8,128]{4,3,2,1,0:T(8,128)S(1)}, f32[16,2,2,8,128]{4,3,2,1,0:T(8,128)}, f32[4,4,16,1024]{3,2,1,0:T(8,128)S(1)}) custom-call(f32[4,2,32,1024]{3,2,1,0:T(8,128)S(1)} %copy-done.1, f32[4,2,32,1024]{3,2,1,0:T(8,128)S(1)} %collective-permute-done.other_ref, ...), custom_call_target="tpu_custom_call", output_to_operand_aliasing={{0}: (4, {}), {1}: (5, {}), {2}: (6, {})} | custom-call | tf_op jit(solution)/shard_map/edge_products/pallas_call | solution.py:344
  31.3 13.3 %all-to-all-start.3 = ((f32[16,2,2,8,128]{4,3,2,1,0:T(8,128)}), f32[16,2,2,8,128]{4,3,2,1,0:T(8,128)S(1)}, u32[]{:S(2)}, u32[]{:S(2)}) async-start(f32[16,2,2,8,128]{4,3,2,1,0:T(8,128)} %get-tuple-element.70.own_ref), calls=%async_computation.3 | async-start | bytes 524288 | tf_op jit(solution)/shard_map/all_to_all | solution.py:355
  44.7 11.8 %collective-permute-start.4 = (f32[16,2,2,8,128]{4,3,2,1,0:T(8,128)S(1)}, f32[16,2,2,8,128]{4,3,2,1,0:T(8,128)S(1)}, u32[]{:S(2)}, u32[]{:S(2)}) collective-permute-start(f32[16,2,2,8,128]{4,3,2,1,0:T(8,128)S(1)} %get-tuple-element.109), channel_id=1, source_target_pairs={{0,16},{16,0},{1,17},{17,1},{2,18},{18,2},{3,19},{19,3},{4,20},{20... | collective-permute-start | bytes 786440 | tf_op jit(solution)/shard_map/ppermute | solution.py:358
  56.5 15.9 %while.18 = (s32[]{:T(128)}, f32[16,2,2,8,128]{4,3,2,1,0:T(8,128)S(1)}, f32[16,128]{1,0:T(8,128)S(1)}) while((s32[]{:T(128)}, f32[16,2,2,8,128]{4,3,2,1,0:T(8,128)S(1)}, f32[16,128]{1,0:T(8,128)S(1)}) %tuple.25), condition=%region_1.0_spmd, body=%region_0.0_spmd | while | flops 1 | bytes 786505 | solution.py:366
  56.5 1.4 %scan_pairs.2 = f32[16,2,2,8,128]{4,3,2,1,0:T(8,128)} custom-call(f32[16,2,2,8,128]{4,3,2,1,0:T(8,128)S(1)} %get-tuple-element.103.in_ref, f32[16,128]{1,0:T(8,128)S(1)} %get-tuple-element.107.cf_ref), custom_call_target="tpu_custom_call" | custom-call | tf_op jit(solution)/shard_map/while/body/scan_pairs/pallas_call | solution.py:344
  58.0 6.6 %all-to-all-start = ((f32[16,2,2,8,128]{4,3,2,1,0:T(8,128)}), f32[16,2,2,8,128]{4,3,2,1,0:T(8,128)S(1)}, u32[]{:S(2)}, u32[]{:S(2)}) async-start(f32[16,2,2,8,128]{4,3,2,1,0:T(8,128)} %scan_pairs.2), calls=%async_computation | async-start | bytes 524288 | tf_op jit(solution)/shard_map/while/body/all_to_all | solution.py:355
  64.6 7.8 %all-to-all-done = f32[16,2,2,8,128]{4,3,2,1,0:T(8,128)S(1)} async-done(((f32[16,2,2,8,128]{4,3,2,1,0:T(8,128)}), f32[16,2,2,8,128]{4,3,2,1,0:T(8,128)S(1)}, u32[]{:S(2)}, u32[]{:S(2)}) %all-to-all-start) | async-done | bytes 262176 | tf_op jit(solution)/shard_map/while/body/all_to_all | solution.py:355
  72.5 1.0 crossing.1
  73.5 4.8 %collective-permute-start.5 = (f32[16,2,2,8,128]{4,3,2,1,0:T(8,128)S(1)}, f32[16,2,2,8,128]{4,3,2,1,0:T(8,128)S(1)}, u32[]{:S(2)}, u32[]{:S(2)}) collective-permute-start(f32[16,2,2,8,128]{4,3,2,1,0:T(8,128)S(1)} %crossing.1), channel_id=1, source_target_pairs={{0,16},{16,0},{1,17},{17,1},{2,18},{18,2},{3,19},{19,3},{4,20},{20... | collective-permute-start | bytes 786440 | tf_op jit(solution)/shard_map/ppermute | solution.py:358
  78.3 1.5 %collective-permute-done.4.partner01_ref = f32[16,2,2,8,128]{4,3,2,1,0:T(8,128)S(1)} collective-permute-done((f32[16,2,2,8,128]{4,3,2,1,0:T(8,128)S(1)}, f32[16,2,2,8,128]{4,3,2,1,0:T(8,128)S(1)}, u32[]{:S(2)}, u32[]{:S(2)}) %collective-permute-start.4) | collective-permute-done | bytes 262176 | tf_op jit(solution)/shard_map/ppermute | solution.py:358
  79.8 27.2 %while.19 = (s32[]{:T(128)}, f32[16,2,2,8,128]{4,3,2,1,0:T(8,128)S(1)}, f32[16,2,2,8,128]{4,3,2,1,0:T(8,128)S(1)}, f32[24,128]{1,0:T(8,128)S(1)}, f32[16,128]{1,0:T(8,128)S(1)}) while((s32[]{:T(128)}, f32[16,2,2,8,128]{4,3,2,1,0:T(8,128)S(1)}, f32[16,2,2,8,128]{4,3,2,1,0:T(8,128)S(1)}, f32[24,128]{1,0:T(8,128)S(1)}, f32[16,128]{1,0:T(8,128)S(1)}) %tuple.31), condition=%region_3.0_spmd, body=%region_2.0_spmd | while | flops 1 | bytes 1310809 | solution.py:366
  79.8 0.8 pair_moments.1
  80.6 14.0 %all_to_all.17.in_ref = f32[16,2,2,8,128]{4,3,2,1,0:T(8,128)S(1)} all-to-all(f32[16,2,2,8,128]{4,3,2,1,0:T(8,128)S(1)} %pair_moments.1), channel_id=1, replica_groups=mesh['y'=4,'x'=4,'zh'=2,'core'=2,'zl'=8] {'y','x'}, dimensions={0} | all-to-all | bytes 524288 | tf_op jit(solution)/shard_map/while/body/all_to_all | solution.py:355
  94.5 1.4 %scan_pairs.3 = f32[16,2,2,8,128]{4,3,2,1,0:T(8,128)} custom-call(f32[16,2,2,8,128]{4,3,2,1,0:T(8,128)S(1)} %all_to_all.17.in_ref, f32[16,128]{1,0:T(8,128)S(1)} %get-tuple-element.122.cf_ref), custom_call_target="tpu_custom_call" | custom-call | tf_op jit(solution)/shard_map/while/body/scan_pairs/pallas_call | solution.py:344
  95.9 3.5 %all-to-all-start.2 = ((f32[16,2,2,8,128]{4,3,2,1,0:T(8,128)}), f32[16,2,2,8,128]{4,3,2,1,0:T(8,128)S(1)}, u32[]{:S(2)}, u32[]{:S(2)}) async-start(f32[16,2,2,8,128]{4,3,2,1,0:T(8,128)} %scan_pairs.3), calls=%async_computation.2 | async-start | bytes 524288 | tf_op jit(solution)/shard_map/while/body/all_to_all | solution.py:355
  99.5 7.5 %all-to-all-done.2 = f32[16,2,2,8,128]{4,3,2,1,0:T(8,128)S(1)} async-done(((f32[16,2,2,8,128]{4,3,2,1,0:T(8,128)}), f32[16,2,2,8,128]{4,3,2,1,0:T(8,128)S(1)}, u32[]{:S(2)}, u32[]{:S(2)}) %all-to-all-start.2) | async-done | bytes 262176 | tf_op jit(solution)/shard_map/while/body/all_to_all | solution.py:355
  107.0 0.9 finish_other.1
  107.9 13.8 %collective-permute-start.6 = (f32[4,2,16,1024]{3,2,1,0:T(8,128)S(1)}, f32[4,2,16,1024]{3,2,1,0:T(8,128)S(1)}, u32[]{:S(2)}, u32[]{:S(2)}) collective-permute-start(f32[4,2,16,1024]{3,2,1,0:T(8,128)S(1)} %finish_other.1), channel_id=1, source_target_pairs={{0,8},{8,0},{1,9},{9,1},{2,10},{10,2},{3,11},{11,3},{4,12},{12,4},... | collective-permute-start | bytes 1572872 | tf_op jit(solution)/shard_map/ppermute | solution.py:309
  121.7 1.8 %finish_own.1 = f32[4,2,32,1024]{3,2,1,0:T(8,128)} custom-call(f32[4,4,16,1024]{3,2,1,0:T(8,128)S(1)} %get-tuple-element.68.part_ref, f32[16,2,2,8,128]{4,3,2,1,0:T(8,128)S(1)} %get-tuple-element.74.carry01_ref, f32[16,2,2,8,128]{4,3,2,1,0:T(8,128)S(1)} %get-tuple-element.138, f32[16,2,2,8,128]{4,3,2,1,0:T(8,128)S(1)} %get-tuple-element.72.carry_ref.carry23_ref, ...), custom_call_target="tpu_custom_call" | custom-call | tf_op jit(solution)/shard_map/finish_own/pallas_call | solution.py:344
  123.5 0.8 constant_dynamic-update-slice_fusion
  (11 shorter events, 0.1 us)
Async XLA Ops:
  0.0 17.1 %collective-permute-start = (f32[4,2,32,1024]{3,2,1,0:T(8,128)}, f32[4,2,32,1024]{3,2,1,0:T(8,128)S(1)}, u32[]{:S(2)}, u32[]{:S(2)}) collective-permute-start(f32[4,2,32,1024]{3,2,1,0:T(8,128)} %own_ref.5), channel_id=1, source_target_pairs={{0,8},{8,0},{1,9},{9,1},{2,10},{10,2},{3,11},{11,3},{4,12},{12,4},... | collective-permute-start | bytes 3145736 | tf_op jit(solution)/shard_map/ppermute | solution.py:309
  3.5 20.5 %collective-permute-start.2 = (f32[32,1024]{1,0:T(8,128)S(1)}, f32[32,1024]{1,0:T(8,128)S(1)}, u32[]{:S(2)}, u32[]{:S(2)}) collective-permute-start(f32[32,1024]{1,0:T(8,128)S(1)} %dynamic-slice_bitcast_fusion), channel_id=1, source_target_pairs={{8,16},{16,8},{24,32},{32,24},{40,48},{48,40},{56,64},{64,56},{72,... | collective-permute-start | bytes 393224 | tf_op jit(solution)/shard_map/ppermute | solution.py:306
  17.1 1.2 copy-start
  18.3 8.4 %copy-start.1 = (f32[4,2,32,1024]{3,2,1,0:T(8,128)S(1)}, f32[4,2,32,1024]{3,2,1,0:T(8,128)}, u32[]{:S(2)}) copy-start(f32[4,2,32,1024]{3,2,1,0:T(8,128)} %own_ref.5) | copy-start | bytes 3145732
  18.3 2.1 %copy-start.2 = (f32[4]{0:T(128)S(1)}, f32[4]{0:T(128)}, u32[]{:S(2)}) copy-start(f32[4]{0:T(128)} %dif_ref.1) | copy-start | bytes 52
  18.3 2.1 %copy-start.3 = (f32[128]{0:T(128)S(1)}, f32[128]{0:T(128)}, u32[]{:S(2)}) copy-start(f32[128]{0:T(128)} %param.8) | copy-start | bytes 1540
  18.4 6.4 %collective-permute-start.1 = (f32[16,1024]{1,0:T(8,128)S(1)}, f32[16,1024]{1,0:T(8,128)S(1)}, u32[]{:S(2)}, u32[]{:S(2)}) collective-permute-start(f32[16,1024]{1,0:T(8,128)S(1)} %row_ends.1), channel_id=1, source_target_pairs={{0,15},{1,8},{2,9},{3,10},{4,11},{5,12},{6,13},{7,14},{8,1},{9,2},... | collective-permute-start | bytes 196616 | tf_op jit(solution)/shard_map/ppermute | solution.py:306
  24.7 4.6 %collective-permute-start.3 = (f32[32,1024]{1,0:T(8,128)S(1)}, f32[32,1024]{1,0:T(8,128)S(1)}, u32[]{:S(2)}, u32[]{:S(2)}) collective-permute-start(f32[32,1024]{1,0:T(8,128)S(1)} %collective-permute-done.2.far_ref), channel_id=1, source_target_pairs={{0,8},{8,0},{1,9},{9,1},{2,10},{10,2},{3,11},{11,3},{4,12},{12,4},... | collective-permute-start | bytes 393224 | tf_op jit(solution)/shard_map/ppermute | solution.py:309
  31.3 25.2 %all-to-all-start.3 = ((f32[16,2,2,8,128]{4,3,2,1,0:T(8,128)}), f32[16,2,2,8,128]{4,3,2,1,0:T(8,128)S(1)}, u32[]{:S(2)}, u32[]{:S(2)}) async-start(f32[16,2,2,8,128]{4,3,2,1,0:T(8,128)} %get-tuple-element.70.own_ref), calls=%async_computation.3 | async-start | bytes 524288 | tf_op jit(solution)/shard_map/all_to_all | solution.py:355
  44.7 35.1 %collective-permute-start.4 = (f32[16,2,2,8,128]{4,3,2,1,0:T(8,128)S(1)}, f32[16,2,2,8,128]{4,3,2,1,0:T(8,128)S(1)}, u32[]{:S(2)}, u32[]{:S(2)}) collective-permute-start(f32[16,2,2,8,128]{4,3,2,1,0:T(8,128)S(1)} %get-tuple-element.109), channel_id=1, source_target_pairs={{0,16},{16,0},{1,17},{17,1},{2,18},{18,2},{3,19},{19,3},{4,20},{20... | collective-permute-start | bytes 786440 | tf_op jit(solution)/shard_map/ppermute | solution.py:358
  58.0 14.5 %all-to-all-start = ((f32[16,2,2,8,128]{4,3,2,1,0:T(8,128)}), f32[16,2,2,8,128]{4,3,2,1,0:T(8,128)S(1)}, u32[]{:S(2)}, u32[]{:S(2)}) async-start(f32[16,2,2,8,128]{4,3,2,1,0:T(8,128)} %scan_pairs.2), calls=%async_computation | async-start | bytes 524288 | tf_op jit(solution)/shard_map/while/body/all_to_all | solution.py:355
  73.5 33.5 %collective-permute-start.5 = (f32[16,2,2,8,128]{4,3,2,1,0:T(8,128)S(1)}, f32[16,2,2,8,128]{4,3,2,1,0:T(8,128)S(1)}, u32[]{:S(2)}, u32[]{:S(2)}) collective-permute-start(f32[16,2,2,8,128]{4,3,2,1,0:T(8,128)S(1)} %crossing.1), channel_id=1, source_target_pairs={{0,16},{16,0},{1,17},{17,1},{2,18},{18,2},{3,19},{19,3},{4,20},{20... | collective-permute-start | bytes 786440 | tf_op jit(solution)/shard_map/ppermute | solution.py:358
  95.9 11.0 %all-to-all-start.2 = ((f32[16,2,2,8,128]{4,3,2,1,0:T(8,128)}), f32[16,2,2,8,128]{4,3,2,1,0:T(8,128)S(1)}, u32[]{:S(2)}, u32[]{:S(2)}) async-start(f32[16,2,2,8,128]{4,3,2,1,0:T(8,128)} %scan_pairs.3), calls=%async_computation.2 | async-start | bytes 524288 | tf_op jit(solution)/shard_map/while/body/all_to_all | solution.py:355
  107.9 15.6 %collective-permute-start.6 = (f32[4,2,16,1024]{3,2,1,0:T(8,128)S(1)}, f32[4,2,16,1024]{3,2,1,0:T(8,128)S(1)}, u32[]{:S(2)}, u32[]{:S(2)}) collective-permute-start(f32[4,2,16,1024]{3,2,1,0:T(8,128)S(1)} %finish_other.1), channel_id=1, source_target_pairs={{0,8},{8,0},{1,9},{9,1},{2,10},{10,2},{3,11},{11,3},{4,12},{12,4},... | collective-permute-start | bytes 1572872 | tf_op jit(solution)/shard_map/ppermute | solution.py:309

commit v6 on v5

--- a/solution.py
+++ b/solution.py
@@ -92,12 +92,21 @@
     return 8 * down + 4 * half + block // 2
 
 
-def ends_kernel(own_ref, other_ref, out_ref):
-    first = lax.axis_index("core") == 0
-    for line in range(8):
-        c, k = line // 2, line % 2
-        for at, ref in ((line, own_ref), (8 + line, other_ref)):
-            out_ref[at : at + 1, :] = jnp.where(first, ref[c, k, 0:1, :], ref[c, k, 31:32, :])
+def ends_kernel(own_ref, other_ref, out_ref, held, arrived):
+    core = lax.axis_index("core")
+    first = core == 0
+    rows = pl.ds(pl.multiple_of(24 * core, 8), 8)
+    fetch = pltpu.make_async_copy(own_ref.at[:, :, rows, :], held, arrived)
+    fetch.start()
+    for c in range(4):
+        for k in range(2):
+            row = jnp.where(first, other_ref[c, k, 0:1, :], other_ref[c, k, 31:32, :])
+            out_ref[8 + 2 * c + k : 9 + 2 * c + k, :] = row
+    fetch.wait()
+    for c in range(4):
+        for k in range(2):
+            row = jnp.where(first, held[c, k, 0:1, :], held[c, k, 7:8, :])
+            out_ref[2 * c + k : 2 * c + k + 1, :] = row
 
 
 def local_kernel(own_ref, other_ref, halo_ref, cf_ref, dif_ref, part_ref, *send_refs):
@@ -323,8 +332,9 @@
     ends = pl.pallas_call(
         ends_kernel,
         out_shape=jax.ShapeDtypeStruct((16, 1024), f32),
-        in_specs=[whole()] * 2,
+        in_specs=[whole(pltpu.HBM), whole()],
         out_specs=whole(),
+        scratch_shapes=[pltpu.VMEM((4, 2, 8, 1024), f32), pltpu.SemaphoreType.DMA],
         compiler_params=params(),
         name="row_ends",
     )(flow_state, other)
@@ -362,10 +372,12 @@
         return in_plane(call(kernel, "scan_pairs", pieces, value, scan_cf))
 
     def in_loop(step, value):
+        def body(state):
+            left, held = lax.optimization_barrier((state[0] - 1, state[1]))
+            return left, step(held)
+
         once = lax.optimization_barrier(jnp.int32(1))
-        return lax.while_loop(
-            lambda state: state[0] > 0, lambda state: (jnp.int32(0), step(state[1])), (once, value)
-        )[1]
+        return lax.while_loop(lambda state: state[0] > 0, body, (once, value))[1]
 
     def array(*shape):
         return jax.ShapeDtypeStruct(shape, f32)
@@ -388,7 +400,7 @@
     )
 
     partner01 = to_partner(sum01)
-    carry23 = in_loop(lambda value: sent_back(value, 2), in_plane(sum23))
+    carry23 = in_loop(lambda value: sent_back(in_plane(value), 2), sum23)
     leaving23 = call(crossing_kernel, "crossing", pieces, sum23, carry23, own_cf)
     partner23 = to_partner(leaving23)
 

time: 125 us -> 116 us (0.928)
  the two profiles are of different devices: /device:TPU:65 before, /device:TPU:1 now
where the time goes in v6:
time: 116 us; the launch traced here: 115 us
  blocking collectives  52 us (45%)
  starting transfers between devices  45.1 us (39%)
  Pallas kernels  10.5 us (9%)
  waiting for transfers between devices  4.32 us (4%)
  local copies, waits for them, and re-layouts  3.01 us (3%)
    all_to_all x4, blocking collectives, in_plane(): lax.all_to_all(value, ('y', 'x'), split_axis=0, concat_axis=0, tiled=True)  52 us
    ppermute x3, starting transfers between devices, across_cores(): return lax.ppermute(value, 'core', [(0, 1), (1, 0)])  23.7 us
    ppermute x2, starting transfers between devices, route(): return lax.ppermute(value, axes, pairs)  12 us
    ppermute x2, starting transfers between devices, to_partner(): return lax.ppermute(value, 'zh', [(0, 1), (1, 0)])  9.36 us
    pallas_call x8, Pallas kernels, call(): pl.pallas_call(kernel, out_shape=outs, in_specs=[whole(pltpu.SMEM if id(a...  8.96 us
    ppermute x2, waiting for transfers between devices, route(): return lax.ppermute(value, axes, pairs)  3.46 us
  transfers between devices with their start and end apart: 7, of which 3 were waited for; matrix products, arithmetic and copies ran while one was open for 1% of the time, Pallas kernels for 7%

profile of v6, /device:TPU:1, one launch (start us, length us, event | category | flops | bytes accessed | tf_op | source)
XLA Modules:
  0.0 115.1 jit_solution(1700767282311944777)
XLA Ops:
  0.0 8.8 %collective-permute-start = (f32[4,2,32,1024]{3,2,1,0:T(8,128)}, f32[4,2,32,1024]{3,2,1,0:T(8,128)S(1)}, u32[]{:S(2)}, u32[]{:S(2)}) collective-permute-start(f32[4,2,32,1024]{3,2,1,0:T(8,128)} %own_ref.5), channel_id=1, source_target_pairs={{0,8},{8,0},{1,9},{9,1},{2,10},{10,2},{3,11},{11,3},{4,12},{12,4},... | collective-permute-start | bytes 3145736 | tf_op jit(solution)/shard_map/ppermute | solution.py:318
  8.8 0.9 dynamic-slice_bitcast_fusion
  9.7 10.0 %collective-permute-start.2 = (f32[32,1024]{1,0:T(8,128)S(1)}, f32[32,1024]{1,0:T(8,128)S(1)}, u32[]{:S(2)}, u32[]{:S(2)}) collective-permute-start(f32[32,1024]{1,0:T(8,128)S(1)} %dynamic-slice_bitcast_fusion), channel_id=1, source_target_pairs={{8,16},{16,8},{24,32},{32,24},{40,48},{48,40},{56,64},{64,56},{72,... | collective-permute-start | bytes 393224 | tf_op jit(solution)/shard_map/ppermute | solution.py:315
  19.7 0.0 copy-start
  19.7 1.2 %copy-done = f32[4,2,32,1024]{3,2,1,0:T(8,128)S(1)} copy-done((f32[4,2,32,1024]{3,2,1,0:T(8,128)S(1)}, f32[4,2,32,1024]{3,2,1,0:T(8,128)}, u32[]{:S(2)}) %copy-start) | copy-done | bytes 1048600
  20.9 0.1 row_ends.1
  21.0 0.0 copy-start.2
  21.0 0.0 copy-start.3
  21.0 2.1 %collective-permute-start.1 = (f32[16,1024]{1,0:T(8,128)S(1)}, f32[16,1024]{1,0:T(8,128)S(1)}, u32[]{:S(2)}, u32[]{:S(2)}) collective-permute-start(f32[16,1024]{1,0:T(8,128)S(1)} %row_ends.1), channel_id=1, source_target_pairs={{0,15},{1,8},{2,9},{3,10},{4,11},{5,12},{6,13},{7,14},{8,1},{9,2},... | collective-permute-start | bytes 196616 | tf_op jit(solution)/shard_map/ppermute | solution.py:315
  23.1 1.5 %coefficients.1 = (f32[24,128]{1,0:T(8,128)S(1)}, f32[16,128]{1,0:T(8,128)S(1)}) custom-call(f32[1,128]{1,0:T(1,128)S(1)} %bitcast.3, f32[4]{0:T(128)S(1)} %copy-done.2), custom_call_target="tpu_custom_call" | custom-call | tf_op jit(solution)/shard_map/coefficients/pallas_call | solution.py:343
  24.6 0.5 collective-permute-done.2.far_ref
  25.1 3.0 %collective-permute-done.1.halo_ref = f32[16,1024]{1,0:T(8,128)S(1)} collective-permute-done((f32[16,1024]{1,0:T(8,128)S(1)}, f32[16,1024]{1,0:T(8,128)S(1)}, u32[]{:S(2)}, u32[]{:S(2)}) %collective-permute-start.1) | collective-permute-done | bytes 65568 | tf_op jit(solution)/shard_map/ppermute | solution.py:315
  28.0 7.0 %collective-permute-start.3 = (f32[32,1024]{1,0:T(8,128)S(1)}, f32[32,1024]{1,0:T(8,128)S(1)}, u32[]{:S(2)}, u32[]{:S(2)}) collective-permute-start(f32[32,1024]{1,0:T(8,128)S(1)} %collective-permute-done.2.far_ref), channel_id=1, source_target_pairs={{0,8},{8,0},{1,9},{9,1},{2,10},{10,2},{3,11},{11,3},{4,12},{12,4},... | collective-permute-start | bytes 393224 | tf_op jit(solution)/shard_map/ppermute | solution.py:318
  35.0 2.0 %local_step.1 = (f32[4,4,16,1024]{3,2,1,0:T(8,128)S(1)}, f32[16,2,2,8,128]{4,3,2,1,0:T(8,128)S(1)}, f32[16,2,2,8,128]{4,3,2,1,0:T(8,128)S(1)}) custom-call(f32[4,2,32,1024]{3,2,1,0:T(8,128)S(1)} %copy-done.1, f32[4,2,32,1024]{3,2,1,0:T(8,128)S(1)} %collective-permute-done.other_ref, f32[16,1024]{1,0:T(8,128)S(1)} %collective-permute-done.1.halo_ref, ...), custom_call_target="tpu_custom_call" | custom-call | tf_op jit(solution)/shard_map/local_step/pallas_call | solution.py:354
  37.1 1.3 %edge_products.1 = (f32[16,2,2,8,128]{4,3,2,1,0:T(8,128)S(1)}, f32[16,2,2,8,128]{4,3,2,1,0:T(8,128)S(1)}, f32[4,4,16,1024]{3,2,1,0:T(8,128)S(1)}) custom-call(f32[4,2,32,1024]{3,2,1,0:T(8,128)S(1)} %copy-done.1, f32[4,2,32,1024]{3,2,1,0:T(8,128)S(1)} %collective-permute-done.other_ref, ...), custom_call_target="tpu_custom_call", output_to_operand_aliasing={{0}: (4, {}), {1}: (5, {}), {2}: (6, {})} | custom-call | tf_op jit(solution)/shard_map/edge_products/pallas_call | solution.py:354
  38.3 5.6 %collective-permute-start.4 = (f32[16,2,2,8,128]{4,3,2,1,0:T(8,128)S(1)}, f32[16,2,2,8,128]{4,3,2,1,0:T(8,128)S(1)}, u32[]{:S(2)}, u32[]{:S(2)}) collective-permute-start(f32[16,2,2,8,128]{4,3,2,1,0:T(8,128)S(1)} %get-tuple-element.230), channel_id=1, source_target_pairs={{0,16},{16,0},{1,17},{17,1},{2,18},{18,2},{3,19},{19,3},{4,20},{20... | collective-permute-start | bytes 786440 | tf_op jit(solution)/shard_map/ppermute | solution.py:368
  44.0 31.9 %while.24 = (s32[]{:T(128)}, f32[16,2,2,8,128]{4,3,2,1,0:T(8,128)S(1)}, f32[16,128]{1,0:T(8,128)S(1)}, s32[]{:T(128)}) while((s32[]{:T(128)}, f32[16,2,2,8,128]{4,3,2,1,0:T(8,128)S(1)}, f32[16,128]{1,0:T(8,128)S(1)}, s32[]{:T(128)}) %tuple.57), condition=%wide.region_1.0_spmd, body=%wide.region_0.0_spmd.sunk | while | flops 2 | bytes 1048629 | solution.py:380
  44.0 20.7 %all_to_all.30.in_ref = f32[16,2,2,8,128]{4,3,2,1,0:T(8,128)S(1)} all-to-all(f32[16,2,2,8,128]{4,3,2,1,0:T(8,128)S(1)} %get-tuple-element.209), channel_id=1, replica_groups=mesh['y'=4,'x'=4,'zh'=2,'core'=2,'zl'=8] {'y','x'}, dimensions={0} | all-to-all | bytes 524288 | tf_op jit(solution)/shard_map/while/body/all_to_all | solution.py:365
  64.7 0.7 scan_pairs.8
  65.4 10.5 %all_to_all.31 = f32[16,2,2,8,128]{4,3,2,1,0:T(8,128)S(1)} all-to-all(f32[16,2,2,8,128]{4,3,2,1,0:T(8,128)S(1)} %scan_pairs.8), channel_id=1, replica_groups=mesh['y'=4,'x'=4,'zh'=2,'core'=2,'zl'=8] {'y','x'}, dimensions={0} | all-to-all | bytes 524288 | tf_op jit(solution)/shard_map/while/body/all_to_all | solution.py:365
  75.9 0.8 crossing.1
  76.6 3.7 %collective-permute-start.5 = (f32[16,2,2,8,128]{4,3,2,1,0:T(8,128)S(1)}, f32[16,2,2,8,128]{4,3,2,1,0:T(8,128)S(1)}, u32[]{:S(2)}, u32[]{:S(2)}) collective-permute-start(f32[16,2,2,8,128]{4,3,2,1,0:T(8,128)S(1)} %crossing.1), channel_id=1, source_target_pairs={{0,16},{16,0},{1,17},{17,1},{2,18},{18,2},{3,19},{19,3},{4,20},{20... | collective-permute-start | bytes 786440 | tf_op jit(solution)/shard_map/ppermute | solution.py:368
  80.4 22.4 %while.25 = (s32[]{:T(128)}, f32[16,2,2,8,128]{4,3,2,1,0:T(8,128)S(1)}, f32[16,2,2,8,128]{4,3,2,1,0:T(8,128)S(1)}, f32[24,128]{1,0:T(8,128)S(1)}, f32[16,128]{1,0:T(8,128)S(1)}, /*index=5*/s32[]{:T(128)}) while((s32[]{:T(128)}, f32[16,2,2,8,128]{4,3,2,1,0:T(8,128)S(1)}, f32[16,2,2,8,128]{4,3,2,1,0:T(8,128)S(1)}, f32[24,128]{1,0:T(8,128)S(1)}, ...), condition=%wide.region_3.0_spmd, body=%wide.region_2.0_spmd.sunk | while | flops 2 | bytes 1048645 | solution.py:380
  80.4 0.8 pair_moments.4
  81.2 10.4 %all_to_all.32.in_ref = f32[16,2,2,8,128]{4,3,2,1,0:T(8,128)S(1)} all-to-all(f32[16,2,2,8,128]{4,3,2,1,0:T(8,128)S(1)} %pair_moments.4), channel_id=1, replica_groups=mesh['y'=4,'x'=4,'zh'=2,'core'=2,'zl'=8] {'y','x'}, dimensions={0} | all-to-all | bytes 524288 | tf_op jit(solution)/shard_map/while/body/all_to_all | solution.py:365
  91.6 0.7 scan_pairs.9
  92.4 10.4 %all_to_all.33 = f32[16,2,2,8,128]{4,3,2,1,0:T(8,128)S(1)} all-to-all(f32[16,2,2,8,128]{4,3,2,1,0:T(8,128)S(1)} %scan_pairs.9), channel_id=1, replica_groups=mesh['y'=4,'x'=4,'zh'=2,'core'=2,'zl'=8] {'y','x'}, dimensions={0} | all-to-all | bytes 524288 | tf_op jit(solution)/shard_map/while/body/all_to_all | solution.py:365
  102.8 0.9 collective-permute-done.5.partner23_ref
  103.7 0.9 finish_other.1
  104.5 7.9 %collective-permute-start.6 = (f32[4,2,16,1024]{3,2,1,0:T(8,128)S(1)}, f32[4,2,16,1024]{3,2,1,0:T(8,128)S(1)}, u32[]{:S(2)}, u32[]{:S(2)}) collective-permute-start(f32[4,2,16,1024]{3,2,1,0:T(8,128)S(1)} %finish_other.1), channel_id=1, source_target_pairs={{0,8},{8,0},{1,9},{9,1},{2,10},{10,2},{3,11},{11,3},{4,12},{12,4},... | collective-permute-start | bytes 1572872 | tf_op jit(solution)/shard_map/ppermute | solution.py:318
  112.4 1.8 %finish_own.1 = f32[4,2,32,1024]{3,2,1,0:T(8,128)} custom-call(f32[4,4,16,1024]{3,2,1,0:T(8,128)S(1)} %get-tuple-element.136.part_ref, f32[16,2,2,8,128]{4,3,2,1,0:T(8,128)S(1)} %get-tuple-element.142.carry01_ref, f32[16,2,2,8,128]{4,3,2,1,0:T(8,128)S(1)} %get-tuple-element.259, f32[16,2,2,8,128]{4,3,2,1,0:T(8,128)S(1)} %get-tuple-element.140.carry_ref.carry23_ref, ...), custom_call_target="tpu_custom_call" | custom-call | tf_op jit(solution)/shard_map/finish_own/pallas_call | solution.py:354
  114.3 0.8 constant_dynamic-update-slice_fusion
  (9 shorter events, 0.0 us)
Async XLA Ops:
  0.0 19.7 %collective-permute-start = (f32[4,2,32,1024]{3,2,1,0:T(8,128)}, f32[4,2,32,1024]{3,2,1,0:T(8,128)S(1)}, u32[]{:S(2)}, u32[]{:S(2)}) collective-permute-start(f32[4,2,32,1024]{3,2,1,0:T(8,128)} %own_ref.5), channel_id=1, source_target_pairs={{0,8},{8,0},{1,9},{9,1},{2,10},{10,2},{3,11},{11,3},{4,12},{12,4},... | collective-permute-start | bytes 3145736 | tf_op jit(solution)/shard_map/ppermute | solution.py:318
  9.7 15.4 %collective-permute-start.2 = (f32[32,1024]{1,0:T(8,128)S(1)}, f32[32,1024]{1,0:T(8,128)S(1)}, u32[]{:S(2)}, u32[]{:S(2)}) collective-permute-start(f32[32,1024]{1,0:T(8,128)S(1)} %dynamic-slice_bitcast_fusion), channel_id=1, source_target_pairs={{8,16},{16,8},{24,32},{32,24},{40,48},{48,40},{56,64},{64,56},{72,... | collective-permute-start | bytes 393224 | tf_op jit(solution)/shard_map/ppermute | solution.py:315
  19.7 1.2 %copy-start = (f32[4,2,32,1024]{3,2,1,0:T(8,128)S(1)}, f32[4,2,32,1024]{3,2,1,0:T(8,128)}, u32[]{:S(2)}) copy-start(f32[4,2,32,1024]{3,2,1,0:T(8,128)} %own_ref.5) | copy-start | bytes 3145732
  20.9 14.1 %copy-start.1 = (f32[4,2,32,1024]{3,2,1,0:T(8,128)S(1)}, f32[4,2,32,1024]{3,2,1,0:T(8,128)}, u32[]{:S(2)}) copy-start(f32[4,2,32,1024]{3,2,1,0:T(8,128)} %own_ref.5) | copy-start | bytes 3145732
  21.0 2.1 %copy-start.2 = (f32[4]{0:T(128)S(1)}, f32[4]{0:T(128)}, u32[]{:S(2)}) copy-start(f32[4]{0:T(128)} %dif_ref.1) | copy-start | bytes 52
  21.0 2.1 %copy-start.3 = (f32[128]{0:T(128)S(1)}, f32[128]{0:T(128)}, u32[]{:S(2)}) copy-start(f32[128]{0:T(128)} %param.8) | copy-start | bytes 1540
  21.0 7.0 %collective-permute-start.1 = (f32[16,1024]{1,0:T(8,128)S(1)}, f32[16,1024]{1,0:T(8,128)S(1)}, u32[]{:S(2)}, u32[]{:S(2)}) collective-permute-start(f32[16,1024]{1,0:T(8,128)S(1)} %row_ends.1), channel_id=1, source_target_pairs={{0,15},{1,8},{2,9},{3,10},{4,11},{5,12},{6,13},{7,14},{8,1},{9,2},... | collective-permute-start | bytes 196616 | tf_op jit(solution)/shard_map/ppermute | solution.py:315
  28.0 9.0 %collective-permute-start.3 = (f32[32,1024]{1,0:T(8,128)S(1)}, f32[32,1024]{1,0:T(8,128)S(1)}, u32[]{:S(2)}, u32[]{:S(2)}) collective-permute-start(f32[32,1024]{1,0:T(8,128)S(1)} %collective-permute-done.2.far_ref), channel_id=1, source_target_pairs={{0,8},{8,0},{1,9},{9,1},{2,10},{10,2},{3,11},{11,3},{4,12},{12,4},... | collective-permute-start | bytes 393224 | tf_op jit(solution)/shard_map/ppermute | solution.py:318
  38.3 42.1 %collective-permute-start.4 = (f32[16,2,2,8,128]{4,3,2,1,0:T(8,128)S(1)}, f32[16,2,2,8,128]{4,3,2,1,0:T(8,128)S(1)}, u32[]{:S(2)}, u32[]{:S(2)}) collective-permute-start(f32[16,2,2,8,128]{4,3,2,1,0:T(8,128)S(1)} %get-tuple-element.230), channel_id=1, source_target_pairs={{0,16},{16,0},{1,17},{17,1},{2,18},{18,2},{3,19},{19,3},{4,20},{20... | collective-permute-start | bytes 786440 | tf_op jit(solution)/shard_map/ppermute | solution.py:368
  76.6 27.0 %collective-permute-start.5 = (f32[16,2,2,8,128]{4,3,2,1,0:T(8,128)S(1)}, f32[16,2,2,8,128]{4,3,2,1,0:T(8,128)S(1)}, u32[]{:S(2)}, u32[]{:S(2)}) collective-permute-start(f32[16,2,2,8,128]{4,3,2,1,0:T(8,128)S(1)} %crossing.1), channel_id=1, source_target_pairs={{0,16},{16,0},{1,17},{17,1},{2,18},{18,2},{3,19},{19,3},{4,20},{20... | collective-permute-start | bytes 786440 | tf_op jit(solution)/shard_map/ppermute | solution.py:368
  104.5 9.8 %collective-permute-start.6 = (f32[4,2,16,1024]{3,2,1,0:T(8,128)S(1)}, f32[4,2,16,1024]{3,2,1,0:T(8,128)S(1)}, u32[]{:S(2)}, u32[]{:S(2)}) collective-permute-start(f32[4,2,16,1024]{3,2,1,0:T(8,128)S(1)} %finish_other.1), channel_id=1, source_target_pairs={{0,8},{8,0},{1,9},{9,1},{2,10},{10,2},{3,11},{11,3},{4,12},{12,4},... | collective-permute-start | bytes 1572872 | tf_op jit(solution)/shard_map/ppermute | solution.py:318

commit v7 on v6

--- a/solution.py
+++ b/solution.py
@@ -79,12 +79,16 @@
     own_ref[16:24, :] = pltpu.roll(four, turn, 1)
 
 
+def entry(ref, row, lane):
+    return ref[row : row + 1, lane : lane + 1]
+
+
 def pair_factors(cf_ref, c):
     lower = lax.axis_index("zh") == 0
-    r0 = jnp.where(lower, cf_ref[16 + c, 2], cf_ref[16 + c, 126])
-    r1 = jnp.where(lower, cf_ref[16 + c, 6], cf_ref[16 + c, 2])
-    s0 = jnp.where(lower, cf_ref[20 + c, 0], cf_ref[20 + c, 124])
-    s1 = jnp.where(lower, cf_ref[20 + c, 4], cf_ref[20 + c, 0])
+    r0 = jnp.where(lower, entry(cf_ref, 16 + c, 2), entry(cf_ref, 16 + c, 126))
+    r1 = jnp.where(lower, entry(cf_ref, 16 + c, 6), entry(cf_ref, 16 + c, 2))
+    s0 = jnp.where(lower, entry(cf_ref, 20 + c, 0), entry(cf_ref, 20 + c, 124))
+    s1 = jnp.where(lower, entry(cf_ref, 20 + c, 4), entry(cf_ref, 20 + c, 0))
     return lower, r0, r1, s0, s1
 
 
@@ -182,8 +186,8 @@
 
 
 def weights(cf_ref, c):
-    r = [cf_ref[c, j] for j in range(6)]
-    s = [cf_ref[4 + c, j] for j in range(6)]
+    r = [entry(cf_ref, c, j) for j in range(6)]
+    s = [entry(cf_ref, 4 + c, j) for j in range(6)]
     rise = [1.0, r[2], r[2] * r[3], r[2] * r[3] * r[4]]
     return rise, [s[1] * s[2] * s[3], s[2] * s[3], s[3], 1.0]
 
@@ -197,15 +201,15 @@
     for half in range(2):
         rows = pl.ds(pl.multiple_of(core * 16 + 8 * half, 8), 8)
         far, near = far_ref[rows, :], near_ref[rows, :]
-        w_low = jnp.where(first, far, near) * -cf_ref[12, 0]
-        w_high = jnp.where(first, near, far) * cf_ref[12, 5]
+        w_low = jnp.where(first, far, near) * -entry(cf_ref, 12, 0)
+        w_high = jnp.where(first, near, far) * entry(cf_ref, 12, 5)
         for c in range(4):
             raw_ref, sum_ref = ((raw01_ref, sum01_ref), (raw23_ref, sum23_ref))[c // 2]
-            r = [cf_ref[c, j] for j in range(6)]
-            s = [cf_ref[4 + c, j] for j in range(6)]
+            r = [entry(cf_ref, c, j) for j in range(6)]
+            s = [entry(cf_ref, 4 + c, j) for j in range(6)]
             lowest = jnp.where(first, own_ref[c, 0, rows, :], other_ref[c, 0, rows, :])
             highest = jnp.where(first, other_ref[c, 1, rows, :], own_ref[c, 1, rows, :])
-            low, high = cf_ref[8 + c, 0] * (w_low * lowest), cf_ref[8 + c, 5] * (w_high * highest)
+            low, high = entry(cf_ref, 8 + c, 0) * (w_low * lowest), entry(cf_ref, 8 + c, 5) * (w_high * highest)
             from_low, from_high = r[1] * low, s[4] * high
             p = (r[2] * r[3] * r[4] * r[5]) * from_low + high
             q = (s[0] * s[1] * s[2] * s[3]) * from_high + low
@@ -238,7 +242,7 @@
 
     def scaled(pair, c, at, by):
         value = in_ref[pair, c]
-        return value if base == 0 else jnp.where(by, cf_ref[8 + at, (8 * pair + 5 if at < 4 else 8 * pair + 127) % 128], 1.0) * value
+        return value if base == 0 else jnp.where(by, entry(cf_ref, 8 + at, (8 * pair + 5 if at < 4 else 8 * pair + 127) % 128), 1.0) * value
 
     @pl.when(upward)
     def _():
@@ -246,7 +250,7 @@
             carry = jnp.zeros((2, 8, 128), jnp.float32)
             for pair in range(16):
                 out_ref[pair, c] = carry
-                carry = cf_ref[base + c, 8 * pair + 1] * carry + scaled(pair, c, base + c, lower)
+                carry = entry(cf_ref, base + c, 8 * pair + 1) * carry + scaled(pair, c, base + c, lower)
 
     @pl.when(jnp.logical_not(upward))
     def _():
@@ -255,7 +259,7 @@
             for pair in range(15, -1, -1):
                 out_ref[pair, c] = carry
                 at = 4 + base + c
-                kept = cf_ref[at, (8 * pair + 127) % 128] * carry
+                kept = entry(cf_ref, at, (8 * pair + 127) % 128) * carry
                 carry = kept + scaled(pair, c, at, jnp.logical_not(lower))
 
 
@@ -350,7 +354,7 @@
     )(spacing.reshape(1, 128), diffusivity)
 
     def call(kernel, name, outs, *args, **more):
-        smem = {id(own_cf), id(scan_cf), id(diffusivity)}
+        smem = {id(own_cf), id(diffusivity)} if kernel is local_kernel else set()
         return pl.pallas_call(
             kernel,
             out_shape=outs,

time: 116 us -> 113 us (0.974)
  Pallas kernels: 10.5 us -> 6.42 us
  waiting for transfers between devices: 4.32 us -> 5.71 us
    pallas_call x8, Pallas kernels: 8.96 us -> 4.88 us  [call(): pl.pallas_call(kernel, out_shape=outs, in_specs=[whole(pltpu.SMEM if id(a...]
    ppermute x2, waiting for transfers between devices: 0.85 us -> 2.05 us  [to_partner(): return lax.ppermute(value, 'zh', [(0, 1), (1, 0)])]
  transfers between devices with their start and end apart: 7 -> 7, of which waited for: 3 -> 4; matrix products, arithmetic and copies ran while one was open for 1% -> 1% of each run, Pallas kernels for 7% -> 5%
where the time goes in v7:
time: 113 us; the launch traced here: 112 us
  blocking collectives  52 us (46%)
  starting transfers between devices  45.1 us (40%)
  Pallas kernels  6.42 us (6%)
  waiting for transfers between devices  5.71 us (5%)
  local copies, waits for them, and re-layouts  3.01 us (3%)
    all_to_all x4, blocking collectives, in_plane(): lax.all_to_all(value, ('y', 'x'), split_axis=0, concat_axis=0, tiled=True)  52 us
    ppermute x3, starting transfers between devices, across_cores(): return lax.ppermute(value, 'core', [(0, 1), (1, 0)])  23.7 us
    ppermute x2, starting transfers between devices, route(): return lax.ppermute(value, axes, pairs)  12 us
    ppermute x2, starting transfers between devices, to_partner(): return lax.ppermute(value, 'zh', [(0, 1), (1, 0)])  9.36 us
    pallas_call x8, Pallas kernels, call(): pl.pallas_call(kernel, out_shape=outs, in_specs=[whole(pltpu.SMEM if id(a...  4.88 us
    ppermute x2, waiting for transfers between devices, route(): return lax.ppermute(value, axes, pairs)  3.46 us
  transfers between devices with their start and end apart: 7, of which 4 were waited for; matrix products, arithmetic and copies ran while one was open for 1% of the time, Pallas kernels for 5%

profile of v7, /device:TPU:1, one launch (start us, length us, event | category | flops | bytes accessed | tf_op | source)
XLA Modules:
  0.0 112.4 jit_solution(239899208703645547)
XLA Ops:
  0.0 8.8 %collective-permute-start = (f32[4,2,32,1024]{3,2,1,0:T(8,128)}, f32[4,2,32,1024]{3,2,1,0:T(8,128)S(1)}, u32[]{:S(2)}, u32[]{:S(2)}) collective-permute-start(f32[4,2,32,1024]{3,2,1,0:T(8,128)} %own_ref.5), channel_id=1, source_target_pairs={{0,8},{8,0},{1,9},{9,1},{2,10},{10,2},{3,11},{11,3},{4,12},{12,4},... | collective-permute-start | bytes 3145736 | tf_op jit(solution)/shard_map/ppermute | solution.py:322
  8.8 0.9 dynamic-slice_bitcast_fusion
  9.7 10.0 %collective-permute-start.2 = (f32[32,1024]{1,0:T(8,128)S(1)}, f32[32,1024]{1,0:T(8,128)S(1)}, u32[]{:S(2)}, u32[]{:S(2)}) collective-permute-start(f32[32,1024]{1,0:T(8,128)S(1)} %dynamic-slice_bitcast_fusion), channel_id=1, source_target_pairs={{8,16},{16,8},{24,32},{32,24},{40,48},{48,40},{56,64},{64,56},{72,... | collective-permute-start | bytes 393224 | tf_op jit(solution)/shard_map/ppermute | solution.py:319
  19.7 0.0 copy-start
  19.7 1.2 %copy-done = f32[4,2,32,1024]{3,2,1,0:T(8,128)S(1)} copy-done((f32[4,2,32,1024]{3,2,1,0:T(8,128)S(1)}, f32[4,2,32,1024]{3,2,1,0:T(8,128)}, u32[]{:S(2)}) %copy-start) | copy-done | bytes 1048600
  20.9 0.1 row_ends.1
  21.0 0.0 copy-start.2
  21.0 2.1 %collective-permute-start.1 = (f32[16,1024]{1,0:T(8,128)S(1)}, f32[16,1024]{1,0:T(8,128)S(1)}, u32[]{:S(2)}, u32[]{:S(2)}) collective-permute-start(f32[16,1024]{1,0:T(8,128)S(1)} %row_ends.1), channel_id=1, source_target_pairs={{0,15},{1,8},{2,9},{3,10},{4,11},{5,12},{6,13},{7,14},{8,1},{9,2},... | collective-permute-start | bytes 196616 | tf_op jit(solution)/shard_map/ppermute | solution.py:319
  23.1 1.5 %coefficients.1 = (f32[24,128]{1,0:T(8,128)S(1)}, f32[16,128]{1,0:T(8,128)S(1)}) custom-call(f32[1,128]{1,0:T(1,128)S(1)} %bitcast.3, f32[4]{0:T(128)S(1)} %copy-done.2), custom_call_target="tpu_custom_call" | custom-call | tf_op jit(solution)/shard_map/coefficients/pallas_call | solution.py:347
  24.6 0.5 collective-permute-done.2.far_ref
  25.1 3.0 %collective-permute-done.1.halo_ref = f32[16,1024]{1,0:T(8,128)S(1)} collective-permute-done((f32[16,1024]{1,0:T(8,128)S(1)}, f32[16,1024]{1,0:T(8,128)S(1)}, u32[]{:S(2)}, u32[]{:S(2)}) %collective-permute-start.1) | collective-permute-done | bytes 65568 | tf_op jit(solution)/shard_map/ppermute | solution.py:319
  28.0 7.0 %collective-permute-start.3 = (f32[32,1024]{1,0:T(8,128)S(1)}, f32[32,1024]{1,0:T(8,128)S(1)}, u32[]{:S(2)}, u32[]{:S(2)}) collective-permute-start(f32[32,1024]{1,0:T(8,128)S(1)} %collective-permute-done.2.far_ref), channel_id=1, source_target_pairs={{0,8},{8,0},{1,9},{9,1},{2,10},{10,2},{3,11},{11,3},{4,12},{12,4},... | collective-permute-start | bytes 393224 | tf_op jit(solution)/shard_map/ppermute | solution.py:322
  35.0 2.0 %local_step.1 = (f32[4,4,16,1024]{3,2,1,0:T(8,128)S(1)}, f32[16,2,2,8,128]{4,3,2,1,0:T(8,128)S(1)}, f32[16,2,2,8,128]{4,3,2,1,0:T(8,128)S(1)}) custom-call(f32[4,2,32,1024]{3,2,1,0:T(8,128)S(1)} %copy-done.1, f32[4,2,32,1024]{3,2,1,0:T(8,128)S(1)} %collective-permute-done.other_ref, f32[16,1024]{1,0:T(8,128)S(1)} %collective-permute-done.1.halo_ref, ...), custom_call_target="tpu_custom_call" | custom-call | tf_op jit(solution)/shard_map/local_step/pallas_call | solution.py:358
  37.1 0.5 edge_products.1
  37.6 5.6 %collective-permute-start.4 = (f32[16,2,2,8,128]{4,3,2,1,0:T(8,128)S(1)}, f32[16,2,2,8,128]{4,3,2,1,0:T(8,128)S(1)}, u32[]{:S(2)}, u32[]{:S(2)}) collective-permute-start(f32[16,2,2,8,128]{4,3,2,1,0:T(8,128)S(1)} %get-tuple-element.230), channel_id=1, source_target_pairs={{0,16},{16,0},{1,17},{17,1},{2,18},{18,2},{3,19},{19,3},{4,20},{20... | collective-permute-start | bytes 786440 | tf_op jit(solution)/shard_map/ppermute | solution.py:372
  43.2 31.3 %while.24 = (s32[]{:T(128)}, f32[16,2,2,8,128]{4,3,2,1,0:T(8,128)S(1)}, f32[16,128]{1,0:T(8,128)S(1)}, s32[]{:T(128)}) while((s32[]{:T(128)}, f32[16,2,2,8,128]{4,3,2,1,0:T(8,128)S(1)}, f32[16,128]{1,0:T(8,128)S(1)}, s32[]{:T(128)}) %tuple.57), condition=%wide.region_1.0_spmd, body=%wide.region_0.0_spmd.sunk | while | flops 2 | bytes 1048629 | solution.py:384
  43.3 20.7 %all_to_all.30.in_ref = f32[16,2,2,8,128]{4,3,2,1,0:T(8,128)S(1)} all-to-all(f32[16,2,2,8,128]{4,3,2,1,0:T(8,128)S(1)} %get-tuple-element.209), channel_id=1, replica_groups=mesh['y'=4,'x'=4,'zh'=2,'core'=2,'zl'=8] {'y','x'}, dimensions={0} | all-to-all | bytes 524288 | tf_op jit(solution)/shard_map/while/body/all_to_all | solution.py:369
  63.9 0.2 scan_pairs.8
  64.1 10.4 %all_to_all.31 = f32[16,2,2,8,128]{4,3,2,1,0:T(8,128)S(1)} all-to-all(f32[16,2,2,8,128]{4,3,2,1,0:T(8,128)S(1)} %scan_pairs.8), channel_id=1, replica_groups=mesh['y'=4,'x'=4,'zh'=2,'core'=2,'zl'=8] {'y','x'}, dimensions={0} | all-to-all | bytes 524288 | tf_op jit(solution)/shard_map/while/body/all_to_all | solution.py:369
  74.6 0.2 crossing.1
  74.8 3.7 %collective-permute-start.5 = (f32[16,2,2,8,128]{4,3,2,1,0:T(8,128)S(1)}, f32[16,2,2,8,128]{4,3,2,1,0:T(8,128)S(1)}, u32[]{:S(2)}, u32[]{:S(2)}) collective-permute-start(f32[16,2,2,8,128]{4,3,2,1,0:T(8,128)S(1)} %crossing.1), channel_id=1, source_target_pairs={{0,16},{16,0},{1,17},{17,1},{2,18},{18,2},{3,19},{19,3},{4,20},{20... | collective-permute-start | bytes 786440 | tf_op jit(solution)/shard_map/ppermute | solution.py:372
  78.5 21.2 %while.25 = (s32[]{:T(128)}, f32[16,2,2,8,128]{4,3,2,1,0:T(8,128)S(1)}, f32[16,2,2,8,128]{4,3,2,1,0:T(8,128)S(1)}, f32[24,128]{1,0:T(8,128)S(1)}, f32[16,128]{1,0:T(8,128)S(1)}, /*index=5*/s32[]{:T(128)}) while((s32[]{:T(128)}, f32[16,2,2,8,128]{4,3,2,1,0:T(8,128)S(1)}, f32[16,2,2,8,128]{4,3,2,1,0:T(8,128)S(1)}, f32[24,128]{1,0:T(8,128)S(1)}, ...), condition=%wide.region_3.0_spmd, body=%wide.region_2.0_spmd.sunk | while | flops 2 | bytes 1048645 | solution.py:384
  78.6 0.1 pair_moments.4
  78.7 10.4 %all_to_all.32.in_ref = f32[16,2,2,8,128]{4,3,2,1,0:T(8,128)S(1)} all-to-all(f32[16,2,2,8,128]{4,3,2,1,0:T(8,128)S(1)} %pair_moments.4), channel_id=1, replica_groups=mesh['y'=4,'x'=4,'zh'=2,'core'=2,'zl'=8] {'y','x'}, dimensions={0} | all-to-all | bytes 524288 | tf_op jit(solution)/shard_map/while/body/all_to_all | solution.py:369
  89.2 0.2 scan_pairs.9
  89.3 10.4 %all_to_all.33 = f32[16,2,2,8,128]{4,3,2,1,0:T(8,128)S(1)} all-to-all(f32[16,2,2,8,128]{4,3,2,1,0:T(8,128)S(1)} %scan_pairs.9), channel_id=1, replica_groups=mesh['y'=4,'x'=4,'zh'=2,'core'=2,'zl'=8] {'y','x'}, dimensions={0} | all-to-all | bytes 524288 | tf_op jit(solution)/shard_map/while/body/all_to_all | solution.py:369
  99.7 2.0 %collective-permute-done.5.partner23_ref = f32[16,2,2,8,128]{4,3,2,1,0:T(8,128)S(1)} collective-permute-done((f32[16,2,2,8,128]{4,3,2,1,0:T(8,128)S(1)}, f32[16,2,2,8,128]{4,3,2,1,0:T(8,128)S(1)}, u32[]{:S(2)}, u32[]{:S(2)}) %collective-permute-start.5) | collective-permute-done | bytes 262176 | tf_op jit(solution)/shard_map/ppermute | solution.py:372
  101.8 0.3 finish_other.1
  102.1 7.9 %collective-permute-start.6 = (f32[4,2,16,1024]{3,2,1,0:T(8,128)S(1)}, f32[4,2,16,1024]{3,2,1,0:T(8,128)S(1)}, u32[]{:S(2)}, u32[]{:S(2)}) collective-permute-start(f32[4,2,16,1024]{3,2,1,0:T(8,128)S(1)} %finish_other.1), channel_id=1, source_target_pairs={{0,8},{8,0},{1,9},{9,1},{2,10},{10,2},{3,11},{11,3},{4,12},{12,4},... | collective-permute-start | bytes 1572872 | tf_op jit(solution)/shard_map/ppermute | solution.py:322
  110.1 1.3 %finish_own.1 = f32[4,2,32,1024]{3,2,1,0:T(8,128)} custom-call(f32[4,4,16,1024]{3,2,1,0:T(8,128)S(1)} %get-tuple-element.136.part_ref, f32[16,2,2,8,128]{4,3,2,1,0:T(8,128)S(1)} %get-tuple-element.142.carry01_ref, f32[16,2,2,8,128]{4,3,2,1,0:T(8,128)S(1)} %get-tuple-element.259, f32[16,2,2,8,128]{4,3,2,1,0:T(8,128)S(1)} %get-tuple-element.140.carry_ref.carry23_ref, ...), custom_call_target="tpu_custom_call" | custom-call | tf_op jit(solution)/shard_map/finish_own/pallas_call | solution.py:358
  111.4 0.2 collective-permute-done.6
  111.6 0.8 constant_dynamic-update-slice_fusion
  (9 shorter events, 0.0 us)
Async XLA Ops:
  0.0 19.7 %collective-permute-start = (f32[4,2,32,1024]{3,2,1,0:T(8,128)}, f32[4,2,32,1024]{3,2,1,0:T(8,128)S(1)}, u32[]{:S(2)}, u32[]{:S(2)}) collective-permute-start(f32[4,2,32,1024]{3,2,1,0:T(8,128)} %own_ref.5), channel_id=1, source_target_pairs={{0,8},{8,0},{1,9},{9,1},{2,10},{10,2},{3,11},{11,3},{4,12},{12,4},... | collective-permute-start | bytes 3145736 | tf_op jit(solution)/shard_map/ppermute | solution.py:322
  9.7 15.4 %collective-permute-start.2 = (f32[32,1024]{1,0:T(8,128)S(1)}, f32[32,1024]{1,0:T(8,128)S(1)}, u32[]{:S(2)}, u32[]{:S(2)}) collective-permute-start(f32[32,1024]{1,0:T(8,128)S(1)} %dynamic-slice_bitcast_fusion), channel_id=1, source_target_pairs={{8,16},{16,8},{24,32},{32,24},{40,48},{48,40},{56,64},{64,56},{72,... | collective-permute-start | bytes 393224 | tf_op jit(solution)/shard_map/ppermute | solution.py:319
  19.7 1.2 %copy-start = (f32[4,2,32,1024]{3,2,1,0:T(8,128)S(1)}, f32[4,2,32,1024]{3,2,1,0:T(8,128)}, u32[]{:S(2)}) copy-start(f32[4,2,32,1024]{3,2,1,0:T(8,128)} %own_ref.5) | copy-start | bytes 3145732
  20.9 14.1 %copy-start.1 = (f32[4,2,32,1024]{3,2,1,0:T(8,128)S(1)}, f32[4,2,32,1024]{3,2,1,0:T(8,128)}, u32[]{:S(2)}) copy-start(f32[4,2,32,1024]{3,2,1,0:T(8,128)} %own_ref.5) | copy-start | bytes 3145732
  21.0 2.1 %copy-start.2 = (f32[4]{0:T(128)S(1)}, f32[4]{0:T(128)}, u32[]{:S(2)}) copy-start(f32[4]{0:T(128)} %dif_ref.1) | copy-start | bytes 52
  21.0 2.1 %copy-start.3 = (f32[128]{0:T(128)S(1)}, f32[128]{0:T(128)}, u32[]{:S(2)}) copy-start(f32[128]{0:T(128)} %param.8) | copy-start | bytes 1540
  21.0 7.0 %collective-permute-start.1 = (f32[16,1024]{1,0:T(8,128)S(1)}, f32[16,1024]{1,0:T(8,128)S(1)}, u32[]{:S(2)}, u32[]{:S(2)}) collective-permute-start(f32[16,1024]{1,0:T(8,128)S(1)} %row_ends.1), channel_id=1, source_target_pairs={{0,15},{1,8},{2,9},{3,10},{4,11},{5,12},{6,13},{7,14},{8,1},{9,2},... | collective-permute-start | bytes 196616 | tf_op jit(solution)/shard_map/ppermute | solution.py:319
  28.0 9.0 %collective-permute-start.3 = (f32[32,1024]{1,0:T(8,128)S(1)}, f32[32,1024]{1,0:T(8,128)S(1)}, u32[]{:S(2)}, u32[]{:S(2)}) collective-permute-start(f32[32,1024]{1,0:T(8,128)S(1)} %collective-permute-done.2.far_ref), channel_id=1, source_target_pairs={{0,8},{8,0},{1,9},{9,1},{2,10},{10,2},{3,11},{11,3},{4,12},{12,4},... | collective-permute-start | bytes 393224 | tf_op jit(solution)/shard_map/ppermute | solution.py:322
  37.6 40.9 %collective-permute-start.4 = (f32[16,2,2,8,128]{4,3,2,1,0:T(8,128)S(1)}, f32[16,2,2,8,128]{4,3,2,1,0:T(8,128)S(1)}, u32[]{:S(2)}, u32[]{:S(2)}) collective-permute-start(f32[16,2,2,8,128]{4,3,2,1,0:T(8,128)S(1)} %get-tuple-element.230), channel_id=1, source_target_pairs={{0,16},{16,0},{1,17},{17,1},{2,18},{18,2},{3,19},{19,3},{4,20},{20... | collective-permute-start | bytes 786440 | tf_op jit(solution)/shard_map/ppermute | solution.py:372
  74.8 27.0 %collective-permute-start.5 = (f32[16,2,2,8,128]{4,3,2,1,0:T(8,128)S(1)}, f32[16,2,2,8,128]{4,3,2,1,0:T(8,128)S(1)}, u32[]{:S(2)}, u32[]{:S(2)}) collective-permute-start(f32[16,2,2,8,128]{4,3,2,1,0:T(8,128)S(1)} %crossing.1), channel_id=1, source_target_pairs={{0,16},{16,0},{1,17},{17,1},{2,18},{18,2},{3,19},{19,3},{4,20},{20... | collective-permute-start | bytes 786440 | tf_op jit(solution)/shard_map/ppermute | solution.py:372
  102.1 9.4 %collective-permute-start.6 = (f32[4,2,16,1024]{3,2,1,0:T(8,128)S(1)}, f32[4,2,16,1024]{3,2,1,0:T(8,128)S(1)}, u32[]{:S(2)}, u32[]{:S(2)}) collective-permute-start(f32[4,2,16,1024]{3,2,1,0:T(8,128)S(1)} %finish_other.1), channel_id=1, source_target_pairs={{0,8},{8,0},{1,9},{9,1},{2,10},{10,2},{3,11},{11,3},{4,12},{12,4},... | collective-permute-start | bytes 1572872 | tf_op jit(solution)/shard_map/ppermute | solution.py:322

commit v8 on v7

--- a/solution.py
+++ b/solution.py
@@ -77,6 +77,7 @@
     own_ref[0:8, :] = pltpu.roll(rs, turn, 1)
     own_ref[8:16, :] = pltpu.roll(gc, turn, 1)
     own_ref[16:24, :] = pltpu.roll(four, turn, 1)
+    own_ref[24:32, :] = rate * (1.0 / cell_width**2)
 
 
 def entry(ref, row, lane):
@@ -113,7 +114,7 @@
             out_ref[2 * c + k : 2 * c + k + 1, :] = row
 
 
-def local_kernel(own_ref, other_ref, halo_ref, cf_ref, dif_ref, part_ref, *send_refs):
+def local_kernel(own_ref, other_ref, halo_ref, cf_ref, part_ref, *send_refs):
     core = lax.axis_index("core")
     first = core == 0
     sub = lax.broadcasted_iota(jnp.int32, (8, 1024), 0)
@@ -136,12 +137,12 @@
         u = [tile(0, level, rows) * rate for level in range(4)]
         v = [tile(1, level, rows) * rate for level in range(4)]
         w = [tile(2, level, rows) for level in range(4)]
-        wc = [w[level] * cf_ref[12, level + 1] for level in range(4)]
+        wc = [w[level] * entry(cf_ref, 12, level + 1) for level in range(4)]
         for c in range(4):
-            r = [cf_ref[c, j] for j in range(6)]
-            s = [cf_ref[4 + c, j] for j in range(6)]
-            g = [cf_ref[8 + c, j] for j in range(6)]
-            spread = dif_ref[c] * (time_step / cell_width**2)
+            r = [entry(cf_ref, c, j) for j in range(6)]
+            s = [entry(cf_ref, 4 + c, j) for j in range(6)]
+            g = [entry(cf_ref, 8 + c, j) for j in range(6)]
+            spread = entry(cf_ref, 24 + c, 0)
             q = w if c == 2 else [tile(c, level, rows) for level in range(4)]
             gs = []
             for level in range(4):
@@ -346,7 +347,7 @@
 
     own_cf, scan_cf = pl.pallas_call(
         coefficients_kernel,
-        out_shape=(jax.ShapeDtypeStruct((24, 128), f32), jax.ShapeDtypeStruct((16, 128), f32)),
+        out_shape=(jax.ShapeDtypeStruct((32, 128), f32), jax.ShapeDtypeStruct((16, 128), f32)),
         in_specs=[whole(), whole(pltpu.SMEM)],
         out_specs=(whole(), whole()),
         compiler_params=params(),
@@ -354,11 +355,10 @@
     )(spacing.reshape(1, 128), diffusivity)
 
     def call(kernel, name, outs, *args, **more):
-        smem = {id(own_cf), id(diffusivity)} if kernel is local_kernel else set()
         return pl.pallas_call(
             kernel,
             out_shape=outs,
-            in_specs=[whole(pltpu.SMEM if id(a) in smem else pltpu.VMEM) for a in args],
+            in_specs=[whole() for _ in args],
             out_specs=jax.tree.map(lambda _: whole(), outs),
             compiler_params=params(),
             name=name,
@@ -393,7 +393,7 @@
         local_kernel,
         "local_step",
         (array(4, 4, 16, 1024), pieces, pieces),
-        flow_state, other, halo, own_cf, diffusivity,
+        flow_state, other, halo, own_cf,
     )
     sum01, sum23, part = call(
         edges_kernel,

time: 113 us -> 113 us (level)
  transfers between devices with their start and end apart: 7 -> 7, of which waited for: 4 -> 4; matrix products, arithmetic and copies ran while one was open for 1% -> 1% of each run, Pallas kernels for 5% -> 4%
where the time goes in v8:
time: 113 us; the launch traced here: 112 us
  blocking collectives  52 us (46%)
  starting transfers between devices  45.1 us (40%)
  Pallas kernels  5.82 us (5%)
  waiting for transfers between devices  5.71 us (5%)
  local copies, waits for them, and re-layouts  3.02 us (3%)
    all_to_all x4, blocking collectives, in_plane(): lax.all_to_all(value, ('y', 'x'), split_axis=0, concat_axis=0, tiled=True)  52 us
    ppermute x3, starting transfers between devices, across_cores(): return lax.ppermute(value, 'core', [(0, 1), (1, 0)])  23.7 us
    ppermute x2, starting transfers between devices, route(): return lax.ppermute(value, axes, pairs)  12 us
    ppermute x2, starting transfers between devices, to_partner(): return lax.ppermute(value, 'zh', [(0, 1), (1, 0)])  9.36 us
    pallas_call x8, Pallas kernels, call(): pl.pallas_call(kernel, out_shape=outs, in_specs=[whole() for _ in args],...  4.28 us
    ppermute x2, waiting for transfers between devices, route(): return lax.ppermute(value, axes, pairs)  3.46 us
  transfers between devices with their start and end apart: 7, of which 4 were waited for; matrix products, arithmetic and copies ran while one was open for 1% of the time, Pallas kernels for 4%

profile of v8, /device:TPU:1, one launch (start us, length us, event | category | flops | bytes accessed | tf_op | source)
XLA Modules:
  0.0 111.8 jit_solution(14095923372407139080)
XLA Ops:
  0.0 8.8 %collective-permute-start = (f32[4,2,32,1024]{3,2,1,0:T(8,128)}, f32[4,2,32,1024]{3,2,1,0:T(8,128)S(1)}, u32[]{:S(2)}, u32[]{:S(2)}) collective-permute-start(f32[4,2,32,1024]{3,2,1,0:T(8,128)} %own_ref.5), channel_id=1, source_target_pairs={{0,8},{8,0},{1,9},{9,1},{2,10},{10,2},{3,11},{11,3},{4,12},{12,4},... | collective-permute-start | bytes 3145736 | tf_op jit(solution)/shard_map/ppermute | solution.py:323
  8.8 0.9 dynamic-slice_bitcast_fusion
  9.7 10.0 %collective-permute-start.2 = (f32[32,1024]{1,0:T(8,128)S(1)}, f32[32,1024]{1,0:T(8,128)S(1)}, u32[]{:S(2)}, u32[]{:S(2)}) collective-permute-start(f32[32,1024]{1,0:T(8,128)S(1)} %dynamic-slice_bitcast_fusion), channel_id=1, source_target_pairs={{8,16},{16,8},{24,32},{32,24},{40,48},{48,40},{56,64},{64,56},{72,... | collective-permute-start | bytes 393224 | tf_op jit(solution)/shard_map/ppermute | solution.py:320
  19.7 0.0 copy-start
  19.7 1.2 %copy-done = f32[4,2,32,1024]{3,2,1,0:T(8,128)S(1)} copy-done((f32[4,2,32,1024]{3,2,1,0:T(8,128)S(1)}, f32[4,2,32,1024]{3,2,1,0:T(8,128)}, u32[]{:S(2)}) %copy-start) | copy-done | bytes 1048600
  20.9 0.1 row_ends.1
  21.0 0.0 copy-start.3
  21.0 2.1 %collective-permute-start.1 = (f32[16,1024]{1,0:T(8,128)S(1)}, f32[16,1024]{1,0:T(8,128)S(1)}, u32[]{:S(2)}, u32[]{:S(2)}) collective-permute-start(f32[16,1024]{1,0:T(8,128)S(1)} %row_ends.1), channel_id=1, source_target_pairs={{0,15},{1,8},{2,9},{3,10},{4,11},{5,12},{6,13},{7,14},{8,1},{9,2},... | collective-permute-start | bytes 196616 | tf_op jit(solution)/shard_map/ppermute | solution.py:320
  23.1 1.5 %coefficients.1 = (f32[32,128]{1,0:T(8,128)S(1)}, f32[16,128]{1,0:T(8,128)S(1)}) custom-call(f32[1,128]{1,0:T(1,128)S(1)} %bitcast.3, f32[4]{0:T(128)S(1)} %copy-done.3), custom_call_target="tpu_custom_call" | custom-call | tf_op jit(solution)/shard_map/coefficients/pallas_call | solution.py:348
  24.6 0.5 collective-permute-done.2.far_ref
  25.1 3.0 %collective-permute-done.1.halo_ref = f32[16,1024]{1,0:T(8,128)S(1)} collective-permute-done((f32[16,1024]{1,0:T(8,128)S(1)}, f32[16,1024]{1,0:T(8,128)S(1)}, u32[]{:S(2)}, u32[]{:S(2)}) %collective-permute-start.1) | collective-permute-done | bytes 65568 | tf_op jit(solution)/shard_map/ppermute | solution.py:320
  28.0 7.0 %collective-permute-start.3 = (f32[32,1024]{1,0:T(8,128)S(1)}, f32[32,1024]{1,0:T(8,128)S(1)}, u32[]{:S(2)}, u32[]{:S(2)}) collective-permute-start(f32[32,1024]{1,0:T(8,128)S(1)} %collective-permute-done.2.far_ref), channel_id=1, source_target_pairs={{0,8},{8,0},{1,9},{9,1},{2,10},{10,2},{3,11},{11,3},{4,12},{12,4},... | collective-permute-start | bytes 393224 | tf_op jit(solution)/shard_map/ppermute | solution.py:323
  35.0 1.4 %local_step.1 = (f32[4,4,16,1024]{3,2,1,0:T(8,128)S(1)}, f32[16,2,2,8,128]{4,3,2,1,0:T(8,128)S(1)}, f32[16,2,2,8,128]{4,3,2,1,0:T(8,128)S(1)}) custom-call(f32[4,2,32,1024]{3,2,1,0:T(8,128)S(1)} %copy-done.1, f32[4,2,32,1024]{3,2,1,0:T(8,128)S(1)} %collective-permute-done.other_ref, f32[16,1024]{1,0:T(8,128)S(1)} %collective-permute-done.1.halo_ref, ...), custom_call_target="tpu_custom_call" | custom-call | tf_op jit(solution)/shard_map/local_step/pallas_call | solution.py:358
  36.5 0.5 edge_products.1
  37.0 5.6 %collective-permute-start.4 = (f32[16,2,2,8,128]{4,3,2,1,0:T(8,128)S(1)}, f32[16,2,2,8,128]{4,3,2,1,0:T(8,128)S(1)}, u32[]{:S(2)}, u32[]{:S(2)}) collective-permute-start(f32[16,2,2,8,128]{4,3,2,1,0:T(8,128)S(1)} %get-tuple-element.230), channel_id=1, source_target_pairs={{0,16},{16,0},{1,17},{17,1},{2,18},{18,2},{3,19},{19,3},{4,20},{20... | collective-permute-start | bytes 786440 | tf_op jit(solution)/shard_map/ppermute | solution.py:372
  42.7 31.3 %while.24 = (s32[]{:T(128)}, f32[16,2,2,8,128]{4,3,2,1,0:T(8,128)S(1)}, f32[16,128]{1,0:T(8,128)S(1)}, s32[]{:T(128)}) while((s32[]{:T(128)}, f32[16,2,2,8,128]{4,3,2,1,0:T(8,128)S(1)}, f32[16,128]{1,0:T(8,128)S(1)}, s32[]{:T(128)}) %tuple.57), condition=%wide.region_1.0_spmd, body=%wide.region_0.0_spmd.sunk | while | flops 2 | bytes 1048629 | solution.py:384
  42.7 20.7 %all_to_all.30.in_ref = f32[16,2,2,8,128]{4,3,2,1,0:T(8,128)S(1)} all-to-all(f32[16,2,2,8,128]{4,3,2,1,0:T(8,128)S(1)} %get-tuple-element.209), channel_id=1, replica_groups=mesh['y'=4,'x'=4,'zh'=2,'core'=2,'zl'=8] {'y','x'}, dimensions={0} | all-to-all | bytes 524288 | tf_op jit(solution)/shard_map/while/body/all_to_all | solution.py:369
  63.3 0.2 scan_pairs.8
  63.5 10.4 %all_to_all.31 = f32[16,2,2,8,128]{4,3,2,1,0:T(8,128)S(1)} all-to-all(f32[16,2,2,8,128]{4,3,2,1,0:T(8,128)S(1)} %scan_pairs.8), channel_id=1, replica_groups=mesh['y'=4,'x'=4,'zh'=2,'core'=2,'zl'=8] {'y','x'}, dimensions={0} | all-to-all | bytes 524288 | tf_op jit(solution)/shard_map/while/body/all_to_all | solution.py:369
  74.0 0.2 crossing.1
  74.2 3.7 %collective-permute-start.5 = (f32[16,2,2,8,128]{4,3,2,1,0:T(8,128)S(1)}, f32[16,2,2,8,128]{4,3,2,1,0:T(8,128)S(1)}, u32[]{:S(2)}, u32[]{:S(2)}) collective-permute-start(f32[16,2,2,8,128]{4,3,2,1,0:T(8,128)S(1)} %crossing.1), channel_id=1, source_target_pairs={{0,16},{16,0},{1,17},{17,1},{2,18},{18,2},{3,19},{19,3},{4,20},{20... | collective-permute-start | bytes 786440 | tf_op jit(solution)/shard_map/ppermute | solution.py:372
  78.0 21.2 %while.25 = (s32[]{:T(128)}, f32[16,2,2,8,128]{4,3,2,1,0:T(8,128)S(1)}, f32[16,2,2,8,128]{4,3,2,1,0:T(8,128)S(1)}, f32[32,128]{1,0:T(8,128)S(1)}, f32[16,128]{1,0:T(8,128)S(1)}, /*index=5*/s32[]{:T(128)}) while((s32[]{:T(128)}, f32[16,2,2,8,128]{4,3,2,1,0:T(8,128)S(1)}, f32[16,2,2,8,128]{4,3,2,1,0:T(8,128)S(1)}, f32[32,128]{1,0:T(8,128)S(1)}, ...), condition=%wide.region_3.0_spmd, body=%wide.region_2.0_spmd.sunk | while | flops 2 | bytes 1048645 | solution.py:384
  78.0 0.1 pair_moments.4
  78.1 10.4 %all_to_all.32.in_ref = f32[16,2,2,8,128]{4,3,2,1,0:T(8,128)S(1)} all-to-all(f32[16,2,2,8,128]{4,3,2,1,0:T(8,128)S(1)} %pair_moments.4), channel_id=1, replica_groups=mesh['y'=4,'x'=4,'zh'=2,'core'=2,'zl'=8] {'y','x'}, dimensions={0} | all-to-all | bytes 524288 | tf_op jit(solution)/shard_map/while/body/all_to_all | solution.py:369
  88.6 0.2 scan_pairs.9
  88.7 10.4 %all_to_all.33 = f32[16,2,2,8,128]{4,3,2,1,0:T(8,128)S(1)} all-to-all(f32[16,2,2,8,128]{4,3,2,1,0:T(8,128)S(1)} %scan_pairs.9), channel_id=1, replica_groups=mesh['y'=4,'x'=4,'zh'=2,'core'=2,'zl'=8] {'y','x'}, dimensions={0} | all-to-all | bytes 524288 | tf_op jit(solution)/shard_map/while/body/all_to_all | solution.py:369
  99.2 2.0 %collective-permute-done.5.partner23_ref = f32[16,2,2,8,128]{4,3,2,1,0:T(8,128)S(1)} collective-permute-done((f32[16,2,2,8,128]{4,3,2,1,0:T(8,128)S(1)}, f32[16,2,2,8,128]{4,3,2,1,0:T(8,128)S(1)}, u32[]{:S(2)}, u32[]{:S(2)}) %collective-permute-start.5) | collective-permute-done | bytes 262176 | tf_op jit(solution)/shard_map/ppermute | solution.py:372
  101.2 0.3 finish_other.1
  101.6 7.9 %collective-permute-start.6 = (f32[4,2,16,1024]{3,2,1,0:T(8,128)S(1)}, f32[4,2,16,1024]{3,2,1,0:T(8,128)S(1)}, u32[]{:S(2)}, u32[]{:S(2)}) collective-permute-start(f32[4,2,16,1024]{3,2,1,0:T(8,128)S(1)} %finish_other.1), channel_id=1, source_target_pairs={{0,8},{8,0},{1,9},{9,1},{2,10},{10,2},{3,11},{11,3},{4,12},{12,4},... | collective-permute-start | bytes 1572872 | tf_op jit(solution)/shard_map/ppermute | solution.py:323
  109.5 1.3 %finish_own.1 = f32[4,2,32,1024]{3,2,1,0:T(8,128)} custom-call(f32[4,4,16,1024]{3,2,1,0:T(8,128)S(1)} %get-tuple-element.136.part_ref, f32[16,2,2,8,128]{4,3,2,1,0:T(8,128)S(1)} %get-tuple-element.142.carry01_ref, f32[16,2,2,8,128]{4,3,2,1,0:T(8,128)S(1)} %get-tuple-element.259, f32[16,2,2,8,128]{4,3,2,1,0:T(8,128)S(1)} %get-tuple-element.140.carry_ref.carry23_ref, ...), custom_call_target="tpu_custom_call" | custom-call | tf_op jit(solution)/shard_map/finish_own/pallas_call | solution.py:358
  110.8 0.2 collective-permute-done.6
  111.0 0.8 constant_dynamic-update-slice_fusion
  (9 shorter events, 0.0 us)
Async XLA Ops:
  0.0 19.7 %collective-permute-start = (f32[4,2,32,1024]{3,2,1,0:T(8,128)}, f32[4,2,32,1024]{3,2,1,0:T(8,128)S(1)}, u32[]{:S(2)}, u32[]{:S(2)}) collective-permute-start(f32[4,2,32,1024]{3,2,1,0:T(8,128)} %own_ref.5), channel_id=1, source_target_pairs={{0,8},{8,0},{1,9},{9,1},{2,10},{10,2},{3,11},{11,3},{4,12},{12,4},... | collective-permute-start | bytes 3145736 | tf_op jit(solution)/shard_map/ppermute | solution.py:323
  9.7 15.4 %collective-permute-start.2 = (f32[32,1024]{1,0:T(8,128)S(1)}, f32[32,1024]{1,0:T(8,128)S(1)}, u32[]{:S(2)}, u32[]{:S(2)}) collective-permute-start(f32[32,1024]{1,0:T(8,128)S(1)} %dynamic-slice_bitcast_fusion), channel_id=1, source_target_pairs={{8,16},{16,8},{24,32},{32,24},{40,48},{48,40},{56,64},{64,56},{72,... | collective-permute-start | bytes 393224 | tf_op jit(solution)/shard_map/ppermute | solution.py:320
  19.7 1.2 %copy-start = (f32[4,2,32,1024]{3,2,1,0:T(8,128)S(1)}, f32[4,2,32,1024]{3,2,1,0:T(8,128)}, u32[]{:S(2)}) copy-start(f32[4,2,32,1024]{3,2,1,0:T(8,128)} %own_ref.5) | copy-start | bytes 3145732
  20.9 14.1 %copy-start.1 = (f32[4,2,32,1024]{3,2,1,0:T(8,128)S(1)}, f32[4,2,32,1024]{3,2,1,0:T(8,128)}, u32[]{:S(2)}) copy-start(f32[4,2,32,1024]{3,2,1,0:T(8,128)} %own_ref.5) | copy-start | bytes 3145732
  21.0 2.1 %copy-start.2 = (f32[128]{0:T(128)S(1)}, f32[128]{0:T(128)}, u32[]{:S(2)}) copy-start(f32[128]{0:T(128)} %param.8) | copy-start | bytes 1540
  21.0 2.1 %copy-start.3 = (f32[4]{0:T(128)S(1)}, f32[4]{0:T(128)}, u32[]{:S(2)}) copy-start(f32[4]{0:T(128)} %diffusivity_ref.1) | copy-start | bytes 52
  21.0 7.0 %collective-permute-start.1 = (f32[16,1024]{1,0:T(8,128)S(1)}, f32[16,1024]{1,0:T(8,128)S(1)}, u32[]{:S(2)}, u32[]{:S(2)}) collective-permute-start(f32[16,1024]{1,0:T(8,128)S(1)} %row_ends.1), channel_id=1, source_target_pairs={{0,15},{1,8},{2,9},{3,10},{4,11},{5,12},{6,13},{7,14},{8,1},{9,2},... | collective-permute-start | bytes 196616 | tf_op jit(solution)/shard_map/ppermute | solution.py:320
  28.0 8.4 %collective-permute-start.3 = (f32[32,1024]{1,0:T(8,128)S(1)}, f32[32,1024]{1,0:T(8,128)S(1)}, u32[]{:S(2)}, u32[]{:S(2)}) collective-permute-start(f32[32,1024]{1,0:T(8,128)S(1)} %collective-permute-done.2.far_ref), channel_id=1, source_target_pairs={{0,8},{8,0},{1,9},{9,1},{2,10},{10,2},{3,11},{11,3},{4,12},{12,4},... | collective-permute-start | bytes 393224 | tf_op jit(solution)/shard_map/ppermute | solution.py:323
  37.0 40.9 %collective-permute-start.4 = (f32[16,2,2,8,128]{4,3,2,1,0:T(8,128)S(1)}, f32[16,2,2,8,128]{4,3,2,1,0:T(8,128)S(1)}, u32[]{:S(2)}, u32[]{:S(2)}) collective-permute-start(f32[16,2,2,8,128]{4,3,2,1,0:T(8,128)S(1)} %get-tuple-element.230), channel_id=1, source_target_pairs={{0,16},{16,0},{1,17},{17,1},{2,18},{18,2},{3,19},{19,3},{4,20},{20... | collective-permute-start | bytes 786440 | tf_op jit(solution)/shard_map/ppermute | solution.py:372
  74.2 27.0 %collective-permute-start.5 = (f32[16,2,2,8,128]{4,3,2,1,0:T(8,128)S(1)}, f32[16,2,2,8,128]{4,3,2,1,0:T(8,128)S(1)}, u32[]{:S(2)}, u32[]{:S(2)}) collective-permute-start(f32[16,2,2,8,128]{4,3,2,1,0:T(8,128)S(1)} %crossing.1), channel_id=1, source_target_pairs={{0,16},{16,0},{1,17},{17,1},{2,18},{18,2},{3,19},{19,3},{4,20},{20... | collective-permute-start | bytes 786440 | tf_op jit(solution)/shard_map/ppermute | solution.py:372
  101.6 9.4 %collective-permute-start.6 = (f32[4,2,16,1024]{3,2,1,0:T(8,128)S(1)}, f32[4,2,16,1024]{3,2,1,0:T(8,128)S(1)}, u32[]{:S(2)}, u32[]{:S(2)}) collective-permute-start(f32[4,2,16,1024]{3,2,1,0:T(8,128)S(1)} %finish_other.1), channel_id=1, source_target_pairs={{0,8},{8,0},{1,9},{9,1},{2,10},{10,2},{3,11},{11,3},{4,12},{12,4},... | collective-permute-start | bytes 1572872 | tf_op jit(solution)/shard_map/ppermute | solution.py:323
